TPU v7x, 32 devices: a whole 2x2x4 slice. The times are simulated.
32 devices in a mesh: grp: 2 (over y), ta: 4 (over z), gx: 2 (over x), gy: 2 (over core).
Axes of the slice: x: 2, y: 2, z: 4, core: 2. Of those that a mesh axis runs over, the one named last changes fastest.
Arguments:
- c_states: float32 [32, 256, 1024], P(('grp', 'ta'), 'gx', 'gy'), parts along dimension 0, may hold values from -2.5 to 2.5
- diffusion: float32 [512, 1024], P(('grp', 'gx'), 'gy'), parts along dimension 0, may hold values from 0.02 to 0.08
- drift_x: float32 [512, 1024], P(('grp', 'gx'), 'gy'), parts along dimension 0, may hold values from -1 to 1
- drift_y: float32 [512, 1024], P(('grp', 'gx'), 'gy'), parts along dimension 0, may hold values from -1 to 1
Outputs:
- relaxed: float32 [32, 256, 1024], P(('grp', 'ta'), 'gx', 'gy'), parts along dimension 0
- residual: float32 [32, 256, 1024], P(('grp', 'ta'), 'gx', 'gy'), parts along dimension 0
There are 2 independent parts, one for each index of `grp`. A program takes and returns all parts, laid end to end along the dimension named above; each array names one. Nothing has to cross between parts.
All inputs are finite; a program needn't handle non-finite values.
Results may differ from a plain program's by a relative error of at most 0.000027.
Values sent between devices are 32-bit elements; how exact they have to be, the bound alone decides.
No kernel may reach another device: no remote copies, remote signals or barrier semaphores. Data moves between devices by JAX's collectives and lax.ppermute only.
A program may use at most 64 MiB of HBM per device.

v0:
```python
import jax
import jax.numpy as jnp
from jax import lax
from jax.sharding import PartitionSpec as P

FACTOR = 4


courant = 0.08


def with_halo(x, sides, width):
    for axis, dim in sides:
        count, length = (lax.axis_size(axis), x.shape[dim])
        up = [(i, (i + 1) % count) for i in range(count - 1)]
        down = [(j, i) for i, j in up]
        last = lax.slice_in_dim(x, length - width, length, axis=dim)
        initial = lax.slice_in_dim(x, 0, width, axis=dim)
        before = lax.ppermute(last, axis, up)
        after = lax.ppermute(initial, axis, down)
        x = jnp.concatenate([before, x, after], axis=dim)
    return x


def shifted(value, axis, steps):
    count = lax.axis_size(axis)
    initial, last = (max(0, -steps), min(count, count - steps))
    return lax.ppermute(value, axis, [(source, source + steps) for source in range(initial, last)])


def local_step(padded, coeffs):
    field = padded[:, 1:-1, 1:-1]
    lower_x = padded[:, :-2, 1:-1]
    upper_x = padded[:, 2:, 1:-1]
    lower_y = padded[:, 1:-1, :-2]
    upper_y = padded[:, 1:-1, 2:]
    laplace = lower_x + upper_x + lower_y + upper_y - 4.0 * field
    speed_x = coeffs[1] + field
    speed_y = coeffs[2] + field
    advect = jnp.maximum(speed_x, 0.0) * (field - lower_x) + jnp.minimum(speed_x, 0.0) * (
        upper_x - field
    )
    advect = (
        advect
        + jnp.maximum(speed_y, 0.0) * (field - lower_y)
        + jnp.minimum(speed_y, 0.0) * (upper_y - field)
    )
    return field + coeffs[0] * laplace - courant * advect


def propagate(states, coeffs):
    for count in range(FACTOR):
        padded = with_halo(states, (("gx", 1), ("gy", 2)), 1)
        states = local_step(padded, coeffs)
    return states


def local(c_states, diffusion, drift_x, drift_y):
    coeffs = jnp.stack([diffusion, drift_x, drift_y])
    is_first = lax.axis_index("ta") == 0
    propagated = propagate(c_states, coeffs)
    carried = shifted(propagated[-1], "ta", 1)
    head = jnp.where(is_first, c_states[0], carried)
    start = jnp.concatenate([head[None], propagated[:-1]], axis=0)
    image = propagate(start, coeffs)
    returned = shifted(image[-1], "ta", 1)
    image_lead = image[:-1]
    relaxed = jnp.concatenate([head[None], propagated[:-1]], axis=0)
    first_residual = jnp.where(is_first, jnp.zeros_like(head), returned - head)
    residual = jnp.concatenate([first_residual[None], image_lead - propagated[:-1]], axis=0)
    return (relaxed, residual)


def solution(mesh):
    return jax.shard_map(
        local,
        mesh=mesh,
        in_specs=(
            P(("grp", "ta"), "gx", "gy"),
            P(("grp", "gx"), "gy"),
            P(("grp", "gx"), "gy"),
            P(("grp", "gx"), "gy"),
        ),
        out_specs=(P(("grp", "ta"), "gx", "gy"), P(("grp", "ta"), "gx", "gy")),
        check_vma=False,
    )
```

profile of v0, /device:TPU:9, one launch (start us, length us, event | category | flops | bytes accessed | tf_op | source)
XLA Modules:
  0.0 144.2 jit_solution(18065735817641275175)
XLA Ops:
  0.6 0.9 fusion.114
  1.5 3.1 %collective-permute-start = (f32[4,1,512]{2,1,0:T(1,128)S(1)}, f32[4,1,512]{2,1,0:T(1,128)S(1)}, u32[]{:S(2)}, u32[]{:S(2)}) collective-permute-start(f32[4,1,512]{2,1,0:T(1,128)S(1)} %get-tuple-element.34), channel_id=1, source_target_pairs={{0,2},{1,3},{4,6},{5,7},{8,10},{9,11},{12,14},{13,15},{16,18},{17,... | collective-permute-start | bytes 24584 | tf_op jit(solution)/shard_map/ppermute | solution.py:19
  4.7 1.4 collective-permute-start.1
  6.1 3.1 %collective-permute-done.1 = f32[4,1,512]{2,1,0:T(1,128)S(1)} collective-permute-done((f32[4,1,512]{2,1,0:T(1,128)S(1)}, f32[4,1,512]{2,1,0:T(1,128)S(1)}, u32[]{:S(2)}, u32[]{:S(2)}) %collective-permute-start.1) | collective-permute-done | bytes 8224 | tf_op jit(solution)/shard_map/ppermute | solution.py:20
  9.2 1.2 pad_maximum_fusion.94
  10.4 1.3 collective-permute-start.2
  11.7 4.0 %collective-permute-start.3 = (f32[4,130,1]{2,1,0:T(8,128)S(1)}, f32[4,130,1]{2,1,0:T(8,128)S(1)}, u32[]{:S(2)}, u32[]{:S(2)}) collective-permute-start(f32[4,130,1]{2,1,0:T(8,128)S(1)} %get-tuple-element.19), channel_id=1, source_target_pairs={{1,0},{3,2},{5,4},{7,6},{9,8},{11,10},{13,12},{15,14},{17,16},{19,... | collective-permute-start | bytes 6248 | tf_op jit(solution)/shard_map/ppermute | solution.py:20
  15.8 1.1 collective-permute-done.3
  16.9 4.7 %fusion.97 = f32[4,128,512]{2,1,0:T(8,128)S(1)} fusion(f32[4,128,512]{2,1,0:T(8,128)} %param.4, f32[4,1,512]{2,1,0:T(1,128)S(1)} %collective-permute-done.1, f32[4,1,512]{2,1,0:T(1,128)S(1)} %collective-permute-done, f32[4,130,1]{2,1,0:T(8,128)S(1)} %collective-permute-done.3, f32[4,130,1]{2,1,0:T(8,128)S(1)} %collective-permute-done.2, ...), kind=kLoop, calls=%fused_computation.169 | loop fusion | flops 8912896 | bytes 2904128 | tf_op jit(solution)/shard_map/sub | solution.py:48
  21.7 1.4 collective-permute-start.4
  23.0 1.3 collective-permute-start.5
  24.3 3.1 %collective-permute-done.5 = f32[4,1,512]{2,1,0:T(1,128)S(1)} collective-permute-done((f32[4,1,512]{2,1,0:T(1,128)S(1)}, f32[4,1,512]{2,1,0:T(1,128)S(1)}, u32[]{:S(2)}, u32[]{:S(2)}) %collective-permute-start.5) | collective-permute-done | bytes 8224 | tf_op jit(solution)/shard_map/ppermute | solution.py:20
  27.6 1.3 collective-permute-start.6
  28.9 3.7 %collective-permute-start.7 = (f32[4,130,1]{2,1,0:T(8,128)S(1)}, f32[4,130,1]{2,1,0:T(8,128)S(1)}, u32[]{:S(2)}, u32[]{:S(2)}) collective-permute-start(f32[4,130,1]{2,1,0:T(8,128)S(1)} %get-tuple-element.17), channel_id=1, source_target_pairs={{1,0},{3,2},{5,4},{7,6},{9,8},{11,10},{13,12},{15,14},{17,16},{19,... | collective-permute-start | bytes 6248 | tf_op jit(solution)/shard_map/ppermute | solution.py:20
  32.7 1.1 collective-permute-done.7
  33.8 2.2 %fusion.82 = f32[4,128,512]{2,1,0:T(8,128)S(1)} fusion(f32[4,128,512]{2,1,0:T(8,128)S(1)} %fusion.97, f32[4,1,512]{2,1,0:T(1,128)S(1)} %collective-permute-done.5, f32[4,1,512]{2,1,0:T(1,128)S(1)} %collective-permute-done.4, f32[4,130,1]{2,1,0:T(8,128)S(1)} %collective-permute-done.7, f32[4,130,1]{2,1,0:T(8,128)S(1)} %collective-permute-done.6, ...), kind=kLoop, calls=%fused_computation.146 | loop fusion | flops 8912896 | bytes 2904128 | tf_op jit(solution)/shard_map/sub | solution.py:48
  36.1 1.4 collective-permute-start.8
  37.4 1.3 collective-permute-start.9
  38.7 3.1 %collective-permute-done.9 = f32[4,1,512]{2,1,0:T(1,128)S(1)} collective-permute-done((f32[4,1,512]{2,1,0:T(1,128)S(1)}, f32[4,1,512]{2,1,0:T(1,128)S(1)}, u32[]{:S(2)}, u32[]{:S(2)}) %collective-permute-start.9) | collective-permute-done | bytes 8224 | tf_op jit(solution)/shard_map/ppermute | solution.py:20
  42.0 1.3 collective-permute-start.10
  43.3 3.7 %collective-permute-start.11 = (f32[4,130,1]{2,1,0:T(8,128)S(1)}, f32[4,130,1]{2,1,0:T(8,128)S(1)}, u32[]{:S(2)}, u32[]{:S(2)}) collective-permute-start(f32[4,130,1]{2,1,0:T(8,128)S(1)} %get-tuple-element.15), channel_id=1, source_target_pairs={{1,0},{3,2},{5,4},{7,6},{9,8},{11,10},{13,12},{15,14},{17,16},{19,... | collective-permute-start | bytes 6248 | tf_op jit(solution)/shard_map/ppermute | solution.py:20
  47.0 1.1 collective-permute-done.11
  48.2 2.2 %fusion.67 = f32[4,128,512]{2,1,0:T(8,128)S(1)} fusion(f32[4,128,512]{2,1,0:T(8,128)S(1)} %fusion.82, f32[4,1,512]{2,1,0:T(1,128)S(1)} %collective-permute-done.9, f32[4,1,512]{2,1,0:T(1,128)S(1)} %collective-permute-done.8, f32[4,130,1]{2,1,0:T(8,128)S(1)} %collective-permute-done.11, f32[4,130,1]{2,1,0:T(8,128)S(1)} %collective-permute-done.10, ...), kind=kLoop, calls=%fused_computation.123 | loop fusion | flops 8912896 | bytes 2904128 | tf_op jit(solution)/shard_map/sub | solution.py:48
  50.4 1.4 collective-permute-start.12
  51.8 1.3 collective-permute-start.13
  53.1 3.1 %collective-permute-done.13 = f32[4,1,512]{2,1,0:T(1,128)S(1)} collective-permute-done((f32[4,1,512]{2,1,0:T(1,128)S(1)}, f32[4,1,512]{2,1,0:T(1,128)S(1)}, u32[]{:S(2)}, u32[]{:S(2)}) %collective-permute-start.13) | collective-permute-done | bytes 8224 | tf_op jit(solution)/shard_map/ppermute | solution.py:20
  56.4 1.3 collective-permute-start.14
  57.7 3.7 %collective-permute-start.15 = (f32[4,130,1]{2,1,0:T(8,128)S(1)}, f32[4,130,1]{2,1,0:T(8,128)S(1)}, u32[]{:S(2)}, u32[]{:S(2)}) collective-permute-start(f32[4,130,1]{2,1,0:T(8,128)S(1)} %get-tuple-element.13), channel_id=1, source_target_pairs={{1,0},{3,2},{5,4},{7,6},{9,8},{11,10},{13,12},{15,14},{17,16},{19,... | collective-permute-start | bytes 6248 | tf_op jit(solution)/shard_map/ppermute | solution.py:20
  61.4 1.1 collective-permute-done.15
  62.6 2.2 %fusion.52 = f32[4,128,512]{2,1,0:T(8,128)S(1)} fusion(f32[4,128,512]{2,1,0:T(8,128)S(1)} %fusion.67, f32[4,1,512]{2,1,0:T(1,128)S(1)} %collective-permute-done.13, f32[4,1,512]{2,1,0:T(1,128)S(1)} %collective-permute-done.12, f32[4,130,1]{2,1,0:T(8,128)S(1)} %collective-permute-done.15, f32[4,130,1]{2,1,0:T(8,128)S(1)} %collective-permute-done.14, ...), kind=kLoop, calls=%fused_computation.100 | loop fusion | flops 8912896 | bytes 2904128 | tf_op jit(solution)/shard_map/sub | solution.py:48
  64.8 3.3 %collective-permute-start.16 = (f32[128,512]{1,0:T(8,128)S(1)}, f32[128,512]{1,0:T(8,128)S(1)}, u32[]{:S(2)}, u32[]{:S(2)}) collective-permute-start(f32[128,512]{1,0:T(8,128)S(1)} %slice_bitcast_fusion.1), channel_id=1, source_target_pairs={{0,4},{4,8},{8,12},{1,5},{5,9},{9,13},{2,6},{6,10},{10,14},{3,7},{... | collective-permute-start | bytes 786440 | tf_op jit(solution)/shard_map/ppermute | solution.py:28
  68.3 6.1 %collective-permute-done.16 = f32[128,512]{1,0:T(8,128)S(1)} collective-permute-done((f32[128,512]{1,0:T(8,128)S(1)}, f32[128,512]{1,0:T(8,128)S(1)}, u32[]{:S(2)}, u32[]{:S(2)}) %collective-permute-start.16) | collective-permute-done | bytes 262176 | tf_op jit(solution)/shard_map/ppermute | solution.py:28
  74.5 1.4 collective-permute-start.17
  75.8 1.3 collective-permute-start.18
  77.1 3.1 %collective-permute-done.18 = f32[4,1,512]{2,1,0:T(1,128)S(1)} collective-permute-done((f32[4,1,512]{2,1,0:T(1,128)S(1)}, f32[4,1,512]{2,1,0:T(1,128)S(1)}, u32[]{:S(2)}, u32[]{:S(2)}) %collective-permute-start.18) | collective-permute-done | bytes 8224 | tf_op jit(solution)/shard_map/ppermute | solution.py:20
  80.2 0.2 pad_maximum_fusion.82
  80.4 1.3 collective-permute-start.19
  81.7 4.6 %collective-permute-start.20 = (f32[4,130,1]{2,1,0:T(8,128)S(1)}, f32[4,130,1]{2,1,0:T(8,128)S(1)}, u32[]{:S(2)}, u32[]{:S(2)}) collective-permute-start(f32[4,130,1]{2,1,0:T(8,128)S(1)} %get-tuple-element.11), channel_id=1, source_target_pairs={{1,0},{3,2},{5,4},{7,6},{9,8},{11,10},{13,12},{15,14},{17,16},{19,... | collective-permute-start | bytes 6248 | tf_op jit(solution)/shard_map/ppermute | solution.py:20
  86.3 1.1 collective-permute-done.20
  87.4 3.1 %multiply_subtract_fusion = (f32[4,128,512]{2,1,0:T(8,128)S(1)}, f32[4,128,512]{2,1,0:T(8,128)}) fusion(f32[4,130,1]{2,1,0:T(8,128)S(1)} %collective-permute-done.20, f32[4,1,512]{2,1,0:T(1,128)S(1)} %collective-permute-done.18, f32[3,128,512]{2,1,0:T(8,128)S(1)} %slice.317, f32[1,128,512]{2,1,0:T(8,128)S(1)} %fusion.105, ...), kind=kLoop, calls=%fused_computation.179 | loop fusion | flops 10223616 | bytes 3952704 | tf_op jit(solution)/shard_map/sub | solution.py:48
  90.5 1.4 collective-permute-start.21
  91.9 1.3 collective-permute-start.22
  93.2 3.1 %collective-permute-done.22 = f32[4,1,512]{2,1,0:T(1,128)S(1)} collective-permute-done((f32[4,1,512]{2,1,0:T(1,128)S(1)}, f32[4,1,512]{2,1,0:T(1,128)S(1)}, u32[]{:S(2)}, u32[]{:S(2)}) %collective-permute-start.22) | collective-permute-done | bytes 8224 | tf_op jit(solution)/shard_map/ppermute | solution.py:20
  96.4 1.3 collective-permute-start.23
  97.7 3.7 %collective-permute-start.24 = (f32[4,130,1]{2,1,0:T(8,128)S(1)}, f32[4,130,1]{2,1,0:T(8,128)S(1)}, u32[]{:S(2)}, u32[]{:S(2)}) collective-permute-start(f32[4,130,1]{2,1,0:T(8,128)S(1)} %get-tuple-element.9), channel_id=1, source_target_pairs={{1,0},{3,2},{5,4},{7,6},{9,8},{11,10},{13,12},{15,14},{17,16},{19,... | collective-permute-start | bytes 6248 | tf_op jit(solution)/shard_map/ppermute | solution.py:20
  101.5 1.1 collective-permute-done.24
  102.6 2.2 %fusion.37 = f32[4,128,512]{2,1,0:T(8,128)S(1)} fusion(f32[4,128,512]{2,1,0:T(8,128)S(1)} %get-tuple-element.2, f32[4,1,512]{2,1,0:T(1,128)S(1)} %collective-permute-done.22, f32[4,1,512]{2,1,0:T(1,128)S(1)} %collective-permute-done.21, f32[4,130,1]{2,1,0:T(8,128)S(1)} %collective-permute-done.24, f32[4,130,1]{2,1,0:T(8,128)S(1)} %collective-permute-done.23, ...), kind=kLoop, calls=%fused_computation.65 | loop fusion | flops 8912896 | bytes 2904128 | tf_op jit(solution)/shard_map/sub | solution.py:48
  104.9 1.4 collective-permute-start.25
  106.3 1.3 collective-permute-start.26
  107.6 3.1 %collective-permute-done.26 = f32[4,1,512]{2,1,0:T(1,128)S(1)} collective-permute-done((f32[4,1,512]{2,1,0:T(1,128)S(1)}, f32[4,1,512]{2,1,0:T(1,128)S(1)}, u32[]{:S(2)}, u32[]{:S(2)}) %collective-permute-start.26) | collective-permute-done | bytes 8224 | tf_op jit(solution)/shard_map/ppermute | solution.py:20
  110.8 1.3 collective-permute-start.27
  112.1 3.7 %collective-permute-start.28 = (f32[4,130,1]{2,1,0:T(8,128)S(1)}, f32[4,130,1]{2,1,0:T(8,128)S(1)}, u32[]{:S(2)}, u32[]{:S(2)}) collective-permute-start(f32[4,130,1]{2,1,0:T(8,128)S(1)} %get-tuple-element.7), channel_id=1, source_target_pairs={{1,0},{3,2},{5,4},{7,6},{9,8},{11,10},{13,12},{15,14},{17,16},{19,... | collective-permute-start | bytes 6248 | tf_op jit(solution)/shard_map/ppermute | solution.py:20
  115.9 1.1 collective-permute-done.28
  117.0 2.2 %fusion.22 = f32[4,128,512]{2,1,0:T(8,128)S(1)} fusion(f32[4,128,512]{2,1,0:T(8,128)S(1)} %fusion.37, f32[4,1,512]{2,1,0:T(1,128)S(1)} %collective-permute-done.26, f32[4,1,512]{2,1,0:T(1,128)S(1)} %collective-permute-done.25, f32[4,130,1]{2,1,0:T(8,128)S(1)} %collective-permute-done.28, f32[4,130,1]{2,1,0:T(8,128)S(1)} %collective-permute-done.27, ...), kind=kLoop, calls=%fused_computation.42 | loop fusion | flops 8912896 | bytes 2904128 | tf_op jit(solution)/shard_map/sub | solution.py:48
  119.3 1.4 collective-permute-start.29
  120.7 1.3 collective-permute-start.30
  122.0 3.1 %collective-permute-done.30 = f32[4,1,512]{2,1,0:T(1,128)S(1)} collective-permute-done((f32[4,1,512]{2,1,0:T(1,128)S(1)}, f32[4,1,512]{2,1,0:T(1,128)S(1)}, u32[]{:S(2)}, u32[]{:S(2)}) %collective-permute-start.30) | collective-permute-done | bytes 8224 | tf_op jit(solution)/shard_map/ppermute | solution.py:20
  125.2 1.3 collective-permute-start.31
  126.5 3.7 %collective-permute-start.32 = (f32[4,130,1]{2,1,0:T(8,128)S(1)}, f32[4,130,1]{2,1,0:T(8,128)S(1)}, u32[]{:S(2)}, u32[]{:S(2)}) collective-permute-start(f32[4,130,1]{2,1,0:T(8,128)S(1)} %get-tuple-element.5), channel_id=1, source_target_pairs={{1,0},{3,2},{5,4},{7,6},{9,8},{11,10},{13,12},{15,14},{17,16},{19,... | collective-permute-start | bytes 6248 | tf_op jit(solution)/shard_map/ppermute | solution.py:20
  130.3 1.1 collective-permute-done.32
  131.4 2.2 %fusion.7 = f32[4,128,512]{2,1,0:T(8,128)S(1)} fusion(f32[4,128,512]{2,1,0:T(8,128)S(1)} %fusion.22, f32[4,1,512]{2,1,0:T(1,128)S(1)} %collective-permute-done.30, f32[4,1,512]{2,1,0:T(1,128)S(1)} %collective-permute-done.29, f32[4,130,1]{2,1,0:T(8,128)S(1)} %collective-permute-done.32, f32[4,130,1]{2,1,0:T(8,128)S(1)} %collective-permute-done.31, ...), kind=kLoop, calls=%fused_computation.19 | loop fusion | flops 8912896 | bytes 2904128 | tf_op jit(solution)/shard_map/sub | solution.py:48
  133.7 3.2 %collective-permute-start.33 = (f32[128,512]{1,0:T(8,128)S(1)}, f32[128,512]{1,0:T(8,128)S(1)}, u32[]{:S(2)}, u32[]{:S(2)}) collective-permute-start(f32[128,512]{1,0:T(8,128)S(1)} %slice_bitcast_fusion), channel_id=1, source_target_pairs={{0,4},{4,8},{8,12},{1,5},{5,9},{9,13},{2,6},{6,10},{10,14},{3,7},{... | collective-permute-start | bytes 786440 | tf_op jit(solution)/shard_map/ppermute | solution.py:28
  137.0 6.1 %collective-permute-done.33 = f32[128,512]{1,0:T(8,128)S(1)} collective-permute-done((f32[128,512]{1,0:T(8,128)S(1)}, f32[128,512]{1,0:T(8,128)S(1)}, u32[]{:S(2)}, u32[]{:S(2)}) %collective-permute-start.33) | collective-permute-done | bytes 262176 | tf_op jit(solution)/shard_map/ppermute | solution.py:28
  143.1 1.0 pad_maximum_fusion.69
  (43 shorter events, 1.4 us)
Async XLA Ops:
  1.5 4.6 %collective-permute-start = (f32[4,1,512]{2,1,0:T(1,128)S(1)}, f32[4,1,512]{2,1,0:T(1,128)S(1)}, u32[]{:S(2)}, u32[]{:S(2)}) collective-permute-start(f32[4,1,512]{2,1,0:T(1,128)S(1)} %get-tuple-element.34), channel_id=1, source_target_pairs={{0,2},{1,3},{4,6},{5,7},{8,10},{9,11},{12,14},{13,15},{16,18},{17,... | collective-permute-start | bytes 24584 | tf_op jit(solution)/shard_map/ppermute | solution.py:19
  4.6 12.3 %copy-start = (f32[128,512]{1,0:T(8,128)S(1)}, f32[128,512]{1,0:T(8,128)}, u32[]{:S(2)}) copy-start(f32[128,512]{1,0:T(8,128)} %param.7) | copy-start | bytes 786436
  4.7 12.3 %copy-start.1 = (f32[128,512]{1,0:T(8,128)S(1)}, f32[128,512]{1,0:T(8,128)}, u32[]{:S(2)}) copy-start(f32[128,512]{1,0:T(8,128)} %param.6) | copy-start | bytes 786436
  4.7 12.3 %copy-start.2 = (f32[128,512]{1,0:T(8,128)S(1)}, f32[128,512]{1,0:T(8,128)}, u32[]{:S(2)}) copy-start(f32[128,512]{1,0:T(8,128)} %param.5) | copy-start | bytes 786436
  4.7 4.5 %collective-permute-start.1 = (f32[4,1,512]{2,1,0:T(1,128)S(1)}, f32[4,1,512]{2,1,0:T(1,128)S(1)}, u32[]{:S(2)}, u32[]{:S(2)}) collective-permute-start(f32[4,1,512]{2,1,0:T(1,128)S(1)} %get-tuple-element.35), channel_id=1, source_target_pairs={{2,0},{3,1},{6,4},{7,5},{10,8},{11,9},{14,12},{15,13},{18,16},{19,... | collective-permute-start | bytes 24584 | tf_op jit(solution)/shard_map/ppermute | solution.py:20
  10.4 5.4 %collective-permute-start.2 = (f32[4,130,1]{2,1,0:T(8,128)S(1)}, f32[4,130,1]{2,1,0:T(8,128)S(1)}, u32[]{:S(2)}, u32[]{:S(2)}) collective-permute-start(f32[4,130,1]{2,1,0:T(8,128)S(1)} %get-tuple-element.18), channel_id=1, source_target_pairs={{0,1},{2,3},{4,5},{6,7},{8,9},{10,11},{12,13},{14,15},{16,17},{18,... | collective-permute-start | bytes 6248 | tf_op jit(solution)/shard_map/ppermute | solution.py:19
  11.7 5.2 %collective-permute-start.3 = (f32[4,130,1]{2,1,0:T(8,128)S(1)}, f32[4,130,1]{2,1,0:T(8,128)S(1)}, u32[]{:S(2)}, u32[]{:S(2)}) collective-permute-start(f32[4,130,1]{2,1,0:T(8,128)S(1)} %get-tuple-element.19), channel_id=1, source_target_pairs={{1,0},{3,2},{5,4},{7,6},{9,8},{11,10},{13,12},{15,14},{17,16},{19,... | collective-permute-start | bytes 6248 | tf_op jit(solution)/shard_map/ppermute | solution.py:20
  21.7 2.7 %collective-permute-start.4 = (f32[4,1,512]{2,1,0:T(1,128)S(1)}, f32[4,1,512]{2,1,0:T(1,128)S(1)}, u32[]{:S(2)}, u32[]{:S(2)}) collective-permute-start(f32[4,1,512]{2,1,0:T(1,128)S(1)} %get-tuple-element.32), channel_id=1, source_target_pairs={{0,2},{1,3},{4,6},{5,7},{8,10},{9,11},{12,14},{13,15},{16,18},{17,... | collective-permute-start | bytes 24584 | tf_op jit(solution)/shard_map/ppermute | solution.py:19
  23.0 4.4 %collective-permute-start.5 = (f32[4,1,512]{2,1,0:T(1,128)S(1)}, f32[4,1,512]{2,1,0:T(1,128)S(1)}, u32[]{:S(2)}, u32[]{:S(2)}) collective-permute-start(f32[4,1,512]{2,1,0:T(1,128)S(1)} %get-tuple-element.33), channel_id=1, source_target_pairs={{2,0},{3,1},{6,4},{7,5},{10,8},{11,9},{14,12},{15,13},{18,16},{19,... | collective-permute-start | bytes 24584 | tf_op jit(solution)/shard_map/ppermute | solution.py:20
  27.6 5.1 %collective-permute-start.6 = (f32[4,130,1]{2,1,0:T(8,128)S(1)}, f32[4,130,1]{2,1,0:T(8,128)S(1)}, u32[]{:S(2)}, u32[]{:S(2)}) collective-permute-start(f32[4,130,1]{2,1,0:T(8,128)S(1)} %get-tuple-element.16), channel_id=1, source_target_pairs={{0,1},{2,3},{4,5},{6,7},{8,9},{10,11},{12,13},{14,15},{16,17},{18,... | collective-permute-start | bytes 6248 | tf_op jit(solution)/shard_map/ppermute | solution.py:19
  28.9 4.9 %collective-permute-start.7 = (f32[4,130,1]{2,1,0:T(8,128)S(1)}, f32[4,130,1]{2,1,0:T(8,128)S(1)}, u32[]{:S(2)}, u32[]{:S(2)}) collective-permute-start(f32[4,130,1]{2,1,0:T(8,128)S(1)} %get-tuple-element.17), channel_id=1, source_target_pairs={{1,0},{3,2},{5,4},{7,6},{9,8},{11,10},{13,12},{15,14},{17,16},{19,... | collective-permute-start | bytes 6248 | tf_op jit(solution)/shard_map/ppermute | solution.py:20
  36.1 2.7 %collective-permute-start.8 = (f32[4,1,512]{2,1,0:T(1,128)S(1)}, f32[4,1,512]{2,1,0:T(1,128)S(1)}, u32[]{:S(2)}, u32[]{:S(2)}) collective-permute-start(f32[4,1,512]{2,1,0:T(1,128)S(1)} %get-tuple-element.30), channel_id=1, source_target_pairs={{0,2},{1,3},{4,6},{5,7},{8,10},{9,11},{12,14},{13,15},{16,18},{17,... | collective-permute-start | bytes 24584 | tf_op jit(solution)/shard_map/ppermute | solution.py:19
  37.4 4.4 %collective-permute-start.9 = (f32[4,1,512]{2,1,0:T(1,128)S(1)}, f32[4,1,512]{2,1,0:T(1,128)S(1)}, u32[]{:S(2)}, u32[]{:S(2)}) collective-permute-start(f32[4,1,512]{2,1,0:T(1,128)S(1)} %get-tuple-element.31), channel_id=1, source_target_pairs={{2,0},{3,1},{6,4},{7,5},{10,8},{11,9},{14,12},{15,13},{18,16},{19,... | collective-permute-start | bytes 24584 | tf_op jit(solution)/shard_map/ppermute | solution.py:20
  42.0 5.0 %collective-permute-start.10 = (f32[4,130,1]{2,1,0:T(8,128)S(1)}, f32[4,130,1]{2,1,0:T(8,128)S(1)}, u32[]{:S(2)}, u32[]{:S(2)}) collective-permute-start(f32[4,130,1]{2,1,0:T(8,128)S(1)} %get-tuple-element.14), channel_id=1, source_target_pairs={{0,1},{2,3},{4,5},{6,7},{8,9},{10,11},{12,13},{14,15},{16,17},{18,... | collective-permute-start | bytes 6248 | tf_op jit(solution)/shard_map/ppermute | solution.py:19
  43.3 4.9 %collective-permute-start.11 = (f32[4,130,1]{2,1,0:T(8,128)S(1)}, f32[4,130,1]{2,1,0:T(8,128)S(1)}, u32[]{:S(2)}, u32[]{:S(2)}) collective-permute-start(f32[4,130,1]{2,1,0:T(8,128)S(1)} %get-tuple-element.15), channel_id=1, source_target_pairs={{1,0},{3,2},{5,4},{7,6},{9,8},{11,10},{13,12},{15,14},{17,16},{19,... | collective-permute-start | bytes 6248 | tf_op jit(solution)/shard_map/ppermute | solution.py:20
  50.4 2.7 %collective-permute-start.12 = (f32[4,1,512]{2,1,0:T(1,128)S(1)}, f32[4,1,512]{2,1,0:T(1,128)S(1)}, u32[]{:S(2)}, u32[]{:S(2)}) collective-permute-start(f32[4,1,512]{2,1,0:T(1,128)S(1)} %get-tuple-element.28), channel_id=1, source_target_pairs={{0,2},{1,3},{4,6},{5,7},{8,10},{9,11},{12,14},{13,15},{16,18},{17,... | collective-permute-start | bytes 24584 | tf_op jit(solution)/shard_map/ppermute | solution.py:19
  51.8 4.4 %collective-permute-start.13 = (f32[4,1,512]{2,1,0:T(1,128)S(1)}, f32[4,1,512]{2,1,0:T(1,128)S(1)}, u32[]{:S(2)}, u32[]{:S(2)}) collective-permute-start(f32[4,1,512]{2,1,0:T(1,128)S(1)} %get-tuple-element.29), channel_id=1, source_target_pairs={{2,0},{3,1},{6,4},{7,5},{10,8},{11,9},{14,12},{15,13},{18,16},{19,... | collective-permute-start | bytes 24584 | tf_op jit(solution)/shard_map/ppermute | solution.py:20
  56.4 5.0 %collective-permute-start.14 = (f32[4,130,1]{2,1,0:T(8,128)S(1)}, f32[4,130,1]{2,1,0:T(8,128)S(1)}, u32[]{:S(2)}, u32[]{:S(2)}) collective-permute-start(f32[4,130,1]{2,1,0:T(8,128)S(1)} %get-tuple-element.12), channel_id=1, source_target_pairs={{0,1},{2,3},{4,5},{6,7},{8,9},{10,11},{12,13},{14,15},{16,17},{18,... | collective-permute-start | bytes 6248 | tf_op jit(solution)/shard_map/ppermute | solution.py:19
  57.7 4.9 %collective-permute-start.15 = (f32[4,130,1]{2,1,0:T(8,128)S(1)}, f32[4,130,1]{2,1,0:T(8,128)S(1)}, u32[]{:S(2)}, u32[]{:S(2)}) collective-permute-start(f32[4,130,1]{2,1,0:T(8,128)S(1)} %get-tuple-element.13), channel_id=1, source_target_pairs={{1,0},{3,2},{5,4},{7,6},{9,8},{11,10},{13,12},{15,14},{17,16},{19,... | collective-permute-start | bytes 6248 | tf_op jit(solution)/shard_map/ppermute | solution.py:20
  64.8 9.6 %copy-start.3 = (f32[4,128,512]{2,1,0:T(8,128)S(1)}, f32[4,128,512]{2,1,0:T(8,128)}, u32[]{:S(2)}) copy-start(f32[4,128,512]{2,1,0:T(8,128)} %param.4) | copy-start | bytes 3145732
  64.8 9.5 %collective-permute-start.16 = (f32[128,512]{1,0:T(8,128)S(1)}, f32[128,512]{1,0:T(8,128)S(1)}, u32[]{:S(2)}, u32[]{:S(2)}) collective-permute-start(f32[128,512]{1,0:T(8,128)S(1)} %slice_bitcast_fusion.1), channel_id=1, source_target_pairs={{0,4},{4,8},{8,12},{1,5},{5,9},{9,13},{2,6},{6,10},{10,14},{3,7},{... | collective-permute-start | bytes 786440 | tf_op jit(solution)/shard_map/ppermute | solution.py:28
  74.5 2.7 %collective-permute-start.17 = (f32[4,1,512]{2,1,0:T(1,128)S(1)}, f32[4,1,512]{2,1,0:T(1,128)S(1)}, u32[]{:S(2)}, u32[]{:S(2)}) collective-permute-start(f32[4,1,512]{2,1,0:T(1,128)S(1)} %get-tuple-element.26), channel_id=1, source_target_pairs={{0,2},{1,3},{4,6},{5,7},{8,10},{9,11},{12,14},{13,15},{16,18},{17,... | collective-permute-start | bytes 24584 | tf_op jit(solution)/shard_map/ppermute | solution.py:19
  75.8 4.4 %collective-permute-start.18 = (f32[4,1,512]{2,1,0:T(1,128)S(1)}, f32[4,1,512]{2,1,0:T(1,128)S(1)}, u32[]{:S(2)}, u32[]{:S(2)}) collective-permute-start(f32[4,1,512]{2,1,0:T(1,128)S(1)} %get-tuple-element.27), channel_id=1, source_target_pairs={{2,0},{3,1},{6,4},{7,5},{10,8},{11,9},{14,12},{15,13},{18,16},{19,... | collective-permute-start | bytes 24584 | tf_op jit(solution)/shard_map/ppermute | solution.py:20
  80.4 5.9 %collective-permute-start.19 = (f32[4,130,1]{2,1,0:T(8,128)S(1)}, f32[4,130,1]{2,1,0:T(8,128)S(1)}, u32[]{:S(2)}, u32[]{:S(2)}) collective-permute-start(f32[4,130,1]{2,1,0:T(8,128)S(1)} %get-tuple-element.10), channel_id=1, source_target_pairs={{0,1},{2,3},{4,5},{6,7},{8,9},{10,11},{12,13},{14,15},{16,17},{18,... | collective-permute-start | bytes 6248 | tf_op jit(solution)/shard_map/ppermute | solution.py:19
  81.7 5.7 %collective-permute-start.20 = (f32[4,130,1]{2,1,0:T(8,128)S(1)}, f32[4,130,1]{2,1,0:T(8,128)S(1)}, u32[]{:S(2)}, u32[]{:S(2)}) collective-permute-start(f32[4,130,1]{2,1,0:T(8,128)S(1)} %get-tuple-element.11), channel_id=1, source_target_pairs={{1,0},{3,2},{5,4},{7,6},{9,8},{11,10},{13,12},{15,14},{17,16},{19,... | collective-permute-start | bytes 6248 | tf_op jit(solution)/shard_map/ppermute | solution.py:20
  90.5 2.7 %collective-permute-start.21 = (f32[4,1,512]{2,1,0:T(1,128)S(1)}, f32[4,1,512]{2,1,0:T(1,128)S(1)}, u32[]{:S(2)}, u32[]{:S(2)}) collective-permute-start(f32[4,1,512]{2,1,0:T(1,128)S(1)} %get-tuple-element.24), channel_id=1, source_target_pairs={{0,2},{1,3},{4,6},{5,7},{8,10},{9,11},{12,14},{13,15},{16,18},{17,... | collective-permute-start | bytes 24584 | tf_op jit(solution)/shard_map/ppermute | solution.py:19
  91.9 4.4 %collective-permute-start.22 = (f32[4,1,512]{2,1,0:T(1,128)S(1)}, f32[4,1,512]{2,1,0:T(1,128)S(1)}, u32[]{:S(2)}, u32[]{:S(2)}) collective-permute-start(f32[4,1,512]{2,1,0:T(1,128)S(1)} %get-tuple-element.25), channel_id=1, source_target_pairs={{2,0},{3,1},{6,4},{7,5},{10,8},{11,9},{14,12},{15,13},{18,16},{19,... | collective-permute-start | bytes 24584 | tf_op jit(solution)/shard_map/ppermute | solution.py:20
  96.4 5.0 %collective-permute-start.23 = (f32[4,130,1]{2,1,0:T(8,128)S(1)}, f32[4,130,1]{2,1,0:T(8,128)S(1)}, u32[]{:S(2)}, u32[]{:S(2)}) collective-permute-start(f32[4,130,1]{2,1,0:T(8,128)S(1)} %get-tuple-element.8), channel_id=1, source_target_pairs={{0,1},{2,3},{4,5},{6,7},{8,9},{10,11},{12,13},{14,15},{16,17},{18,... | collective-permute-start | bytes 6248 | tf_op jit(solution)/shard_map/ppermute | solution.py:19
  97.7 4.9 %collective-permute-start.24 = (f32[4,130,1]{2,1,0:T(8,128)S(1)}, f32[4,130,1]{2,1,0:T(8,128)S(1)}, u32[]{:S(2)}, u32[]{:S(2)}) collective-permute-start(f32[4,130,1]{2,1,0:T(8,128)S(1)} %get-tuple-element.9), channel_id=1, source_target_pairs={{1,0},{3,2},{5,4},{7,6},{9,8},{11,10},{13,12},{15,14},{17,16},{19,... | collective-permute-start | bytes 6248 | tf_op jit(solution)/shard_map/ppermute | solution.py:20
  104.9 2.7 %collective-permute-start.25 = (f32[4,1,512]{2,1,0:T(1,128)S(1)}, f32[4,1,512]{2,1,0:T(1,128)S(1)}, u32[]{:S(2)}, u32[]{:S(2)}) collective-permute-start(f32[4,1,512]{2,1,0:T(1,128)S(1)} %get-tuple-element.22), channel_id=1, source_target_pairs={{0,2},{1,3},{4,6},{5,7},{8,10},{9,11},{12,14},{13,15},{16,18},{17,... | collective-permute-start | bytes 24584 | tf_op jit(solution)/shard_map/ppermute | solution.py:19
  106.3 4.4 %collective-permute-start.26 = (f32[4,1,512]{2,1,0:T(1,128)S(1)}, f32[4,1,512]{2,1,0:T(1,128)S(1)}, u32[]{:S(2)}, u32[]{:S(2)}) collective-permute-start(f32[4,1,512]{2,1,0:T(1,128)S(1)} %get-tuple-element.23), channel_id=1, source_target_pairs={{2,0},{3,1},{6,4},{7,5},{10,8},{11,9},{14,12},{15,13},{18,16},{19,... | collective-permute-start | bytes 24584 | tf_op jit(solution)/shard_map/ppermute | solution.py:20
  110.8 5.0 %collective-permute-start.27 = (f32[4,130,1]{2,1,0:T(8,128)S(1)}, f32[4,130,1]{2,1,0:T(8,128)S(1)}, u32[]{:S(2)}, u32[]{:S(2)}) collective-permute-start(f32[4,130,1]{2,1,0:T(8,128)S(1)} %get-tuple-element.6), channel_id=1, source_target_pairs={{0,1},{2,3},{4,5},{6,7},{8,9},{10,11},{12,13},{14,15},{16,17},{18,... | collective-permute-start | bytes 6248 | tf_op jit(solution)/shard_map/ppermute | solution.py:19
  112.1 4.9 %collective-permute-start.28 = (f32[4,130,1]{2,1,0:T(8,128)S(1)}, f32[4,130,1]{2,1,0:T(8,128)S(1)}, u32[]{:S(2)}, u32[]{:S(2)}) collective-permute-start(f32[4,130,1]{2,1,0:T(8,128)S(1)} %get-tuple-element.7), channel_id=1, source_target_pairs={{1,0},{3,2},{5,4},{7,6},{9,8},{11,10},{13,12},{15,14},{17,16},{19,... | collective-permute-start | bytes 6248 | tf_op jit(solution)/shard_map/ppermute | solution.py:20
  119.3 2.7 %collective-permute-start.29 = (f32[4,1,512]{2,1,0:T(1,128)S(1)}, f32[4,1,512]{2,1,0:T(1,128)S(1)}, u32[]{:S(2)}, u32[]{:S(2)}) collective-permute-start(f32[4,1,512]{2,1,0:T(1,128)S(1)} %get-tuple-element.20), channel_id=1, source_target_pairs={{0,2},{1,3},{4,6},{5,7},{8,10},{9,11},{12,14},{13,15},{16,18},{17,... | collective-permute-start | bytes 24584 | tf_op jit(solution)/shard_map/ppermute | solution.py:19
  120.7 4.4 %collective-permute-start.30 = (f32[4,1,512]{2,1,0:T(1,128)S(1)}, f32[4,1,512]{2,1,0:T(1,128)S(1)}, u32[]{:S(2)}, u32[]{:S(2)}) collective-permute-start(f32[4,1,512]{2,1,0:T(1,128)S(1)} %get-tuple-element.21), channel_id=1, source_target_pairs={{2,0},{3,1},{6,4},{7,5},{10,8},{11,9},{14,12},{15,13},{18,16},{19,... | collective-permute-start | bytes 24584 | tf_op jit(solution)/shard_map/ppermute | solution.py:20
  125.2 5.0 %collective-permute-start.31 = (f32[4,130,1]{2,1,0:T(8,128)S(1)}, f32[4,130,1]{2,1,0:T(8,128)S(1)}, u32[]{:S(2)}, u32[]{:S(2)}) collective-permute-start(f32[4,130,1]{2,1,0:T(8,128)S(1)} %get-tuple-element.4), channel_id=1, source_target_pairs={{0,1},{2,3},{4,5},{6,7},{8,9},{10,11},{12,13},{14,15},{16,17},{18,... | collective-permute-start | bytes 6248 | tf_op jit(solution)/shard_map/ppermute | solution.py:19
  126.5 4.9 %collective-permute-start.32 = (f32[4,130,1]{2,1,0:T(8,128)S(1)}, f32[4,130,1]{2,1,0:T(8,128)S(1)}, u32[]{:S(2)}, u32[]{:S(2)}) collective-permute-start(f32[4,130,1]{2,1,0:T(8,128)S(1)} %get-tuple-element.5), channel_id=1, source_target_pairs={{1,0},{3,2},{5,4},{7,6},{9,8},{11,10},{13,12},{15,14},{17,16},{19,... | collective-permute-start | bytes 6248 | tf_op jit(solution)/shard_map/ppermute | solution.py:20
  133.7 9.4 %collective-permute-start.33 = (f32[128,512]{1,0:T(8,128)S(1)}, f32[128,512]{1,0:T(8,128)S(1)}, u32[]{:S(2)}, u32[]{:S(2)}) collective-permute-start(f32[128,512]{1,0:T(8,128)S(1)} %slice_bitcast_fusion), channel_id=1, source_target_pairs={{0,4},{4,8},{8,12},{1,5},{5,9},{9,13},{2,6},{6,10},{10,14},{3,7},{... | collective-permute-start | bytes 786440 | tf_op jit(solution)/shard_map/ppermute | solution.py:28
where the time goes:
time: 146 us; the launch traced here: 144 us
  starting transfers between devices  71.1 us (49%)
  waiting for transfers between devices  46 us (32%)
  other arithmetic  24.7 us (17%)
    ppermute x16, starting transfers between devices, with_halo(): after = lax.ppermute(initial, axis, down)  41.5 us
    ppermute x16, waiting for transfers between devices, with_halo(): after = lax.ppermute(initial, axis, down)  33.8 us
    ppermute x16, starting transfers between devices, with_halo(): before = lax.ppermute(last, axis, up)  23 us
    sub x8, other arithmetic, local_step(): return field + coeffs[0] * laplace - courant * advect  21.2 us
    ppermute x2, waiting for transfers between devices, shifted(): lax.ppermute(value, axis, [(source, source + steps) for source in range(i...  12.2 us
    ppermute x2, starting transfers between devices, shifted(): lax.ppermute(value, axis, [(source, source + steps) for source in range(i...  6.54 us
  transfers between devices with their start and end apart: 34, of which 18 were waited for; matrix products, arithmetic and copies ran while one was open for 0% of the time, Pallas kernels for 0%

commit v1 on v0

v1 whole, which is shorter than its diff:
```python
import functools

import jax
import jax.numpy as jnp
from jax import lax
from jax.experimental import pallas as pl
from jax.experimental.pallas import tpu as pltpu
from jax.sharding import PartitionSpec as P

FACTOR = 4
HALO = 2 * FACTOR
LANES = 128
SUBLANES = 8
FIELDS = 7

courant = 0.08

VMEM = pl.BlockSpec(memory_space=pltpu.VMEM)
ANY = pl.BlockSpec(memory_space=pl.ANY)
F32 = jnp.float32


def lane_index(shape):
    return lax.broadcasted_iota(jnp.int32, shape, len(shape) - 1)


def pack_kernel(ends, c, dif, dx, dy, xs, ys, ds, last, second, edge, sems):
    rows, cols = dif.shape
    gy = lax.axis_index("gy")
    column = pl.multiple_of((1 - gy) * (cols - LANES), LANES)
    coeffs = (dif, dx, dy)
    copies = [
        pltpu.make_async_copy(c.at[3], last, sems.at[0]),
        pltpu.make_async_copy(c.at[2], second, sems.at[1]),
        pltpu.make_async_copy(c.at[:, :, pl.ds(column, LANES)], edge.at[pl.ds(0, 4)], sems.at[2]),
    ]
    for i, ref in enumerate(coeffs):
        copies.append(pltpu.make_async_copy(ref.at[:, pl.ds(column, LANES)], edge.at[4 + i], sems.at[3 + i]))
    k = 6
    for e in range(len(ends)):
        if len(ends) == 1:
            row = pl.multiple_of((1 - lax.axis_index("gx")) * (rows - HALO), HALO)
        else:
            row = ends[e] * (rows - HALO)
        copies.append(pltpu.make_async_copy(c.at[:, pl.ds(row, HALO), :], xs.at[e, pl.ds(0, 4)], sems.at[k]))
        k += 1
        for i, ref in enumerate(coeffs):
            copies.append(pltpu.make_async_copy(ref.at[pl.ds(row, HALO), :], xs.at[e, 4 + i], sems.at[k]))
            k += 1
    for copy in copies:
        copy.start()
    for copy in copies[2:]:
        copy.wait()
    lane = lane_index((rows, LANES))
    packed = jnp.zeros((rows, LANES), F32)
    for f in range(FIELDS):
        moved = pltpu.roll(edge[f], f * HALO + HALO * (1 - gy), 1)
        packed = jnp.where((lane >= f * HALO) & (lane < (f + 1) * HALO), moved, packed)
    ys[...] = packed
    for e in range(len(ends)):
        if len(ends) == 1:
            row = pl.multiple_of((1 - lax.axis_index("gx")) * (rows - HALO), HALO)
        else:
            row = ends[e] * (rows - HALO)
        ds[e] = ys[pl.ds(row, HALO), :]
    for copy in copies[:2]:
        copy.wait()


def pack(ends, c, dif, dx, dy):
    rows, cols = dif.shape
    n = len(ends)
    return pl.pallas_call(
        functools.partial(pack_kernel, ends),
        out_shape=(
            jax.ShapeDtypeStruct((n, FIELDS, HALO, cols), F32),
            jax.ShapeDtypeStruct((rows, LANES), F32),
            jax.ShapeDtypeStruct((n, HALO, LANES), F32),
            jax.ShapeDtypeStruct((rows, cols), F32),
            jax.ShapeDtypeStruct((rows, cols), F32),
        ),
        in_specs=[ANY] * 4,
        out_specs=(VMEM,) * 5,
        scratch_shapes=[pltpu.VMEM((FIELDS, rows, LANES), F32), pltpu.SemaphoreType.DMA((6 + 4 * n,))],
        name="pack",
    )(c, dif, dx, dy)


def unpacked(value, f, gy):
    moved = pltpu.roll(value, (LANES - f * HALO + gy * (LANES - HALO)) % LANES, 1)
    lane = lane_index(value.shape)
    begin = gy * (LANES - HALO)
    return jnp.where((lane >= begin) & (lane < begin + HALO), moved, 0.0)


def put_halos(pad, above, below, side, corner_above, corner_below, f, rows, cols):
    gx, gy = lax.axis_index("gx"), lax.axis_index("gy")
    has_above = gx > 0
    has_below = gx < lax.axis_size("gx") - 1
    blocks = cols // LANES
    for k in range(blocks):
        lanes = slice(k * LANES, (k + 1) * LANES)
        pad[k, pl.ds(0, HALO)] = jnp.where(has_above, above[:, lanes], 0.0)
        pad[k, pl.ds(HALO + rows, HALO)] = jnp.where(has_below, below[:, lanes], 0.0)
    pad[blocks, pl.ds(HALO, rows)] = unpacked(side, f, gy)
    pad[blocks, pl.ds(0, HALO)] = jnp.where(has_above, unpacked(corner_above, f, gy), 0.0)
    pad[blocks, pl.ds(HALO + rows, HALO)] = jnp.where(has_below, unpacked(corner_below, f, gy), 0.0)


def block_copies(flat, pad, sems, inward):
    rows, cols = flat.shape
    copies = []
    for k in range(cols // LANES):
        ends = (flat.at[:, pl.ds(k * LANES, LANES)], pad.at[k, pl.ds(HALO, rows)])
        copies.append(pltpu.make_async_copy(*(ends if inward else ends[::-1]), sems.at[k]))
    return copies


def start(copies):
    for copy in copies:
        copy.start()


def wait(copies):
    for copy in copies:
        copy.wait()


def to_strided(pad, w, scale):
    count = w.shape[0]
    for r in range(count):
        for k in range(pad.shape[0]):
            value = pad[k, pl.ds(r, SUBLANES, stride=count), :]
            w[r, :, pl.ds(k * LANES, LANES)] = value if scale is None else value * scale


def step(w, coeffs):
    count, _, lanes = w.shape
    initial, last = w[0], w[count - 1]
    field = initial
    before = field - pltpu.roll(last, 1, 0)
    for r in range(count):
        following = w[r + 1] if r < count - 1 else pltpu.roll(initial, SUBLANES - 1, 0)
        after = following - field
        left = field - pltpu.roll(field, 1, 1)
        right = pltpu.roll(left, lanes - 1, 1)
        speed_x = coeffs[1, r] + field
        speed_y = coeffs[2, r] + field
        laplace = (after - before) + (right - left)
        upwind_x = jnp.where(speed_x > 0.0, before, after)
        upwind_y = jnp.where(speed_y > 0.0, left, right)
        w[r] = field + coeffs[0, r] * laplace - speed_x * upwind_x - speed_y * upwind_y
        field, before = following, after


def propagate(w, coeffs):
    def body(count, carry):
        step(w, coeffs)
        return carry

    lax.fori_loop(0, FACTOR, body, 0)


def from_strided(out, w, other=None):
    count = w.shape[0]
    for r in range(count):
        for k in range(out.shape[0]):
            lanes = pl.ds(k * LANES, LANES)
            value = w[r, :, lanes]
            if other is not None:
                value = value - other[r, :, lanes]
            out[k, pl.ds(r, SUBLANES, stride=count), :] = value * (1.0 / courant)


def own_kernel(c, dif, dx, dy, xa, xb, ys, da, db, relaxed, residual, coeffs, kept, pads, ws, outs, sems, out_sems):
    rows, cols = dif.shape
    ta = lax.axis_index("ta")
    sources = [dif, dx, dy, c.at[0], c.at[1], c.at[2]]
    fields = [4, 5, 6, 0, 1, 2]
    copies = [block_copies(ref, pads.at[i], sems.at[i], True) for i, ref in enumerate(sources)]
    for group in copies:
        start(group)
    for i, f in enumerate(fields):
        put_halos(pads.at[i], xa[f], xb[f], ys[...], da[...], db[...], f, rows, cols)
    written = []

    def write(target, slot):
        group = block_copies(target, outs.at[slot], out_sems.at[slot], False)
        start(group)
        written.extend(group)

    for i in range(3):
        wait(copies[i])
        to_strided(pads.at[i], coeffs.at[i], None if i == 0 else courant)
    for n in range(3):
        wait(copies[3 + n])

    def body(n, carry):
        to_strided(pads.at[3 + n], ws.at[n], courant)
        propagate(ws.at[n], coeffs)
        from_strided(outs.at[n], ws.at[n])
        return carry

    lax.fori_loop(0, 3, body, 0)
    for n in range(3):
        write(relaxed.at[n + 1], n)
    kept[...] = ws[0]

    def body_again(n, carry):
        propagate(ws.at[n], coeffs)
        from_strided(outs.at[3 + n], ws.at[n], ws.at[n + 1])
        return carry

    lax.fori_loop(0, 2, body_again, 0)
    for n in range(2):
        write(residual.at[n + 2], 3 + n)

    @pl.when(ta == 0)
    def _():
        outs[5] = jnp.zeros_like(outs[5])
        group = block_copies(relaxed.at[0], pads.at[3], sems.at[0], False)
        for n in range(2):
            group += block_copies(residual.at[n], outs.at[5], sems.at[1 + n], False)
        start(group)
        wait(group)

    wait(written)


def own(c, dif, dx, dy, xa, xb, ys, da, db):
    rows, cols = dif.shape
    height, blocks = rows + 2 * HALO, cols // LANES
    strided = (height // SUBLANES, SUBLANES, cols + LANES)
    return pl.pallas_call(
        own_kernel,
        out_shape=(
            jax.ShapeDtypeStruct(c.shape, F32),
            jax.ShapeDtypeStruct(c.shape, F32),
            jax.ShapeDtypeStruct((3, *strided), F32),
            jax.ShapeDtypeStruct(strided, F32),
        ),
        in_specs=[ANY] * 4 + [VMEM] * 5,
        out_specs=(ANY, ANY, VMEM, VMEM),
        scratch_shapes=[
            pltpu.VMEM((6, blocks + 1, height, LANES), F32),
            pltpu.VMEM((3, *strided), F32),
            pltpu.VMEM((6, blocks, height, LANES), F32),
            pltpu.SemaphoreType.DMA((6, blocks)),
            pltpu.SemaphoreType.DMA((6, blocks)),
        ],
        compiler_params=pltpu.CompilerParams(vmem_limit_bytes=32 << 20),
        cost_estimate=pl.CostEstimate(flops=5 * 4 * 20 * rows * cols, bytes_accessed=3 << 20, transcendentals=0),
        name="own",
    )(c, dif, dx, dy, xa, xb, ys, da, db)


def received_kernel(f, slot, top, u, v, xa, xb, ys, da, db, coeffs, base, relaxed_in, residual_in, *rest):
    relaxed, residual, *kept, pad, w, outs, sems = rest
    del relaxed_in, residual_in
    rows, cols = u.shape
    ta = lax.axis_index("ta")

    @pl.when(ta > 0)
    def _():
        @pl.when(ta % 2 == 1)
        def _():
            start(block_copies(u, pad, sems.at[0], True))

        @pl.when(ta % 2 == 0)
        def _():
            start(block_copies(v, pad, sems.at[0], True))

        put_halos(pad, xa[f - 2], xb[f - 2], ys[...], da[...], db[...], f, rows, cols)
        wait(block_copies(u, pad, sems.at[0], True))
        to_strided(pad, w, courant)
        propagate(w, coeffs)
        if top:
            from_strided(outs.at[0], w)
            start(block_copies(relaxed.at[0], outs.at[0], sems.at[1], False))
            kept[0][...] = w[...]
        propagate(w, coeffs)
        from_strided(outs.at[1], w, base)
        copies = block_copies(residual.at[slot], outs.at[1], sems.at[2], False)
        start(copies)
        if top:
            copies += block_copies(relaxed.at[0], outs.at[0], sems.at[1], False)
        wait(copies)


def received(f, slot, top, u, v, xa, xb, ys, da, db, coeffs, base, relaxed, residual):
    rows, cols = u.shape
    strided, height, blocks = base.shape, rows + 2 * HALO, cols // LANES
    shape = jax.ShapeDtypeStruct(relaxed.shape, F32)
    more = (jax.ShapeDtypeStruct(strided, F32),) if top else ()
    return pl.pallas_call(
        functools.partial(received_kernel, f, slot, top),
        out_shape=(shape, shape, *more),
        in_specs=[ANY] * 2 + [VMEM] * 7 + [ANY] * 2,
        out_specs=(ANY, ANY) + (VMEM,) * len(more),
        scratch_shapes=[
            pltpu.VMEM((blocks + 1, height, LANES), F32),
            pltpu.VMEM(strided, F32),
            pltpu.VMEM((2, blocks, height, LANES), F32),
            pltpu.SemaphoreType.DMA((3, blocks)),
        ],
        input_output_aliases={9: 0, 10: 1},
        compiler_params=pltpu.CompilerParams(vmem_limit_bytes=32 << 20),
        cost_estimate=pl.CostEstimate(flops=2 * 4 * 20 * rows * cols, bytes_accessed=1 << 20, transcendentals=0),
        name="received",
    )(u, v, xa, xb, ys, da, db, coeffs, base, relaxed, residual)


def group_swaps(groups, sides):
    tables = []
    for begin in (0, 1):
        to = {g: g for g in range(groups)}
        for g in range(begin, groups - 1, 2):
            to[g], to[g + 1] = g + 1, g
        tables.append(
            [(g * sides + s, to[g] * sides + (s if to[g] != g else sides - 1 - s)) for g in range(groups) for s in range(sides)]
        )
    return tables


def local(c, dif, dx, dy):
    groups, nx, ny = (lax.axis_size(name) for name in ("ta", "gx", "gy"))
    assert ny == 2 and c.shape[0] == 4 and dif.shape[0] % SUBLANES == 0 and dif.shape[1] % LANES == 0
    ends = (1,) if nx == 2 else (1, 0)
    xs, ys, ds, last, second = pack(ends, c, dif, dx, dy)
    even, odd = group_swaps(groups, ny)
    u_last = lax.ppermute(last, ("ta", "gy"), even)
    v_last = lax.ppermute(last, ("ta", "gy"), odd)
    side = lax.ppermute(ys, "gy", [(0, 1), (1, 0)])
    if nx == 2:
        x = lax.ppermute(xs[0], "gx", [(0, 1), (1, 0)])
        corner = lax.ppermute(ds[0], ("gx", "gy"), [(0, 3), (3, 0), (1, 2), (2, 1)])
        xr, dr = [x, x], [corner, corner]
    else:
        xr, dr = [], []
        for e, hop in enumerate((1, -1)):
            pairs = [(i, i + hop) for i in range(nx) if 0 <= i + hop < nx]
            xr.append(lax.ppermute(xs[e], "gx", pairs))
            crossed = [(i * 2 + s, j * 2 + 1 - s) for i, j in pairs for s in range(2)]
            dr.append(lax.ppermute(ds[e], ("gx", "gy"), crossed))
    u_second = lax.ppermute(second, ("ta", "gy"), even)
    v_second = lax.ppermute(second, ("ta", "gy"), odd)

    n = len(ends)
    cols = c.shape[2]
    blocks = cols // LANES
    parts = [side]
    for e in range(n):
        parts.append(xr[e][2:4].reshape(2, HALO, blocks, LANES).transpose(0, 2, 1, 3).reshape(-1, LANES))
        parts.append(dr[e])
    bundle = lax.ppermute(jnp.concatenate(parts, axis=0), "ta", [(i, (i + 1) % groups) for i in range(groups)])

    relaxed, residual, coeffs, kept = own(c, dif, dx, dy, xr[0], xr[1], side, dr[0], dr[1])

    at = side.shape[0]
    side_before = bundle[:at]
    xb, db = [], []
    for e in range(n):
        size = 2 * HALO * blocks
        xb.append(bundle[at : at + size].reshape(2, blocks, HALO, LANES).transpose(0, 2, 1, 3).reshape(2, HALO, cols))
        db.append(bundle[at + size : at + size + HALO])
        at += size + HALO
    halos = (xb[0], xb[-1], side_before, db[0], db[-1])
    relaxed, residual, kept = received(3, 1, True, u_last, v_last, *halos, coeffs, kept, relaxed, residual)
    return received(2, 0, False, u_second, v_second, *halos, coeffs, kept, relaxed, residual)


def solution(mesh):
    return jax.shard_map(
        local,
        mesh=mesh,
        in_specs=(
            P(("grp", "ta"), "gx", "gy"),
            P(("grp", "gx"), "gy"),
            P(("grp", "gx"), "gy"),
            P(("grp", "gx"), "gy"),
        ),
        out_specs=(P(("grp", "ta"), "gx", "gy"), P(("grp", "ta"), "gx", "gy")),
        check_vma=False,
    )
```

time: 146 us -> 39.1 us (0.27); the launches traced: 144 us -> 38.9 us
  starting transfers between devices: 71.1 us -> 7.63 us
  waiting for transfers between devices: 46 us -> 0.54 us
  Pallas kernels: 0 us -> 29.9 us
  other arithmetic: 24.7 us -> 0.01 us
    ppermute x34 -> x8, starting transfers between devices: 71.1 us -> 7.63 us  [the longest x1 2.56 us: local(): v_last = lax.ppermute(last, ('ta', 'gy'), odd)]
    ppermute x34 -> x8, waiting for transfers between devices: 46 us -> 0.54 us  [the longest x1 0.52 us: local(): corner = lax.ppermute(ds[0], ('gx', 'gy'), [(0, 3), (3, 0), (1, 2), (2, 1)])]
    pallas_call x0 -> x4, Pallas kernels: none -> 29.9 us  [the longest x1 14.9 us: own(): pl.pallas_call(own_kernel, out_shape=(jax.ShapeDtypeStruct(c.shape, F32),...]
    sub x9 -> x0, other arithmetic: 21.3 us -> none  [the longest x8 21.2 us: local_step(): return field + coeffs[0] * laplace - courant * advect]
    slice x8 -> x0, other arithmetic: 2.28 us -> none  [with_halo(): last = lax.slice_in_dim(x, length - width, length, axis=dim)]
  transfers between devices with their start and end apart: 34 -> 8, of which waited for: 18 -> 1; matrix products, arithmetic and copies ran while one was open for 0% -> 0% of each run, Pallas kernels for 0% -> 55%
where the time goes in v1:
time: 39.1 us; the launch traced here: 38.9 us
  Pallas kernels  29.9 us (76%)
  starting transfers between devices  7.63 us (20%)
  between operations  0.79 us (2%)
  waiting for transfers between devices  0.54 us (1%)
    pallas_call x1, Pallas kernels, own(): pl.pallas_call(own_kernel, out_shape=(jax.ShapeDtypeStruct(c.shape, F32),...  14.9 us
    pallas_call x2, Pallas kernels, received(): pl.pallas_call(functools.partial(received_kernel, f, slot, top), out_shap...  12.6 us
    ppermute x1, starting transfers between devices, local(): v_last = lax.ppermute(last, ('ta', 'gy'), odd)  2.56 us
    ppermute x1, starting transfers between devices, local(): v_second = lax.ppermute(second, ('ta', 'gy'), odd)  2.41 us
    pallas_call x1, Pallas kernels, pack(): pl.pallas_call(functools.partial(pack_kernel, ends), out_shape=(jax.Shape...  2.41 us
    ppermute x1, starting transfers between devices, local(): x = lax.ppermute(xs[0], 'gx', [(0, 1), (1, 0)])  1.28 us
    ppermute x1, starting transfers between devices, local(): side = lax.ppermute(ys, 'gy', [(0, 1), (1, 0)])  0.96 us
  transfers between devices with their start and end apart: 8, of which 1 were waited for; matrix products, arithmetic and copies ran while one was open for 0% of the time, Pallas kernels for 55%

profile of v1, /device:TPU:9, one launch (start us, length us, event | category | flops | bytes accessed | tf_op | source)
XLA Modules:
  0.0 38.9 jit_solution(5892069891734941891)
XLA Ops:
  0.6 0.0 copy-start
  0.6 0.0 copy-start.1
  0.7 0.0 copy-start.2
  0.7 0.0 copy-start.3
  0.7 2.4 %pack.1 = (f32[1,7,8,512]{3,2,1,0:T(8,128)}, f32[128,128]{1,0:T(8,128)}, f32[1,8,128]{2,1,0:T(8,128)}, f32[128,512]{1,0:T(8,128)}, f32[128,512]{1,0:T(8,128)}) custom-call(f32[4,128,512]{2,1,0:T(8,128)} %c.3, f32[128,512]{1,0:T(8,128)} %dif.3, f32[128,512]{1,0:T(8,128)} %dx.3, f32[128,512]{1,0:T(8,128)} %dy.3), custom_call_target="tpu_custom_call" | custom-call | tf_op jit(solution)/shard_map/pack/pallas_call | solution.py:73
  3.1 1.3 %collective-permute-start.3 = (f32[7,8,512]{2,1,0:T(8,128)}, f32[7,8,512]{2,1,0:T(8,128)S(1)}, u32[]{:S(2)}, u32[]{:S(2)}) collective-permute-start(f32[7,8,512]{2,1,0:T(8,128)} %bitcast.17), channel_id=1, source_target_pairs={{0,2},{2,0},{1,3},{3,1},{4,6},{6,4},{5,7},{7,5},{8,10},{10,8},{9,1... | collective-permute-start | bytes 344072 | tf_op jit(solution)/shard_map/ppermute | solution.py:335
  4.4 1.0 %collective-permute-start.2 = (f32[128,128]{1,0:T(8,128)}, f32[128,128]{1,0:T(8,128)S(1)}, u32[]{:S(2)}, u32[]{:S(2)}) collective-permute-start(f32[128,128]{1,0:T(8,128)} %get-tuple-element.15), channel_id=1, source_target_pairs={{0,1},{1,0},{2,3},{3,2},{4,5},{5,4},{6,7},{7,6},{8,9},{9,8},{10,11... | collective-permute-start | bytes 196616 | tf_op jit(solution)/shard_map/ppermute | solution.py:333
  5.3 0.1 collective-permute-start.4
  5.5 0.0 collective-permute-start.6
  5.5 2.6 %collective-permute-start.7 = (f32[128,512]{1,0:T(8,128)}, f32[128,512]{1,0:T(8,128)S(1)}, u32[]{:S(2)}, u32[]{:S(2)}) collective-permute-start(f32[128,512]{1,0:T(8,128)} %get-tuple-element.19), channel_id=1, source_target_pairs={{0,1},{1,0},{4,8},{5,9},{8,4},{9,5},{12,13},{13,12},{2,3},{3,2},{6... | collective-permute-start | bytes 786440 | tf_op jit(solution)/shard_map/ppermute | solution.py:332
  8.1 0.5 %collective-permute-done.4.da.db = f32[8,128]{1,0:T(8,128)S(1)} collective-permute-done((f32[8,128]{1,0:T(8,128)}, f32[8,128]{1,0:T(8,128)S(1)}, u32[]{:S(2)}, u32[]{:S(2)}) %collective-permute-start.4) | collective-permute-done | bytes 4128 | tf_op jit(solution)/shard_map/ppermute | solution.py:336
  8.6 0.2 collective-permute-start
  8.8 0.0 collective-permute-done.3.xa.xb
  8.8 2.4 %collective-permute-start.1 = (f32[128,512]{1,0:T(8,128)}, f32[128,512]{1,0:T(8,128)S(1)}, u32[]{:S(2)}, u32[]{:S(2)}) collective-permute-start(f32[128,512]{1,0:T(8,128)} %get-tuple-element.14), channel_id=1, source_target_pairs={{0,1},{1,0},{4,8},{5,9},{8,4},{9,5},{12,13},{13,12},{2,3},{3,2},{6... | collective-permute-start | bytes 786440 | tf_op jit(solution)/shard_map/ppermute | solution.py:346
  11.2 0.0 collective-permute-done.2.ys
  11.2 0.1 collective-permute-start.5
  11.3 0.0 copy-done
  11.3 0.0 copy-done.1
  11.3 0.0 copy-done.2
  11.3 0.0 copy-done.3
  11.3 14.9 %own.1 = (f32[4,128,512]{2,1,0:T(8,128)}, f32[4,128,512]{2,1,0:T(8,128)}, f32[3,18,8,640]{3,2,1,0:T(8,128)S(1)}, f32[18,8,640]{2,1,0:T(8,128)S(1)}) custom-call(f32[4,128,512]{2,1,0:T(8,128)S(1)} %copy-done, f32[128,512]{1,0:T(8,128)S(1)} %copy-done.1, f32[128,512]{1,0:T(8,128)S(1)} %copy-done.2, f32[128,512]{1,0:T(8,128)S(1)} %copy-done.3, ...), custom_call_target="tpu_custom_call" | custom-call | flops 26214400 | bytes 3145728 | tf_op jit(solution)/shard_map/own/pallas_call | solution.py:234
  26.2 0.0 collective-permute-done.5
  26.3 0.0 collective-permute-done.6.u
  26.3 0.0 collective-permute-done.7.v
  26.3 6.3 %received.2 = (f32[4,128,512]{2,1,0:T(8,128)}, f32[4,128,512]{2,1,0:T(8,128)}, f32[18,8,640]{2,1,0:T(8,128)S(1)}) custom-call(f32[128,512]{1,0:T(8,128)S(1)} %collective-permute-done.6.u, f32[128,512]{1,0:T(8,128)S(1)} %collective-permute-done.7.v, f32[2,8,512]{2,1,0:T(8,128)S(1)} %bitcast.12, ...), custom_call_target="tpu_custom_call", output_to_operand_aliasing={{0}: (9, {}), {1}: (10, {})} | custom-call | flops 10485760 | bytes 1048576 | tf_op jit(solution)/shard_map/received/pallas_call | solution.py:295
  32.6 0.0 collective-permute-done.u
  32.6 0.0 collective-permute-done.1.v
  32.7 6.3 %received.3 = (f32[4,128,512]{2,1,0:T(8,128)}, f32[4,128,512]{2,1,0:T(8,128)}) custom-call(f32[128,512]{1,0:T(8,128)S(1)} %collective-permute-done.u, f32[128,512]{1,0:T(8,128)S(1)} %collective-permute-done.1.v, f32[2,8,512]{2,1,0:T(8,128)S(1)} %bitcast.14, f32[2,8,512]{2,1,0:T(8,128)S(1)} %bitcast.15, ...), custom_call_target="tpu_custom_call", output_to_operand_aliasing={{0}: (9, {}), {1}: (10, {})} | custom-call | flops 10485760 | bytes 1048576 | tf_op jit(solution)/shard_map/received/pallas_call | solution.py:295
  (5 shorter events, 0.0 us)
Async XLA Ops:
  0.6 10.6 %copy-start = (f32[4,128,512]{2,1,0:T(8,128)S(1)}, f32[4,128,512]{2,1,0:T(8,128)}, u32[]{:S(2)}) copy-start(f32[4,128,512]{2,1,0:T(8,128)} %c.3) | copy-start | bytes 3145732
  0.6 10.6 %copy-start.1 = (f32[128,512]{1,0:T(8,128)S(1)}, f32[128,512]{1,0:T(8,128)}, u32[]{:S(2)}) copy-start(f32[128,512]{1,0:T(8,128)} %dif.3) | copy-start | bytes 786436
  0.7 10.6 %copy-start.2 = (f32[128,512]{1,0:T(8,128)S(1)}, f32[128,512]{1,0:T(8,128)}, u32[]{:S(2)}) copy-start(f32[128,512]{1,0:T(8,128)} %dx.3) | copy-start | bytes 786436
  0.7 10.6 %copy-start.3 = (f32[128,512]{1,0:T(8,128)S(1)}, f32[128,512]{1,0:T(8,128)}, u32[]{:S(2)}) copy-start(f32[128,512]{1,0:T(8,128)} %dy.3) | copy-start | bytes 786436
  3.1 5.7 %collective-permute-start.3 = (f32[7,8,512]{2,1,0:T(8,128)}, f32[7,8,512]{2,1,0:T(8,128)S(1)}, u32[]{:S(2)}, u32[]{:S(2)}) collective-permute-start(f32[7,8,512]{2,1,0:T(8,128)} %bitcast.17), channel_id=1, source_target_pairs={{0,2},{2,0},{1,3},{3,1},{4,6},{6,4},{5,7},{7,5},{8,10},{10,8},{9,1... | collective-permute-start | bytes 344072 | tf_op jit(solution)/shard_map/ppermute | solution.py:335
  4.4 6.8 %collective-permute-start.2 = (f32[128,128]{1,0:T(8,128)}, f32[128,128]{1,0:T(8,128)S(1)}, u32[]{:S(2)}, u32[]{:S(2)}) collective-permute-start(f32[128,128]{1,0:T(8,128)} %get-tuple-element.15), channel_id=1, source_target_pairs={{0,1},{1,0},{2,3},{3,2},{4,5},{5,4},{6,7},{7,6},{8,9},{9,8},{10,11... | collective-permute-start | bytes 196616 | tf_op jit(solution)/shard_map/ppermute | solution.py:333
  5.3 3.3 %collective-permute-start.4 = (f32[8,128]{1,0:T(8,128)}, f32[8,128]{1,0:T(8,128)S(1)}, u32[]{:S(2)}, u32[]{:S(2)}) collective-permute-start(f32[8,128]{1,0:T(8,128)} %bitcast.18), channel_id=1, source_target_pairs={{0,3},{3,0},{1,2},{2,1},{4,7},{7,4},{5,6},{6,5},{8,11},{11,8},{9,1... | collective-permute-start | bytes 12296 | tf_op jit(solution)/shard_map/ppermute | solution.py:336
  5.5 20.8 %collective-permute-start.6 = (f32[128,512]{1,0:T(8,128)}, f32[128,512]{1,0:T(8,128)S(1)}, u32[]{:S(2)}, u32[]{:S(2)}) collective-permute-start(f32[128,512]{1,0:T(8,128)} %get-tuple-element.19), channel_id=1, source_target_pairs={{0,4},{1,5},{4,0},{5,1},{8,12},{9,13},{12,8},{13,9},{2,6},{3,7},{6... | collective-permute-start | bytes 786440 | tf_op jit(solution)/shard_map/ppermute | solution.py:331
  5.5 20.8 %collective-permute-start.7 = (f32[128,512]{1,0:T(8,128)}, f32[128,512]{1,0:T(8,128)S(1)}, u32[]{:S(2)}, u32[]{:S(2)}) collective-permute-start(f32[128,512]{1,0:T(8,128)} %get-tuple-element.19), channel_id=1, source_target_pairs={{0,1},{1,0},{4,8},{5,9},{8,4},{9,5},{12,13},{13,12},{2,3},{3,2},{6... | collective-permute-start | bytes 786440 | tf_op jit(solution)/shard_map/ppermute | solution.py:332
  8.6 24.1 %collective-permute-start = (f32[128,512]{1,0:T(8,128)}, f32[128,512]{1,0:T(8,128)S(1)}, u32[]{:S(2)}, u32[]{:S(2)}) collective-permute-start(f32[128,512]{1,0:T(8,128)} %get-tuple-element.14), channel_id=1, source_target_pairs={{0,4},{1,5},{4,0},{5,1},{8,12},{9,13},{12,8},{13,9},{2,6},{3,7},{6... | collective-permute-start | bytes 786440 | tf_op jit(solution)/shard_map/ppermute | solution.py:345
  8.8 23.9 %collective-permute-start.1 = (f32[128,512]{1,0:T(8,128)}, f32[128,512]{1,0:T(8,128)S(1)}, u32[]{:S(2)}, u32[]{:S(2)}) collective-permute-start(f32[128,512]{1,0:T(8,128)} %get-tuple-element.14), channel_id=1, source_target_pairs={{0,1},{1,0},{4,8},{5,9},{8,4},{9,5},{12,13},{13,12},{2,3},{3,2},{6... | collective-permute-start | bytes 786440 | tf_op jit(solution)/shard_map/ppermute | solution.py:346
  11.2 15.1 %collective-permute-start.5 = (f32[200,128]{1,0:T(8,128)S(1)}, f32[200,128]{1,0:T(8,128)S(1)}, u32[]{:S(2)}, u32[]{:S(2)}) collective-permute-start(f32[200,128]{1,0:T(8,128)S(1)} %pad_maximum_fusion), channel_id=1, source_target_pairs={{0,4},{4,8},{8,12},{12,0},{1,5},{5,9},{9,13},{13,1},{2,6},{6,10},{... | collective-permute-start | bytes 307208 | tf_op jit(solution)/shard_map/ppermute | solution.py:355

commit v2 on v0

v2 whole, which is shorter than its diff:
```python
import functools

import jax
import jax.numpy as jnp
from jax import lax
from jax.experimental import pallas as pl
from jax.experimental.pallas import tpu as pltpu
from jax.sharding import PartitionSpec as P

FACTOR = 4
HALO = 2 * FACTOR
LANES = 128
SUBLANES = 8
FIELDS = 7
USED = (4, 5, 6, 0, 1, 2)

courant = 0.08

VMEM = pl.BlockSpec(memory_space=pltpu.VMEM)
HBM = pl.BlockSpec(memory_space=pltpu.HBM)
ANY = pl.BlockSpec(memory_space=pl.ANY)
F32 = jnp.float32
BF16 = jnp.bfloat16


def lane_index(shape):
    return lax.broadcasted_iota(jnp.int32, shape, len(shape) - 1)


def order(cols):
    blocks = cols // LANES
    place = lax.broadcasted_iota(jnp.int32, (cols, cols), 0)
    to = (place % blocks) * LANES + place // blocks
    return jnp.where(lane_index((cols, cols)) == to, 1.0, 0.0).astype(BF16)


def permuted(x, matrix, back=False):
    high = x.astype(BF16)
    rest = x - high.astype(F32)
    middle = rest.astype(BF16)
    low = (rest - middle.astype(F32)).astype(BF16)
    dims = (((1,), (1 if back else 0,)), ((), ()))
    product = functools.partial(lax.dot_general, rhs=matrix, dimension_numbers=dims, preferred_element_type=F32)
    return product(high) + (product(middle) + product(low))


def start(copies):
    for copy in copies:
        copy.start()


def wait(copies):
    for copy in copies:
        copy.wait()


def edge_column(cols):
    return pl.multiple_of((1 - lax.axis_index("gy")) * (cols - LANES), LANES)


def first_row(ends, e, rows):
    if len(ends) == 1:
        return pl.multiple_of((1 - lax.axis_index("gx")) * (rows - HALO), HALO)
    return ends[e] * (rows - HALO)


def pack_kernel(ends, c, dif, dx, dy, *refs):
    n = len(ends)
    xs, (ys, pair, fields, matrix, sems) = refs[:n], refs[n:]
    rows, cols = dif.shape
    gy = lax.axis_index("gy")
    copies = [
        pltpu.make_async_copy(c, fields.at[pl.ds(0, 4)], sems.at[0]),
        pltpu.make_async_copy(dif, fields.at[4], sems.at[1]),
        pltpu.make_async_copy(dx, fields.at[5], sems.at[2]),
        pltpu.make_async_copy(dy, fields.at[6], sems.at[3]),
        pltpu.make_async_copy(c.at[pl.ds(2, 2)], pair, sems.at[4]),
    ]
    start(copies)
    matrix[...] = order(cols)
    wait(copies)
    for e, x in enumerate(xs):
        x[pl.ds(0, FIELDS)] = fields[:, pl.ds(first_row(ends, e, rows), HALO), :]
    lane = lane_index((rows, LANES))
    packed = jnp.zeros((rows, LANES), F32)
    for f in range(FIELDS):
        moved = pltpu.roll(fields[f, :, pl.ds(edge_column(cols), LANES)], f * HALO + HALO * (1 - gy), 1)
        packed = jnp.where((lane >= f * HALO) & (lane < (f + 1) * HALO), moved, packed)
    ys[...] = packed


def pack(ends, c, dif, dx, dy):
    rows, cols = dif.shape
    n = len(ends)
    return pl.pallas_call(
        functools.partial(pack_kernel, ends),
        out_shape=(
            *[jax.ShapeDtypeStruct((FIELDS + 1, HALO, cols), F32)] * n,
            jax.ShapeDtypeStruct((rows, LANES), F32),
            jax.ShapeDtypeStruct((2, rows, cols), F32),
            jax.ShapeDtypeStruct((FIELDS, rows, cols), F32),
            jax.ShapeDtypeStruct((cols, cols), BF16),
        ),
        in_specs=[HBM] * 4,
        out_specs=(VMEM,) * (n + 4),
        scratch_shapes=[pltpu.SemaphoreType.DMA((5,))],
        compiler_params=pltpu.CompilerParams(vmem_limit_bytes=16 << 20),
        name="pack",
    )(*[pltpu.with_memory_space_constraint(x, pltpu.HBM) for x in (c, dif, dx, dy)])


def add_corners_kernel(ends, side, *refs):
    n = len(ends)
    rows = side.shape[0]
    for e in range(n):
        refs[n + e][...] = refs[e][...]
        refs[n + e][FIELDS, :, pl.ds(0, LANES)] = side[pl.ds(first_row(ends, e, rows), HALO), :]


def add_corners(ends, side, xs):
    n = len(xs)
    return pl.pallas_call(
        functools.partial(add_corners_kernel, ends),
        out_shape=[jax.ShapeDtypeStruct(x.shape, F32) for x in xs],
        in_specs=[VMEM] * (n + 1),
        out_specs=[VMEM] * n,
        compiler_params=pltpu.CompilerParams(vmem_limit_bytes=4 << 20),
        name="add_corners",
    )(side, *xs)


def bundle_kernel(side, z, *refs):
    del z
    *xr, out = refs
    rows, cols = side.shape[0], xr[0].shape[2]
    out[pl.ds(0, rows)] = side[...]
    at = rows
    for x in xr:
        out[pl.ds(at, HALO)] = x[FIELDS, :, pl.ds(0, LANES)]
        at += HALO
        for f in (2, 3):
            for k in range(cols // LANES):
                out[pl.ds(at, HALO)] = x[f, :, pl.ds(k * LANES, LANES)]
                at += HALO


def bundle(side, z, xr):
    height = side.shape[0] + len(xr) * HALO * (1 + 2 * (xr[0].shape[2] // LANES))
    return pl.pallas_call(
        bundle_kernel,
        out_shape=jax.ShapeDtypeStruct((height, LANES), F32),
        in_specs=[VMEM, ANY] + [VMEM] * len(xr),
        out_specs=VMEM,
        compiler_params=pltpu.CompilerParams(vmem_limit_bytes=4 << 20),
        name="bundle",
    )(side, z, *xr)


def put_columns(z, begin, value):
    rows, cols = value.shape
    for k in range(cols // LANES):
        z[k, pl.ds(begin, rows)] = value[:, k * LANES : (k + 1) * LANES]


def own_edge(block):
    return pltpu.roll(block, (1 - lax.axis_index("gy")) * (LANES - 1), 1)


def with_halo(block, packed, f):
    gy = lax.axis_index("gy")
    begin = (1 - gy) * (LANES - 1) + gy * (LANES - HALO)
    moved = pltpu.roll(packed, (begin - f * HALO) % LANES, 1)
    return jnp.where((lane_index(block.shape) - begin) % LANES < HALO, moved, block)


def prepare_kernel(fields, matrix, x, z):
    del x
    rows, cols = fields.shape[1:]
    column = pl.ds(edge_column(cols), LANES)
    scales = [1.0 if f == 4 else courant for f in USED]
    for i in range(0, len(USED), 2):
        pair = [fields[USED[i + m]] * scales[i + m] for m in range(2)]
        y = permuted(jnp.concatenate(pair, axis=0), matrix[...])
        for m in range(2):
            put_columns(z.at[i + m], 0, y[m * rows : (m + 1) * rows])
            z[i + m, cols // LANES] = own_edge(fields[USED[i + m], :, column]) * scales[i + m]


def prepare(fields, matrix, x):
    rows, cols = fields.shape[1:]
    n = len(USED)
    return pl.pallas_call(
        prepare_kernel,
        out_shape=jax.ShapeDtypeStruct((n, cols // LANES + 1, rows, LANES), F32),
        in_specs=[VMEM] * 2 + [ANY],
        out_specs=VMEM,
        compiler_params=pltpu.CompilerParams(vmem_limit_bytes=24 << 20),
        cost_estimate=pl.CostEstimate(flops=100 * n * rows * cols, bytes_accessed=2 << 20, transcendentals=0),
        name="prepare",
    )(fields, matrix, x)


def to_strided(z, w):
    count = w.shape[0]
    for r in range(count):
        for k in range(w.shape[1]):
            w[r, k] = z[k, pl.ds(r, SUBLANES, stride=count), :]


def from_strided(z, w, other=None):
    count = w.shape[0]
    for r in range(count):
        for k in range(z.shape[0]):
            value = w[r, k] if other is None else w[r, k] - other[r, k]
            z[k, pl.ds(r, SUBLANES, stride=count), :] = value * (1.0 / courant)


def finish(zs, rows, matrix):
    flat = [
        jnp.concatenate([z[k, pl.ds(HALO, rows)] for k in range(z.shape[0])], axis=1)
        for z in zs
    ]
    return permuted(jnp.concatenate(flat, axis=0), matrix[...], back=True)


def step(w, coeffs):
    count, vectors = w.shape[:2]
    blocks = vectors - 1
    lane = lane_index(w.shape[2:])
    at_left, at_right = lane == 0, lane == LANES - 1
    on_right = lax.axis_index("gy") == 1
    initial = [w[0, k] for k in range(vectors)]
    field = initial
    before = [value - pltpu.roll(w[count - 1, k], 1, 0) for k, value in enumerate(initial)]
    for r in range(count):
        if r < count - 1:
            following = [w[r + 1, k] for k in range(vectors)]
        else:
            following = [pltpu.roll(value, SUBLANES - 1, 0) for value in initial]
        after = [following[k] - field[k] for k in range(vectors)]
        edge = field[blocks] - pltpu.roll(field[blocks], 1, 1)
        begin = jnp.where(on_right, edge, field[0])
        end = jnp.where(on_right, -field[blocks - 1], edge)
        left = [jnp.where(at_left, begin, field[0] - pltpu.roll(field[blocks - 1], 1, 1))]
        left += [field[k] - field[k - 1] for k in range(1, blocks)]
        right = left[1:]
        right.append(jnp.where(at_right, end, pltpu.roll(field[0], LANES - 1, 1) - field[blocks - 1]))
        left.append(edge)
        right.append(pltpu.roll(edge, LANES - 1, 1))
        for k in range(vectors):
            speed_x = coeffs[1, r, k] + field[k]
            speed_y = coeffs[2, r, k] + field[k]
            laplace = (after[k] - before[k]) + (right[k] - left[k])
            upwind_x = jnp.where(speed_x > 0.0, before[k], after[k])
            upwind_y = jnp.where(speed_y > 0.0, left[k], right[k])
            w[r, k] = field[k] + coeffs[0, r, k] * laplace - speed_x * upwind_x - speed_y * upwind_y
        field, before = following, after


def propagate(w, coeffs):
    def body(count, carry):
        step(w, coeffs)
        return carry

    lax.fori_loop(0, FACTOR, body, 0)


def sides_in_grid():
    gx = lax.axis_index("gx")
    return gx > 0, gx < lax.axis_size("gx") - 1


def own_kernel(n, *refs):
    xr, (side, z_in, matrix), refs = refs[:n], refs[n : n + 3], refs[n + 3 :]
    relaxed, residual, coeffs, kept, z, ws, zs, outs, sems = refs
    rows, cols = outs.shape[1:]
    blocks = cols // LANES
    has = sides_in_grid()
    fills = [(0, has[0], 0), (HALO + rows, has[1], n - 1)]
    scale = [1.0 if f == 4 else courant for f in USED]
    halo_rows = [
        permuted(jnp.concatenate([x[f] * s for f, s in zip(USED, scale)], axis=0), matrix[...]) for x in xr
    ]
    for i, f in enumerate(USED):
        z[i, pl.ds(0, blocks), pl.ds(HALO, rows)] = z_in[i, pl.ds(0, blocks)]
        z[i, blocks, pl.ds(HALO, rows)] = with_halo(z_in[i, blocks], side[...] * scale[i], f)
        for begin, there, e in fills:
            y = halo_rows[e][i * HALO : (i + 1) * HALO]
            put_columns(z.at[i], begin, jnp.where(there, y, 0.0))
            block = own_edge(xr[e][f, :, pl.ds(edge_column(cols), LANES)])
            value = with_halo(block, xr[e][FIELDS, :, pl.ds(0, LANES)], f) * scale[i]
            z[i, blocks, pl.ds(begin, HALO)] = jnp.where(there, value, 0.0)
    for i in range(3):
        to_strided(z.at[i], coeffs.at[i])

    def body(m, carry):
        to_strided(z.at[3 + m], ws.at[m])
        propagate(ws.at[m], coeffs)
        from_strided(zs.at[m], ws.at[m])
        return carry

    lax.fori_loop(0, 3, body, 0)
    kept[...] = ws[0]
    values = finish([zs.at[m] for m in range(3)], rows, matrix)
    written = []
    for m in range(3):
        outs[m] = values[m * rows : (m + 1) * rows]
        written.append(pltpu.make_async_copy(outs.at[m], relaxed.at[m + 1], sems.at[m]))
    start(written)

    def body_again(m, carry):
        propagate(ws.at[m], coeffs)
        from_strided(zs.at[m], ws.at[m], ws.at[m + 1])
        return carry

    lax.fori_loop(0, 2, body_again, 0)
    values = finish([zs.at[m] for m in range(2)], rows, matrix)
    for m in range(2):
        outs[3 + m] = values[m * rows : (m + 1) * rows]
        written.append(pltpu.make_async_copy(outs.at[3 + m], residual.at[m + 2], sems.at[3 + m]))
    start(written[3:])
    wait(written)


def own(c, xr, side, z, matrix):
    rows, cols = c.shape[1:]
    height, blocks, n = rows + 2 * HALO, cols // LANES, len(xr)
    strided = (height // SUBLANES, blocks + 1, SUBLANES, LANES)
    return pl.pallas_call(
        functools.partial(own_kernel, n),
        out_shape=(
            jax.ShapeDtypeStruct(c.shape, F32),
            jax.ShapeDtypeStruct(c.shape, F32),
            jax.ShapeDtypeStruct((3, *strided), F32),
            jax.ShapeDtypeStruct(strided, F32),
        ),
        in_specs=[VMEM] * (n + 3),
        out_specs=(HBM, HBM, VMEM, VMEM),
        scratch_shapes=[
            pltpu.VMEM((len(USED), blocks + 1, height, LANES), F32),
            pltpu.VMEM((3, *strided), F32),
            pltpu.VMEM((3, blocks, height, LANES), F32),
            pltpu.VMEM((5, rows, cols), F32),
            pltpu.SemaphoreType.DMA((5,)),
        ],
        compiler_params=pltpu.CompilerParams(vmem_limit_bytes=24 << 20),
        cost_estimate=pl.CostEstimate(flops=2000 * rows * cols, bytes_accessed=3 << 20, transcendentals=0),
        name="own",
    )(*xr, side, z, matrix)


def received_kernel(n, pair, halos, fields, coeffs, base, matrix, relaxed_in, residual_in, relaxed, residual, z, ws, zs, outs, sems):
    del relaxed_in, residual_in
    rows, cols = pair.shape[1:]
    blocks = cols // LANES
    has = sides_in_grid()
    first = lax.axis_index("ta") == 0
    targets = [relaxed.at[0], residual.at[0], residual.at[1]]

    @pl.when(first)
    def _():
        outs[0] = jnp.zeros_like(outs[0])
        sources = [fields.at[0], outs.at[0], outs.at[0]]
        copies = [pltpu.make_async_copy(*ends, sems.at[i]) for i, ends in enumerate(zip(sources, targets))]
        start(copies)
        wait(copies)

    @pl.when(jnp.logical_not(first))
    def _():
        at = rows
        corners, parts = [], []
        for e in range(n):
            corners.append(halos[pl.ds(at, HALO)])
            at += HALO
            parts.append([])
            for m in range(2):
                line = [halos[pl.ds(at + k * HALO, HALO)] for k in range(blocks)]
                parts[e].append(jnp.concatenate(line, axis=1))
                at += blocks * HALO
        packed = [jnp.where(has[0], corners[0], 0.0), halos[pl.ds(0, rows)], jnp.where(has[1], corners[n - 1], 0.0)]
        packed = jnp.concatenate(packed, axis=0)
        x = []
        for m in range(2):
            x += [jnp.where(has[0], parts[0][m], 0.0), pair[m], jnp.where(has[1], parts[n - 1][m], 0.0)]
        y = permuted(jnp.concatenate(x, axis=0) * courant, matrix[...])
        height = rows + 2 * HALO
        column = pl.ds(edge_column(cols), LANES)
        for m in range(2):
            put_columns(z.at[m], 0, y[m * height : (m + 1) * height])
            z[m, blocks, pl.ds(HALO, rows)] = own_edge(pair[m, :, column])
        for e, begin, k in ((0, 0, 0), (n - 1, HALO + rows, 1)):
            for m in range(2):
                left, right = parts[e][m][:, :LANES], parts[e][m][:, cols - LANES :]
                block = jnp.where(has[k], jnp.where(lax.axis_index("gy") == 0, right, left), 0.0)
                z[m, blocks, pl.ds(begin, HALO)] = own_edge(block)
        for m in range(2):
            z[m, blocks] = with_halo(z[m, blocks], packed, 2 + m) * courant

        def body(m, carry):
            to_strided(z.at[m], ws.at[m])
            propagate(ws.at[m], coeffs)
            return carry

        lax.fori_loop(0, 2, body, 0)
        from_strided(zs.at[0], ws.at[1])
        propagate(ws.at[0], coeffs)
        from_strided(zs.at[1], ws.at[0], ws.at[1])
        propagate(ws.at[1], coeffs)
        from_strided(zs.at[2], ws.at[1], base)
        values = finish([zs.at[m] for m in range(3)], rows, matrix)
        copies = []
        for m, target in enumerate(targets):
            outs[m] = values[m * rows : (m + 1) * rows]
            copies.append(pltpu.make_async_copy(outs.at[m], target, sems.at[m]))
        start(copies)
        wait(copies)


def received(n, pair, halos, fields, coeffs, base, matrix, relaxed, residual):
    rows, cols = pair.shape[1:]
    strided, height, blocks = base.shape, rows + 2 * HALO, cols // LANES
    shape = jax.ShapeDtypeStruct(relaxed.shape, F32)
    return pl.pallas_call(
        functools.partial(received_kernel, n),
        out_shape=(shape, shape),
        in_specs=[VMEM] * 6 + [HBM] * 2,
        out_specs=(HBM, HBM),
        scratch_shapes=[
            pltpu.VMEM((2, blocks + 1, height, LANES), F32),
            pltpu.VMEM((2, *strided), F32),
            pltpu.VMEM((3, blocks, height, LANES), F32),
            pltpu.VMEM((3, rows, cols), F32),
            pltpu.SemaphoreType.DMA((3,)),
        ],
        input_output_aliases={6: 0, 7: 1},
        compiler_params=pltpu.CompilerParams(vmem_limit_bytes=24 << 20),
        cost_estimate=pl.CostEstimate(flops=1600 * rows * cols, bytes_accessed=2 << 20, transcendentals=0),
        name="received",
    )(pair, halos, fields, coeffs, base, matrix, relaxed, residual)


def local(c, dif, dx, dy):
    groups, nx, ny = (lax.axis_size(name) for name in ("ta", "gx", "gy"))
    rows, cols = dif.shape
    assert ny == 2 and c.shape[0] == 4 and rows % SUBLANES == 0 and cols % LANES == 0
    ends = (1,) if nx == 2 else (1, 0)
    ring = [(i, (i + 1) % groups) for i in range(groups)]
    *xs, ys, pair, fields, matrix = pack(ends, c, dif, dx, dy)
    side = lax.ppermute(ys, "gy", [(0, 1), (1, 0)])
    pair = lax.ppermute(pair, "ta", ring)
    xs = add_corners(ends, side, xs)
    if nx == 2:
        xr = [lax.ppermute(xs[0], "gx", [(0, 1), (1, 0)])]
    else:
        hops = [[(i, i + hop) for i in range(nx) if 0 <= i + hop < nx] for hop in (1, -1)]
        xr = [lax.ppermute(x, "gx", pairs) for x, pairs in zip(xs, hops)]
    z = prepare(fields, matrix, xs[0])
    halos = lax.ppermute(bundle(side, z, xr), "ta", ring)
    relaxed, residual, coeffs, kept = own(c, xr, side, z, matrix)
    return received(len(ends), pair, halos, fields, coeffs, kept, matrix, relaxed, residual)


def solution(mesh):
    return jax.shard_map(
        local,
        mesh=mesh,
        in_specs=(
            P(("grp", "ta"), "gx", "gy"),
            P(("grp", "gx"), "gy"),
            P(("grp", "gx"), "gy"),
            P(("grp", "gx"), "gy"),
        ),
        out_specs=(P(("grp", "ta"), "gx", "gy"), P(("grp", "ta"), "gx", "gy")),
        check_vma=False,
    )
```

time: 146 us -> 27.4 us (0.19)
  the two profiles are of different devices: /device:TPU:9 before, /device:TPU:10 now
where the time goes in v2:
time: 27.4 us; the launch traced here: 27.3 us
  Pallas kernels  17.9 us (65%)
  waiting for transfers between devices  4.86 us (18%)
  starting transfers between devices  3.86 us (14%)
  between operations  0.68 us (2%)
    pallas_call x1, Pallas kernels, own(): pl.pallas_call(functools.partial(own_kernel, n), out_shape=(jax.ShapeDtyp...  8.05 us
    pallas_call x1, Pallas kernels, received(): pl.pallas_call(functools.partial(received_kernel, n), out_shape=(shape, s...  6.54 us
    ppermute x1, waiting for transfers between devices, local(): xr = [lax.ppermute(xs[0], 'gx', [(0, 1), (1, 0)])]  3.61 us
    pallas_call x1, Pallas kernels, pack(): pl.pallas_call(functools.partial(pack_kernel, ends), out_shape=(*[jax.Sha...  1.83 us
    ppermute x1, starting transfers between devices, local(): pair = lax.ppermute(pair, 'ta', ring)  1.63 us
    ppermute x1, starting transfers between devices, local(): halos = lax.ppermute(bundle(side, z, xr), 'ta', ring)  1.63 us
    pallas_call x1, Pallas kernels, prepare(): pl.pallas_call(prepare_kernel, out_shape=jax.ShapeDtypeStruct((n, cols //...  1.42 us
    ppermute x1, waiting for transfers between devices, local(): side = lax.ppermute(ys, 'gy', [(0, 1), (1, 0)])  1.25 us
  transfers between devices with their start and end apart: 4, of which 2 were waited for; matrix products, arithmetic and copies ran while one was open for 0% of the time, Pallas kernels for 35%

profile of v2, /device:TPU:10, one launch (start us, length us, event | category | flops | bytes accessed | tf_op | source)
XLA Modules:
  0.0 27.3 jit_solution(13489968634179026079)
XLA Ops:
  0.6 1.8 %pack.1 = (f32[8,8,512]{2,1,0:T(8,128)S(1)}, f32[128,128]{1,0:T(8,128)S(1)}, f32[2,128,512]{2,1,0:T(8,128)S(1)}, f32[7,128,512]{2,1,0:T(8,128)S(1)}, bf16[512,512]{1,0:T(8,128)(2,1)S(1)}) custom-call(f32[4,128,512]{2,1,0:T(8,128)} %c.1, f32[128,512]{1,0:T(8,128)} %dif.1, f32[128,512]{1,0:T(8,128)} %dx.1, f32[128,512]{1,0:T(8,128)} %dy.1), custom_call_target="tpu_custom_call" | custom-call | tf_op jit(solution)/shard_map/pack/pallas_call | solution.py:95
  2.5 1.6 %collective-permute-start = (f32[2,128,512]{2,1,0:T(8,128)S(1)}, f32[2,128,512]{2,1,0:T(8,128)S(1)}, u32[]{:S(2)}, u32[]{:S(2)}) collective-permute-start(f32[2,128,512]{2,1,0:T(8,128)S(1)} %get-tuple-element.11), channel_id=1, source_target_pairs={{0,4},{4,8},{8,12},{12,0},{1,5},{5,9},{9,13},{13,1},{2,6},{6,10},{... | collective-permute-start | bytes 1572872 | tf_op jit(solution)/shard_map/ppermute | solution.py:450
  4.1 0.0 collective-permute-start.1
  4.1 1.3 %collective-permute-done.1.side.refs_1_ = f32[128,128]{1,0:T(8,128)S(1)} collective-permute-done((f32[128,128]{1,0:T(8,128)S(1)}, f32[128,128]{1,0:T(8,128)S(1)}, u32[]{:S(2)}, u32[]{:S(2)}) %collective-permute-start.1) | collective-permute-done | bytes 65568 | tf_op jit(solution)/shard_map/ppermute | solution.py:449
  5.4 0.6 %collective-permute-start.2 = (f32[8,8,512]{2,1,0:T(8,128)S(1)}, f32[8,8,512]{2,1,0:T(8,128)S(1)}, u32[]{:S(2)}, u32[]{:S(2)}) collective-permute-start(f32[8,8,512]{2,1,0:T(8,128)S(1)} %add_corners.1.x), channel_id=1, source_target_pairs={{0,2},{2,0},{1,3},{3,1},{4,6},{6,4},{5,7},{7,5},{8,10},{10,8},{9,1... | collective-permute-start | bytes 393224 | tf_op jit(solution)/shard_map/ppermute | solution.py:453
  6.0 1.4 %prepare.1.z.refs_2_ = f32[6,5,128,128]{3,2,1,0:T(8,128)S(1)} custom-call(f32[7,128,512]{2,1,0:T(8,128)S(1)} %get-tuple-element.13.fields, bf16[512,512]{1,0:T(8,128)(2,1)S(1)} %get-tuple-element.14.matrix.refs_3_, f32[8,8,512]{2,1,0:T(8,128)S(1)} %add_corners.1.x), custom_call_target="tpu_custom_call" | custom-call | flops 39321600 | bytes 2097152 | tf_op jit(solution)/shard_map/prepare/pallas_call | solution.py:192
  7.4 3.6 %collective-permute-done.2.refs_0_ = f32[8,8,512]{2,1,0:T(8,128)S(1)} collective-permute-done((f32[8,8,512]{2,1,0:T(8,128)S(1)}, f32[8,8,512]{2,1,0:T(8,128)S(1)}, u32[]{:S(2)}, u32[]{:S(2)}) %collective-permute-start.2) | collective-permute-done | bytes 131104 | tf_op jit(solution)/shard_map/ppermute | solution.py:453
  11.0 1.6 %collective-permute-start.3 = (f32[200,128]{1,0:T(8,128)S(1)}, f32[200,128]{1,0:T(8,128)S(1)}, u32[]{:S(2)}, u32[]{:S(2)}) collective-permute-start(f32[200,128]{1,0:T(8,128)S(1)} %bundle.1), channel_id=1, source_target_pairs={{0,4},{4,8},{8,12},{12,0},{1,5},{5,9},{9,13},{13,1},{2,6},{6,10},{... | collective-permute-start | bytes 307208 | tf_op jit(solution)/shard_map/ppermute | solution.py:458
  12.6 8.1 %own.1 = (f32[4,128,512]{2,1,0:T(8,128)}, f32[4,128,512]{2,1,0:T(8,128)}, f32[3,18,5,8,128]{4,3,2,1,0:T(8,128)S(1)}, f32[18,5,8,128]{3,2,1,0:T(8,128)S(1)}) custom-call(f32[8,8,512]{2,1,0:T(8,128)S(1)} %collective-permute-done.2.refs_0_, f32[128,128]{1,0:T(8,128)S(1)} %collective-permute-done.1.side.refs_1_, f32[6,5,128,128]{3,2,1,0:T(8,128)S(1)} %prepare.1.z.refs_2_, ...), custom_call_target="tpu_custom_call" | custom-call | flops 131072000 | bytes 3145728 | tf_op jit(solution)/shard_map/own/pallas_call | solution.py:329
  20.7 0.0 collective-permute-done.3.halos
  20.7 0.0 collective-permute-done.pair
  20.7 6.5 %received.1 = (f32[4,128,512]{2,1,0:T(8,128)}, f32[4,128,512]{2,1,0:T(8,128)}) custom-call(f32[2,128,512]{2,1,0:T(8,128)S(1)} %collective-permute-done.pair, f32[200,128]{1,0:T(8,128)S(1)} %collective-permute-done.3.halos, f32[7,128,512]{2,1,0:T(8,128)S(1)} %get-tuple-element.13.fields, ...), custom_call_target="tpu_custom_call", output_to_operand_aliasing={{0}: (6, {}), {1}: (7, {})} | custom-call | flops 104857600 | bytes 2097152 | tf_op jit(solution)/shard_map/received/pallas_call | solution.py:423
  (2 shorter events, 0.0 us)
Async XLA Ops:
  2.5 18.2 %collective-permute-start = (f32[2,128,512]{2,1,0:T(8,128)S(1)}, f32[2,128,512]{2,1,0:T(8,128)S(1)}, u32[]{:S(2)}, u32[]{:S(2)}) collective-permute-start(f32[2,128,512]{2,1,0:T(8,128)S(1)} %get-tuple-element.11), channel_id=1, source_target_pairs={{0,4},{4,8},{8,12},{12,0},{1,5},{5,9},{9,13},{13,1},{2,6},{6,10},{... | collective-permute-start | bytes 1572872 | tf_op jit(solution)/shard_map/ppermute | solution.py:450
  4.1 1.3 %collective-permute-start.1 = (f32[128,128]{1,0:T(8,128)S(1)}, f32[128,128]{1,0:T(8,128)S(1)}, u32[]{:S(2)}, u32[]{:S(2)}) collective-permute-start(f32[128,128]{1,0:T(8,128)S(1)} %get-tuple-element.12), channel_id=1, source_target_pairs={{0,1},{1,0},{2,3},{3,2},{4,5},{5,4},{6,7},{7,6},{8,9},{9,8},{10,11... | collective-permute-start | bytes 196616 | tf_op jit(solution)/shard_map/ppermute | solution.py:449
  5.4 5.6 %collective-permute-start.2 = (f32[8,8,512]{2,1,0:T(8,128)S(1)}, f32[8,8,512]{2,1,0:T(8,128)S(1)}, u32[]{:S(2)}, u32[]{:S(2)}) collective-permute-start(f32[8,8,512]{2,1,0:T(8,128)S(1)} %add_corners.1.x), channel_id=1, source_target_pairs={{0,2},{2,0},{1,3},{3,1},{4,6},{6,4},{5,7},{7,5},{8,10},{10,8},{9,1... | collective-permute-start | bytes 393224 | tf_op jit(solution)/shard_map/ppermute | solution.py:453
  11.0 9.7 %collective-permute-start.3 = (f32[200,128]{1,0:T(8,128)S(1)}, f32[200,128]{1,0:T(8,128)S(1)}, u32[]{:S(2)}, u32[]{:S(2)}) collective-permute-start(f32[200,128]{1,0:T(8,128)S(1)} %bundle.1), channel_id=1, source_target_pairs={{0,4},{4,8},{8,12},{12,0},{1,5},{5,9},{9,13},{13,1},{2,6},{6,10},{... | collective-permute-start | bytes 307208 | tf_op jit(solution)/shard_map/ppermute | solution.py:458

commit v3 on v2

--- a/solution.py
+++ b/solution.py
@@ -66,7 +66,7 @@
 
 def pack_kernel(ends, c, dif, dx, dy, *refs):
     n = len(ends)
-    xs, (ys, pair, fields, matrix, sems) = refs[:n], refs[n:]
+    xs, ds, (ys, fields, matrix, sems) = refs[:n], refs[n : 2 * n], refs[2 * n :]
     rows, cols = dif.shape
     gy = lax.axis_index("gy")
     copies = [
@@ -74,19 +74,20 @@
         pltpu.make_async_copy(dif, fields.at[4], sems.at[1]),
         pltpu.make_async_copy(dx, fields.at[5], sems.at[2]),
         pltpu.make_async_copy(dy, fields.at[6], sems.at[3]),
-        pltpu.make_async_copy(c.at[pl.ds(2, 2)], pair, sems.at[4]),
     ]
     start(copies)
     matrix[...] = order(cols)
     wait(copies)
     for e, x in enumerate(xs):
-        x[pl.ds(0, FIELDS)] = fields[:, pl.ds(first_row(ends, e, rows), HALO), :]
+        x[...] = fields[:, pl.ds(first_row(ends, e, rows), HALO), :]
     lane = lane_index((rows, LANES))
     packed = jnp.zeros((rows, LANES), F32)
     for f in range(FIELDS):
         moved = pltpu.roll(fields[f, :, pl.ds(edge_column(cols), LANES)], f * HALO + HALO * (1 - gy), 1)
         packed = jnp.where((lane >= f * HALO) & (lane < (f + 1) * HALO), moved, packed)
     ys[...] = packed
+    for e, d in enumerate(ds):
+        d[...] = ys[pl.ds(first_row(ends, e, rows), HALO), :]
 
 
 def pack(ends, c, dif, dx, dy):
@@ -95,48 +96,43 @@
     return pl.pallas_call(
         functools.partial(pack_kernel, ends),
         out_shape=(
-            *[jax.ShapeDtypeStruct((FIELDS + 1, HALO, cols), F32)] * n,
+            *[jax.ShapeDtypeStruct((FIELDS, HALO, cols), F32)] * n,
+            *[jax.ShapeDtypeStruct((HALO, LANES), F32)] * n,
             jax.ShapeDtypeStruct((rows, LANES), F32),
-            jax.ShapeDtypeStruct((2, rows, cols), F32),
             jax.ShapeDtypeStruct((FIELDS, rows, cols), F32),
             jax.ShapeDtypeStruct((cols, cols), BF16),
         ),
         in_specs=[HBM] * 4,
-        out_specs=(VMEM,) * (n + 4),
-        scratch_shapes=[pltpu.SemaphoreType.DMA((5,))],
+        out_specs=(VMEM,) * (2 * n + 3),
+        scratch_shapes=[pltpu.SemaphoreType.DMA((4,))],
         compiler_params=pltpu.CompilerParams(vmem_limit_bytes=16 << 20),
         name="pack",
     )(*[pltpu.with_memory_space_constraint(x, pltpu.HBM) for x in (c, dif, dx, dy)])
 
 
-def add_corners_kernel(ends, side, *refs):
-    n = len(ends)
-    rows = side.shape[0]
-    for e in range(n):
-        refs[n + e][...] = refs[e][...]
-        refs[n + e][FIELDS, :, pl.ds(0, LANES)] = side[pl.ds(first_row(ends, e, rows), HALO), :]
-
-
-def add_corners(ends, side, xs):
-    n = len(xs)
-    return pl.pallas_call(
-        functools.partial(add_corners_kernel, ends),
-        out_shape=[jax.ShapeDtypeStruct(x.shape, F32) for x in xs],
-        in_specs=[VMEM] * (n + 1),
-        out_specs=[VMEM] * n,
-        compiler_params=pltpu.CompilerParams(vmem_limit_bytes=4 << 20),
-        name="add_corners",
-    )(side, *xs)
-
-
-def bundle_kernel(side, z, *refs):
+def take_kernel(fields, pair):
+    pair[...] = fields[pl.ds(2, 2)]
+
+
+def take(fields):
+    return pl.pallas_call(
+        take_kernel,
+        out_shape=jax.ShapeDtypeStruct((2, *fields.shape[1:]), F32),
+        in_specs=[VMEM],
+        out_specs=VMEM,
+        compiler_params=pltpu.CompilerParams(vmem_limit_bytes=8 << 20),
+        name="take",
+    )(fields)
+
+
+def bundle_kernel(n, side, z, *refs):
     del z
-    *xr, out = refs
+    xr, dr, out = refs[:n], refs[n : 2 * n], refs[2 * n]
     rows, cols = side.shape[0], xr[0].shape[2]
     out[pl.ds(0, rows)] = side[...]
     at = rows
-    for x in xr:
-        out[pl.ds(at, HALO)] = x[FIELDS, :, pl.ds(0, LANES)]
+    for x, d in zip(xr, dr):
+        out[pl.ds(at, HALO)] = d[...]
         at += HALO
         for f in (2, 3):
             for k in range(cols // LANES):
@@ -144,16 +140,17 @@
                 at += HALO
 
 
-def bundle(side, z, xr):
-    height = side.shape[0] + len(xr) * HALO * (1 + 2 * (xr[0].shape[2] // LANES))
-    return pl.pallas_call(
-        bundle_kernel,
+def bundle(side, z, xr, dr):
+    n = len(xr)
+    height = side.shape[0] + n * HALO * (1 + 2 * (xr[0].shape[2] // LANES))
+    return pl.pallas_call(
+        functools.partial(bundle_kernel, n),
         out_shape=jax.ShapeDtypeStruct((height, LANES), F32),
-        in_specs=[VMEM, ANY] + [VMEM] * len(xr),
+        in_specs=[VMEM, ANY] + [VMEM] * (2 * n),
         out_specs=VMEM,
         compiler_params=pltpu.CompilerParams(vmem_limit_bytes=4 << 20),
         name="bundle",
-    )(side, z, *xr)
+    )(side, z, *xr, *dr)
 
 
 def put_columns(z, begin, value):
@@ -195,7 +192,7 @@
         in_specs=[VMEM] * 2 + [ANY],
         out_specs=VMEM,
         compiler_params=pltpu.CompilerParams(vmem_limit_bytes=24 << 20),
-        cost_estimate=pl.CostEstimate(flops=100 * n * rows * cols, bytes_accessed=2 << 20, transcendentals=0),
+        cost_estimate=pl.CostEstimate(flops=100 * n * rows * cols, bytes_accessed=6 << 20, transcendentals=0),
         name="prepare",
     )(fields, matrix, x)
 
@@ -271,7 +268,7 @@
 
 
 def own_kernel(n, *refs):
-    xr, (side, z_in, matrix), refs = refs[:n], refs[n : n + 3], refs[n + 3 :]
+    xr, dr, (side, z_in, matrix), refs = refs[:n], refs[n : 2 * n], refs[2 * n : 2 * n + 3], refs[2 * n + 3 :]
     relaxed, residual, coeffs, kept, z, ws, zs, outs, sems = refs
     rows, cols = outs.shape[1:]
     blocks = cols // LANES
@@ -288,7 +285,7 @@
             y = halo_rows[e][i * HALO : (i + 1) * HALO]
             put_columns(z.at[i], begin, jnp.where(there, y, 0.0))
             block = own_edge(xr[e][f, :, pl.ds(edge_column(cols), LANES)])
-            value = with_halo(block, xr[e][FIELDS, :, pl.ds(0, LANES)], f) * scale[i]
+            value = with_halo(block, dr[e][...], f) * scale[i]
             z[i, blocks, pl.ds(begin, HALO)] = jnp.where(there, value, 0.0)
     for i in range(3):
         to_strided(z.at[i], coeffs.at[i])
@@ -322,7 +319,7 @@
     wait(written)
 
 
-def own(c, xr, side, z, matrix):
+def own(c, xr, dr, side, z, matrix):
     rows, cols = c.shape[1:]
     height, blocks, n = rows + 2 * HALO, cols // LANES, len(xr)
     strided = (height // SUBLANES, blocks + 1, SUBLANES, LANES)
@@ -334,7 +331,7 @@
             jax.ShapeDtypeStruct((3, *strided), F32),
             jax.ShapeDtypeStruct(strided, F32),
         ),
-        in_specs=[VMEM] * (n + 3),
+        in_specs=[VMEM] * (2 * n + 3),
         out_specs=(HBM, HBM, VMEM, VMEM),
         scratch_shapes=[
             pltpu.VMEM((len(USED), blocks + 1, height, LANES), F32),
@@ -344,9 +341,9 @@
             pltpu.SemaphoreType.DMA((5,)),
         ],
         compiler_params=pltpu.CompilerParams(vmem_limit_bytes=24 << 20),
-        cost_estimate=pl.CostEstimate(flops=2000 * rows * cols, bytes_accessed=3 << 20, transcendentals=0),
+        cost_estimate=pl.CostEstimate(flops=2000 * rows * cols, bytes_accessed=30 << 20, transcendentals=0),
         name="own",
-    )(*xr, side, z, matrix)
+    )(*xr, *dr, side, z, matrix)
 
 
 def received_kernel(n, pair, halos, fields, coeffs, base, matrix, relaxed_in, residual_in, relaxed, residual, z, ws, zs, outs, sems):
@@ -434,7 +431,7 @@
         ],
         input_output_aliases={6: 0, 7: 1},
         compiler_params=pltpu.CompilerParams(vmem_limit_bytes=24 << 20),
-        cost_estimate=pl.CostEstimate(flops=1600 * rows * cols, bytes_accessed=2 << 20, transcendentals=0),
+        cost_estimate=pl.CostEstimate(flops=1600 * rows * cols, bytes_accessed=24 << 20, transcendentals=0),
         name="received",
     )(pair, halos, fields, coeffs, base, matrix, relaxed, residual)
 
@@ -445,19 +442,23 @@
     assert ny == 2 and c.shape[0] == 4 and rows % SUBLANES == 0 and cols % LANES == 0
     ends = (1,) if nx == 2 else (1, 0)
     ring = [(i, (i + 1) % groups) for i in range(groups)]
-    *xs, ys, pair, fields, matrix = pack(ends, c, dif, dx, dy)
-    side = lax.ppermute(ys, "gy", [(0, 1), (1, 0)])
-    pair = lax.ppermute(pair, "ta", ring)
-    xs = add_corners(ends, side, xs)
+    n = len(ends)
+    *sent, ys, fields, matrix = pack(ends, c, dif, dx, dy)
+    xs, ds = sent[:n], sent[n:]
     if nx == 2:
         xr = [lax.ppermute(xs[0], "gx", [(0, 1), (1, 0)])]
+        dr = [lax.ppermute(ds[0], ("gx", "gy"), [(0, 3), (3, 0), (1, 2), (2, 1)])]
     else:
         hops = [[(i, i + hop) for i in range(nx) if 0 <= i + hop < nx] for hop in (1, -1)]
         xr = [lax.ppermute(x, "gx", pairs) for x, pairs in zip(xs, hops)]
-    z = prepare(fields, matrix, xs[0])
-    halos = lax.ppermute(bundle(side, z, xr), "ta", ring)
-    relaxed, residual, coeffs, kept = own(c, xr, side, z, matrix)
-    return received(len(ends), pair, halos, fields, coeffs, kept, matrix, relaxed, residual)
+        crossed = [[(i * 2 + s, j * 2 + 1 - s) for i, j in pairs for s in range(2)] for pairs in hops]
+        dr = [lax.ppermute(d, ("gx", "gy"), pairs) for d, pairs in zip(ds, crossed)]
+    side = lax.ppermute(ys, "gy", [(0, 1), (1, 0)])
+    pair = lax.ppermute(take(fields), "ta", ring)
+    z = prepare(fields, matrix, side)
+    halos = lax.ppermute(bundle(side, z, xr, dr), "ta", ring)
+    relaxed, residual, coeffs, kept = own(c, xr, dr, side, z, matrix)
+    return received(n, pair, halos, fields, coeffs, kept, matrix, relaxed, residual)
 
 
 def solution(mesh):

time: 27.4 us -> 25.6 us (0.934)
  the two profiles are of different devices: /device:TPU:10 before, /device:TPU:9 now
where the time goes in v3:
time: 25.6 us; the launch traced here: 25.5 us
  Pallas kernels  17.7 us (69%)
  starting transfers between devices  5.29 us (21%)
  waiting for transfers between devices  1.76 us (7%)
  between operations  0.68 us (3%)
    pallas_call x1, Pallas kernels, own(): pl.pallas_call(functools.partial(own_kernel, n), out_shape=(jax.ShapeDtyp...  8.06 us
    pallas_call x1, Pallas kernels, received(): pl.pallas_call(functools.partial(received_kernel, n), out_shape=(shape, s...  6.57 us
    pallas_call x1, Pallas kernels, pack(): pl.pallas_call(functools.partial(pack_kernel, ends), out_shape=(*[jax.Sha...  1.65 us
    pallas_call x1, Pallas kernels, prepare(): pl.pallas_call(prepare_kernel, out_shape=jax.ShapeDtypeStruct((n, cols //...  1.43 us
    ppermute x1, starting transfers between devices, local(): pair = lax.ppermute(take(fields), 'ta', ring)  1.35 us
    ppermute x1, starting transfers between devices, local(): halos = lax.ppermute(bundle(side, z, xr, dr), 'ta', ring)  1.35 us
    ppermute x1, starting transfers between devices, local(): side = lax.ppermute(ys, 'gy', [(0, 1), (1, 0)])  1.24 us
    ppermute x1, starting transfers between devices, local(): xr = [lax.ppermute(xs[0], 'gx', [(0, 1), (1, 0)])]  1.21 us
  transfers between devices with their start and end apart: 5, of which 2 were waited for; matrix products, arithmetic and copies ran while one was open for 0% of the time, Pallas kernels for 37%

profile of v3, /device:TPU:9, one launch (start us, length us, event | category | flops | bytes accessed | tf_op | source)
XLA Modules:
  0.0 25.5 jit_solution(8134633203383689025)
XLA Ops:
  0.6 1.6 %pack.1 = (f32[7,8,512]{2,1,0:T(8,128)S(1)}, f32[8,128]{1,0:T(8,128)S(1)}, f32[128,128]{1,0:T(8,128)S(1)}, f32[7,128,512]{2,1,0:T(8,128)S(1)}, bf16[512,512]{1,0:T(8,128)(2,1)S(1)}) custom-call(f32[4,128,512]{2,1,0:T(8,128)} %c.1, f32[128,512]{1,0:T(8,128)} %dif.1, f32[128,512]{1,0:T(8,128)} %dx.1, f32[128,512]{1,0:T(8,128)} %dy.1), custom_call_target="tpu_custom_call" | custom-call | tf_op jit(solution)/shard_map/pack/pallas_call | solution.py:96
  2.3 1.3 %collective-permute-start = (f32[2,128,512]{2,1,0:T(8,128)S(1)}, f32[2,128,512]{2,1,0:T(8,128)S(1)}, u32[]{:S(2)}, u32[]{:S(2)}) collective-permute-start(f32[2,128,512]{2,1,0:T(8,128)S(1)} %take.1), channel_id=1, source_target_pairs={{0,4},{4,8},{8,12},{12,0},{1,5},{5,9},{9,13},{13,1},{2,6},{6,10},{... | collective-permute-start | bytes 1572872 | tf_op jit(solution)/shard_map/ppermute | solution.py:457
  3.7 1.2 %collective-permute-start.2 = (f32[7,8,512]{2,1,0:T(8,128)S(1)}, f32[7,8,512]{2,1,0:T(8,128)S(1)}, u32[]{:S(2)}, u32[]{:S(2)}) collective-permute-start(f32[7,8,512]{2,1,0:T(8,128)S(1)} %get-tuple-element.14), channel_id=1, source_target_pairs={{0,2},{2,0},{1,3},{3,1},{4,6},{6,4},{5,7},{7,5},{8,10},{10,8},{9,1... | collective-permute-start | bytes 344072 | tf_op jit(solution)/shard_map/ppermute | solution.py:449
  4.9 1.2 %collective-permute-start.1 = (f32[128,128]{1,0:T(8,128)S(1)}, f32[128,128]{1,0:T(8,128)S(1)}, u32[]{:S(2)}, u32[]{:S(2)}) collective-permute-start(f32[128,128]{1,0:T(8,128)S(1)} %get-tuple-element.12), channel_id=1, source_target_pairs={{0,1},{1,0},{2,3},{3,2},{4,5},{5,4},{6,7},{7,6},{8,9},{9,8},{10,11... | collective-permute-start | bytes 196616 | tf_op jit(solution)/shard_map/ppermute | solution.py:456
  6.1 0.1 collective-permute-start.3
  6.3 0.8 %collective-permute-done.1.x.side.refs_2_ = f32[128,128]{1,0:T(8,128)S(1)} collective-permute-done((f32[128,128]{1,0:T(8,128)S(1)}, f32[128,128]{1,0:T(8,128)S(1)}, u32[]{:S(2)}, u32[]{:S(2)}) %collective-permute-start.1) | collective-permute-done | bytes 65568 | tf_op jit(solution)/shard_map/ppermute | solution.py:456
  7.0 1.4 %prepare.1.z.refs_3_ = f32[6,5,128,128]{3,2,1,0:T(8,128)S(1)} custom-call(f32[7,128,512]{2,1,0:T(8,128)S(1)} %get-tuple-element.11.fields, bf16[512,512]{1,0:T(8,128)(2,1)S(1)} %get-tuple-element.13.matrix.refs_4_, f32[128,128]{1,0:T(8,128)S(1)} %collective-permute-done.1.x.side.refs_2_), custom_call_target="tpu_custom_call" | custom-call | flops 39321600 | bytes 6291456 | tf_op jit(solution)/shard_map/prepare/pallas_call | solution.py:189
  8.5 1.0 %collective-permute-done.3.refs_1_ = f32[8,128]{1,0:T(8,128)S(1)} collective-permute-done((f32[8,128]{1,0:T(8,128)S(1)}, f32[8,128]{1,0:T(8,128)S(1)}, u32[]{:S(2)}, u32[]{:S(2)}) %collective-permute-start.3) | collective-permute-done | bytes 4128 | tf_op jit(solution)/shard_map/ppermute | solution.py:450
  9.5 0.0 collective-permute-done.2.refs_0_
  9.5 1.3 %collective-permute-start.4 = (f32[200,128]{1,0:T(8,128)S(1)}, f32[200,128]{1,0:T(8,128)S(1)}, u32[]{:S(2)}, u32[]{:S(2)}) collective-permute-start(f32[200,128]{1,0:T(8,128)S(1)} %bundle.1), channel_id=1, source_target_pairs={{0,4},{4,8},{8,12},{12,0},{1,5},{5,9},{9,13},{13,1},{2,6},{6,10},{... | collective-permute-start | bytes 307208 | tf_op jit(solution)/shard_map/ppermute | solution.py:459
  10.8 8.1 %own.1 = (f32[4,128,512]{2,1,0:T(8,128)}, f32[4,128,512]{2,1,0:T(8,128)}, f32[3,18,5,8,128]{4,3,2,1,0:T(8,128)S(1)}, f32[18,5,8,128]{3,2,1,0:T(8,128)S(1)}) custom-call(f32[7,8,512]{2,1,0:T(8,128)S(1)} %collective-permute-done.2.refs_0_, f32[8,128]{1,0:T(8,128)S(1)} %collective-permute-done.3.refs_1_, f32[128,128]{1,0:T(8,128)S(1)} %collective-permute-done.1.x.side.refs_2_, ...), custom_call_target="tpu_custom_call" | custom-call | flops 131072000 | bytes 31457280 | tf_op jit(solution)/shard_map/own/pallas_call | solution.py:326
  18.9 0.0 collective-permute-done.4.halos
  18.9 0.0 collective-permute-done.pair
  18.9 6.6 %received.1 = (f32[4,128,512]{2,1,0:T(8,128)}, f32[4,128,512]{2,1,0:T(8,128)}) custom-call(f32[2,128,512]{2,1,0:T(8,128)S(1)} %collective-permute-done.pair, f32[200,128]{1,0:T(8,128)S(1)} %collective-permute-done.4.halos, f32[7,128,512]{2,1,0:T(8,128)S(1)} %get-tuple-element.11.fields, ...), custom_call_target="tpu_custom_call", output_to_operand_aliasing={{0}: (6, {}), {1}: (7, {})} | custom-call | flops 104857600 | bytes 25165824 | tf_op jit(solution)/shard_map/received/pallas_call | solution.py:420
  (2 shorter events, 0.0 us)
Async XLA Ops:
  2.3 16.6 %collective-permute-start = (f32[2,128,512]{2,1,0:T(8,128)S(1)}, f32[2,128,512]{2,1,0:T(8,128)S(1)}, u32[]{:S(2)}, u32[]{:S(2)}) collective-permute-start(f32[2,128,512]{2,1,0:T(8,128)S(1)} %take.1), channel_id=1, source_target_pairs={{0,4},{4,8},{8,12},{12,0},{1,5},{5,9},{9,13},{13,1},{2,6},{6,10},{... | collective-permute-start | bytes 1572872 | tf_op jit(solution)/shard_map/ppermute | solution.py:457
  3.7 5.8 %collective-permute-start.2 = (f32[7,8,512]{2,1,0:T(8,128)S(1)}, f32[7,8,512]{2,1,0:T(8,128)S(1)}, u32[]{:S(2)}, u32[]{:S(2)}) collective-permute-start(f32[7,8,512]{2,1,0:T(8,128)S(1)} %get-tuple-element.14), channel_id=1, source_target_pairs={{0,2},{2,0},{1,3},{3,1},{4,6},{6,4},{5,7},{7,5},{8,10},{10,8},{9,1... | collective-permute-start | bytes 344072 | tf_op jit(solution)/shard_map/ppermute | solution.py:449
  4.9 2.1 %collective-permute-start.1 = (f32[128,128]{1,0:T(8,128)S(1)}, f32[128,128]{1,0:T(8,128)S(1)}, u32[]{:S(2)}, u32[]{:S(2)}) collective-permute-start(f32[128,128]{1,0:T(8,128)S(1)} %get-tuple-element.12), channel_id=1, source_target_pairs={{0,1},{1,0},{2,3},{3,2},{4,5},{5,4},{6,7},{7,6},{8,9},{9,8},{10,11... | collective-permute-start | bytes 196616 | tf_op jit(solution)/shard_map/ppermute | solution.py:456
  6.1 3.3 %collective-permute-start.3 = (f32[8,128]{1,0:T(8,128)S(1)}, f32[8,128]{1,0:T(8,128)S(1)}, u32[]{:S(2)}, u32[]{:S(2)}) collective-permute-start(f32[8,128]{1,0:T(8,128)S(1)} %get-tuple-element.15), channel_id=1, source_target_pairs={{0,3},{3,0},{1,2},{2,1},{4,7},{7,4},{5,6},{6,5},{8,11},{11,8},{9,1... | collective-permute-start | bytes 12296 | tf_op jit(solution)/shard_map/ppermute | solution.py:450
  9.5 9.4 %collective-permute-start.4 = (f32[200,128]{1,0:T(8,128)S(1)}, f32[200,128]{1,0:T(8,128)S(1)}, u32[]{:S(2)}, u32[]{:S(2)}) collective-permute-start(f32[200,128]{1,0:T(8,128)S(1)} %bundle.1), channel_id=1, source_target_pairs={{0,4},{4,8},{8,12},{12,0},{1,5},{5,9},{9,13},{13,1},{2,6},{6,10},{... | collective-permute-start | bytes 307208 | tf_op jit(solution)/shard_map/ppermute | solution.py:459

commit v4 on v3

v4 whole, which is shorter than its diff:
```python
import functools

import jax
import jax.numpy as jnp
from jax import lax
from jax.experimental import pallas as pl
from jax.experimental.pallas import tpu as pltpu
from jax.sharding import PartitionSpec as P

FACTOR = 4
HALO = 2 * FACTOR
LANES = 128
SUBLANES = 8
FOLDS = LANES // (2 * HALO)
FIELDS = 7
USED = (4, 5, 6, 0, 1, 2)

courant = 0.08

VMEM = pl.BlockSpec(memory_space=pltpu.VMEM)
HBM = pl.BlockSpec(memory_space=pltpu.HBM)
ANY = pl.BlockSpec(memory_space=pl.ANY)
F32 = jnp.float32
BF16 = jnp.bfloat16


def lane_index(shape):
    return lax.broadcasted_iota(jnp.int32, shape, len(shape) - 1)


def order(cols):
    blocks = cols // LANES
    place = lax.broadcasted_iota(jnp.int32, (cols, cols), 0)
    to = (place % blocks) * LANES + place // blocks
    return jnp.where(lane_index((cols, cols)) == to, 1.0, 0.0).astype(BF16)


def permuted(x, matrix):
    high = x.astype(BF16)
    rest = x - high.astype(F32)
    middle = rest.astype(BF16)
    low = (rest - middle.astype(F32)).astype(BF16)
    product = functools.partial(jnp.dot, preferred_element_type=F32)
    return product(high, matrix) + (product(middle, matrix) + product(low, matrix))


def restored(x, matrix):
    high = x.astype(BF16)
    low = (x - high.astype(F32)).astype(BF16)
    dims = (((1,), (1,)), ((), ()))
    product = functools.partial(lax.dot_general, dimension_numbers=dims, preferred_element_type=F32)
    return product(high, matrix) + product(low, matrix)


def start(copies):
    for copy in copies:
        copy.start()


def wait(copies):
    for copy in copies:
        copy.wait()


def place():
    return lax.axis_index("gx"), lax.axis_index("gy")


def edge_column(cols, gy):
    return pl.multiple_of((1 - gy) * (cols - LANES), LANES)


def first_row(ends, e, rows, gx):
    if len(ends) == 1:
        return pl.multiple_of((1 - gx) * (rows - HALO), HALO)
    return ends[e] * (rows - HALO)


def pack_kernel(ends, c, fixed, *refs):
    n = len(ends)
    xs, ds, (ys, matrix) = refs[:n], refs[n : 2 * n], refs[2 * n :]
    rows, cols = fixed.shape[1:]
    gx, gy = place()
    fields = [*[c.at[f] for f in range(4)], *[fixed.at[i] for i in range(3)]]
    lane = lane_index((rows, LANES))
    packed = jnp.zeros((rows, LANES), F32)
    for f, field in enumerate(fields):
        for e, x in enumerate(xs):
            x[f] = field[pl.ds(first_row(ends, e, rows, gx), HALO), :]
        moved = pltpu.roll(field[:, pl.ds(edge_column(cols, gy), LANES)], f * HALO + HALO * (1 - gy), 1)
        packed = jnp.where((lane >= f * HALO) & (lane < (f + 1) * HALO), moved, packed)
    ys[...] = packed
    for e, d in enumerate(ds):
        d[...] = ys[pl.ds(first_row(ends, e, rows, gx), HALO), :]
    matrix[...] = order(cols)


def pack(ends, c, fixed):
    rows, cols = fixed.shape[1:]
    n = len(ends)
    return pl.pallas_call(
        functools.partial(pack_kernel, ends),
        out_shape=(
            *[jax.ShapeDtypeStruct((FIELDS, HALO, cols), F32)] * n,
            *[jax.ShapeDtypeStruct((HALO, LANES), F32)] * n,
            jax.ShapeDtypeStruct((rows, LANES), F32),
            jax.ShapeDtypeStruct((cols, cols), BF16),
        ),
        in_specs=[VMEM] * 2,
        out_specs=(VMEM,) * (2 * n + 2),
        compiler_params=pltpu.CompilerParams(vmem_limit_bytes=16 << 20),
        name="pack",
    )(c, fixed)


def take_kernel(c, dif, dx, dy, pair, fixed, sems):
    copies = [pltpu.make_async_copy(c.at[pl.ds(2, 2)], pair, sems.at[3])]
    copies += [pltpu.make_async_copy(ref, fixed.at[i], sems.at[i]) for i, ref in enumerate((dif, dx, dy))]
    start(copies)
    wait(copies)


def take(c, dif, dx, dy):
    return pl.pallas_call(
        take_kernel,
        out_shape=[jax.ShapeDtypeStruct((count, *dif.shape), F32) for count in (2, 3)],
        in_specs=[HBM] * 4,
        out_specs=[VMEM] * 2,
        scratch_shapes=[pltpu.SemaphoreType.DMA((4,))],
        compiler_params=pltpu.CompilerParams(vmem_limit_bytes=4 << 20),
        name="take",
    )(*[pltpu.with_memory_space_constraint(x, pltpu.HBM) for x in (c, dif, dx, dy)])


def bundle_kernel(n, side, z, *refs):
    del z
    xr, dr, out = refs[:n], refs[n : 2 * n], refs[2 * n]
    cols = xr[0].shape[2]
    fold = side.shape[0] // FOLDS
    lane = lane_index((fold, LANES))
    folded = jnp.zeros((fold, LANES), F32)
    for j in range(FOLDS):
        begin = 2 * HALO * j
        moved = pltpu.roll(side[pl.ds(j * fold, fold), :], (begin - 2 * HALO) % LANES, 1)
        folded = jnp.where((lane >= begin) & (lane < begin + 2 * HALO), moved, folded)
    out[pl.ds(0, fold)] = folded
    at = fold
    for x, d in zip(xr, dr):
        out[pl.ds(at, HALO)] = d[...]
        at += HALO
        for f in (2, 3):
            for k in range(cols // LANES):
                out[pl.ds(at, HALO)] = x[f, :, pl.ds(k * LANES, LANES)]
                at += HALO


def bundle(side, z, xr, dr):
    n = len(xr)
    height = side.shape[0] // FOLDS + n * HALO * (1 + 2 * (xr[0].shape[2] // LANES))
    return pl.pallas_call(
        functools.partial(bundle_kernel, n),
        out_shape=jax.ShapeDtypeStruct((height, LANES), F32),
        in_specs=[VMEM, ANY] + [VMEM] * (2 * n),
        out_specs=VMEM,
        compiler_params=pltpu.CompilerParams(vmem_limit_bytes=4 << 20),
        name="bundle",
    )(side, z, *xr, *dr)


def put_columns(z, begin, value):
    rows, cols = value.shape
    for k in range(cols // LANES):
        z[k, pl.ds(begin, rows)] = value[:, k * LANES : (k + 1) * LANES]


def own_edge(block, gy):
    return pltpu.roll(block, (1 - gy) * (LANES - 1), 1)


def with_halo(block, packed, f, gy):
    return inserted(block, moved_to_halo(packed, f * HALO, gy), gy)


def moved_to_halo(value, lane, gy):
    return pltpu.roll(value, (halo_lane(gy) - lane) % LANES, 1)


def halo_lane(gy):
    return (1 - gy) * (LANES - 1) + gy * (LANES - HALO)


def inserted(block, moved, gy):
    return jnp.where((lane_index(block.shape) - halo_lane(gy)) % LANES < HALO, moved, block)


def fills(n, rows, gx):
    if n == 1:
        return [(rows, None, 0)]
    return [(rows, gx < lax.axis_size("gx") - 1, 1), (rows + HALO, gx > 0, 0)]


def masked(there, value):
    return value if there is None else jnp.where(there, value, 0.0)


def prepare_kernel(c, fixed, matrix, z):
    _, gy = place()
    rows, cols = fixed.shape[1:]
    fields = [*[c.at[f] for f in range(4)], *[fixed.at[i] for i in range(3)]]
    column = pl.ds(edge_column(cols, gy), LANES)
    scales = [1.0 if f == 4 else courant for f in USED]
    for i in range(0, len(USED), 2):
        pair = [fields[USED[i + m]][...] * scales[i + m] for m in range(2)]
        y = permuted(jnp.concatenate(pair, axis=0), matrix[...])
        for m in range(2):
            put_columns(z.at[i + m], 0, y[m * rows : (m + 1) * rows])
            z[i + m, cols // LANES] = own_edge(fields[USED[i + m]][:, column], gy) * scales[i + m]


def prepare(c, fixed, matrix):
    rows, cols = fixed.shape[1:]
    n = len(USED)
    return pl.pallas_call(
        prepare_kernel,
        out_shape=jax.ShapeDtypeStruct((n, cols // LANES + 1, rows, LANES), F32),
        in_specs=[VMEM] * 3,
        out_specs=VMEM,
        compiler_params=pltpu.CompilerParams(vmem_limit_bytes=24 << 20),
        cost_estimate=pl.CostEstimate(flops=100 * n * rows * cols, bytes_accessed=6 << 20, transcendentals=0),
        name="prepare",
    )(c, fixed, matrix)


def to_strided(z, w):
    count = w.shape[0]
    for r in range(count):
        for k in range(w.shape[1]):
            w[r, k] = z[k, pl.ds(r, SUBLANES, stride=count), :]


def from_strided(z, w):
    count = w.shape[0]
    for r in range(count):
        for k in range(z.shape[0]):
            z[k, pl.ds(r, SUBLANES, stride=count), :] = w[r, k] * (1.0 / courant)


def finish(ws, targets, matrix, zs, outs, sems):
    rows = outs.shape[1]
    flat = []
    for i, w in enumerate(ws):
        from_strided(zs.at[i], w)
        flat.append(jnp.concatenate([zs[i, k, pl.ds(0, rows)] for k in range(zs.shape[1])], axis=1))
    values = restored(jnp.concatenate(flat, axis=0), matrix[...])
    copies = []
    for i, target in enumerate(targets):
        outs[i] = values[i * rows : (i + 1) * rows]
        copies.append(pltpu.make_async_copy(outs.at[i], target, sems.at[i]))
    start(copies)
    return copies


def step(rows, gx, gy, w, coeffs):
    count, vectors = w.shape[:2]
    blocks = vectors - 1
    lane, sublane = lane_index(w.shape[2:]), lax.broadcasted_iota(jnp.int32, w.shape[2:], 0)
    at_left, at_right = lane == 0, lane == LANES - 1
    on_right = gy == 1
    cut = lax.axis_size("gx") == 2
    last_sublane, last_row = divmod(rows - 1, count)
    assert last_row < count - 1
    none_above = sublane == jnp.where(gx == 0, 0, -1)
    none_below = sublane == jnp.where(gx == 1, last_sublane, -1)
    initial = [w[0, k] for k in range(vectors)]
    field = initial
    above = [pltpu.roll(w[count - 1, k], 1, 0) for k in range(vectors)]
    if cut:
        above = [jnp.where(none_above, 0.0, value) for value in above]
    before = [field[k] - above[k] for k in range(vectors)]
    for r in range(count):
        if r < count - 1:
            following = [w[r + 1, k] for k in range(vectors)]
        else:
            following = [pltpu.roll(value, SUBLANES - 1, 0) for value in initial]
        below = following
        if cut and r == last_row:
            below = [jnp.where(none_below, 0.0, value) for value in following]
        after = [below[k] - field[k] for k in range(vectors)]
        edge = field[blocks] - pltpu.roll(field[blocks], 1, 1)
        begin = jnp.where(on_right, edge, field[0])
        end = jnp.where(on_right, -field[blocks - 1], edge)
        left = [jnp.where(at_left, begin, field[0] - pltpu.roll(field[blocks - 1], 1, 1))]
        left += [field[k] - field[k - 1] for k in range(1, blocks)]
        right = left[1:]
        right.append(jnp.where(at_right, end, pltpu.roll(field[0], LANES - 1, 1) - field[blocks - 1]))
        left.append(edge)
        right.append(pltpu.roll(edge, LANES - 1, 1))
        for k in range(vectors):
            speed_x = coeffs[1, r, k] + field[k]
            speed_y = coeffs[2, r, k] + field[k]
            laplace = (after[k] - before[k]) + (right[k] - left[k])
            upwind_x = jnp.where(speed_x > 0.0, before[k], after[k])
            upwind_y = jnp.where(speed_y > 0.0, left[k], right[k])
            w[r, k] = field[k] + coeffs[0, r, k] * laplace - speed_x * upwind_x - speed_y * upwind_y
        field, before = following, after


def propagate(rows, gx, gy, w, coeffs):
    def body(count, carry):
        step(rows, gx, gy, w, coeffs)
        return carry

    lax.fori_loop(0, FACTOR, body, 0)


def layout(n, rows, cols):
    height = rows + n * HALO
    return height, (height // SUBLANES, cols // LANES + 1, SUBLANES, LANES)


def own_kernel(n, *refs):
    xr, dr, (side, z_in, matrix), refs = refs[:n], refs[n : 2 * n], refs[2 * n : 2 * n + 3], refs[2 * n + 3 :]
    coeffs, once, difference, relaxed, z, ws, zs, outs, sems = refs
    rows, cols = z_in.shape[2], matrix.shape[0]
    blocks = cols // LANES
    gx, gy = place()
    scale = [1.0 if f == 4 else courant for f in USED]
    halo_rows = [
        permuted(jnp.concatenate([x[f] * s for f, s in zip(USED, scale)], axis=0), matrix[...]) for x in xr
    ]
    for i, f in enumerate(USED):
        z[i, pl.ds(0, blocks), pl.ds(0, rows)] = z_in[i, pl.ds(0, blocks)]
        z[i, blocks, pl.ds(0, rows)] = with_halo(z_in[i, blocks], side[...] * scale[i], f, gy)
        for begin, there, which in fills(n, rows, gx):
            y = halo_rows[which][i * HALO : (i + 1) * HALO]
            put_columns(z.at[i], begin, masked(there, y))
            block = own_edge(xr[which][f, :, pl.ds(edge_column(cols, gy), LANES)], gy)
            z[i, blocks, pl.ds(begin, HALO)] = masked(there, with_halo(block, dr[which][...], f, gy) * scale[i])
    for i in range(3):
        to_strided(z.at[i], coeffs.at[i])

    def body(m, carry):
        to_strided(z.at[3 + m], ws.at[m])
        propagate(rows, gx, gy, ws.at[m], coeffs)
        once[m] = ws[m, :, pl.ds(0, blocks)]
        return carry

    lax.fori_loop(0, 3, body, 0)
    targets = [relaxed.at[m + 1] for m in range(3)]
    written = finish([once.at[m] for m in range(3)], targets, matrix, zs, outs, sems)

    def body_again(m, carry):
        propagate(rows, gx, gy, ws.at[m], coeffs)
        difference[m] = ws[m, :, pl.ds(0, blocks)] - once[m + 1]
        return carry

    lax.fori_loop(0, 2, body_again, 0)
    wait(written)


def own(xr, dr, side, z, matrix):
    n, (rows, cols) = len(xr), (z.shape[2], matrix.shape[0])
    height, strided = layout(n, rows, cols)
    body = (strided[0], strided[1] - 1, *strided[2:])
    return pl.pallas_call(
        functools.partial(own_kernel, n),
        out_shape=(
            jax.ShapeDtypeStruct((3, *strided), F32),
            jax.ShapeDtypeStruct((3, *body), F32),
            jax.ShapeDtypeStruct((2, *body), F32),
            jax.ShapeDtypeStruct((4, rows, cols), F32),
        ),
        in_specs=[VMEM] * (2 * n + 3),
        out_specs=(VMEM, VMEM, VMEM, HBM),
        scratch_shapes=[
            pltpu.VMEM((len(USED), strided[1], height, LANES), F32),
            pltpu.VMEM((3, *strided), F32),
            pltpu.VMEM((3, strided[1] - 1, height, LANES), F32),
            pltpu.VMEM((3, rows, cols), F32),
            pltpu.SemaphoreType.DMA((3,)),
        ],
        compiler_params=pltpu.CompilerParams(vmem_limit_bytes=24 << 20),
        cost_estimate=pl.CostEstimate(flops=2000 * rows * cols, bytes_accessed=30 << 20, transcendentals=0),
        name="own",
    )(*xr, *dr, side, z, matrix)


def received_kernel(n, pair, halos, c, coeffs, once, difference, matrix, relaxed_in, *refs):
    relaxed, residual, z, ws, late, zs, outs, sems = refs
    del relaxed_in
    rows, cols = pair.shape[1:]
    blocks, height = cols // LANES, z.shape[2]
    first = lax.axis_index("ta") == 0
    gx, gy = place()
    sources = [difference.at[m] for m in range(2)]
    targets = [residual.at[m + 2] for m in range(2)]
    count = len(sources)
    written = finish(sources, targets, matrix, zs, outs, sems)
    targets = [relaxed.at[0], residual.at[0], residual.at[1]]
    late_outs, late_sems = outs.at[pl.ds(count, 3)], sems.at[pl.ds(count, 3)]

    @pl.when(first)
    def _():
        late_outs[0] = c[0]
        late_outs[1] = jnp.zeros_like(late_outs[1])
        values = [late_outs.at[0], late_outs.at[1], late_outs.at[1]]
        copies = [pltpu.make_async_copy(*ends, late_sems.at[i]) for i, ends in enumerate(zip(values, targets))]
        start(copies)
        wait(copies)

    @pl.when(jnp.logical_not(first))
    def _():
        at = fold = rows // FOLDS
        folded = halos[pl.ds(0, fold)]
        corners, parts = [], []
        for e in range(n):
            corners.append(halos[pl.ds(at, HALO)])
            at += HALO
            parts.append([])
            for m in range(2):
                line = [halos[pl.ds(at + k * HALO, HALO)] for k in range(blocks)]
                parts[e].append(jnp.concatenate(line, axis=1))
                at += blocks * HALO
        places = fills(n, rows, gx)
        x = []
        for m in range(2):
            x += [pair[m]] + [masked(there, parts[which][m]) for _, there, which in places]
        y = permuted(jnp.concatenate(x, axis=0) * courant, matrix[...])
        for m in range(2):
            put_columns(z.at[m], 0, y[m * height : (m + 1) * height])
            block = [pair[m, :, pl.ds(edge_column(cols, gy), LANES)]]
            for _, there, which in places:
                left, right = parts[which][m][:, :LANES], parts[which][m][:, cols - LANES :]
                block.append(masked(there, jnp.where(gy == 0, right, left)))
            block = own_edge(jnp.concatenate(block, axis=0), gy)
            moved = [moved_to_halo(folded, (2 * j + m) * HALO, gy) for j in range(FOLDS)]
            for _, there, which in places:
                moved.append(masked(there, moved_to_halo(corners[which], (2 + m) * HALO, gy)))
            z[m, blocks] = inserted(block, jnp.concatenate(moved, axis=0), gy) * courant

        def body(m, carry):
            to_strided(z.at[m], ws.at[m])
            propagate(rows, gx, gy, ws.at[m], coeffs)
            return carry

        lax.fori_loop(0, 2, body, 0)
        body_part = pl.ds(0, blocks)
        late[0] = ws[1, :, body_part]

        def body_again(m, carry):
            propagate(rows, gx, gy, ws.at[m], coeffs)
            return carry

        lax.fori_loop(0, 2, body_again, 0)
        late[1] = ws[0, :, body_part] - late[0]
        late[2] = ws[1, :, body_part] - once[0]
        wait(finish([late.at[m] for m in range(3)], targets, matrix, zs, late_outs, late_sems))

    wait(written)


def received(n, pair, halos, c, coeffs, once, difference, matrix, relaxed):
    rows, cols = pair.shape[1:]
    blocks = cols // LANES
    height, strided = layout(n, rows, cols)
    shape = jax.ShapeDtypeStruct((4, rows, cols), F32)
    return pl.pallas_call(
        functools.partial(received_kernel, n),
        out_shape=(shape, shape),
        in_specs=[VMEM] * 7 + [HBM],
        out_specs=(HBM, HBM),
        input_output_aliases={7: 0},
        scratch_shapes=[
            pltpu.VMEM((2, blocks + 1, height, LANES), F32),
            pltpu.VMEM((2, *strided), F32),
            pltpu.VMEM((3, *once.shape[1:]), F32),
            pltpu.VMEM((3, blocks, height, LANES), F32),
            pltpu.VMEM((5, rows, cols), F32),
            pltpu.SemaphoreType.DMA((5,)),
        ],
        compiler_params=pltpu.CompilerParams(vmem_limit_bytes=24 << 20),
        cost_estimate=pl.CostEstimate(flops=1600 * rows * cols, bytes_accessed=24 << 20, transcendentals=0),
        name="received",
    )(pair, halos, c, coeffs, once, difference, matrix, relaxed)


def local(c, dif, dx, dy):
    groups, nx, ny = (lax.axis_size(name) for name in ("ta", "gx", "gy"))
    rows, cols = dif.shape
    assert ny == 2 and c.shape[0] == 4 and rows % SUBLANES == 0 and cols % LANES == 0
    ends = (1,) if nx == 2 else (1, 0)
    ring = [(i, (i + 1) % groups) for i in range(groups)]
    n = len(ends)
    pair, fixed = take(c, dif, dx, dy)
    *sent, ys, matrix = pack(ends, c, fixed)
    xs, ds = sent[:n], sent[n:]
    if nx == 2:
        xr = [lax.ppermute(xs[0], "gx", [(0, 1), (1, 0)])]
        dr = [lax.ppermute(ds[0], ("gx", "gy"), [(0, 3), (3, 0), (1, 2), (2, 1)])]
    else:
        hops = [[(i, i + hop) for i in range(nx) if 0 <= i + hop < nx] for hop in (1, -1)]
        xr = [lax.ppermute(x, "gx", pairs) for x, pairs in zip(xs, hops)]
        crossed = [[(i * 2 + s, j * 2 + 1 - s) for i, j in pairs for s in range(2)] for pairs in hops]
        dr = [lax.ppermute(d, ("gx", "gy"), pairs) for d, pairs in zip(ds, crossed)]
    side = lax.ppermute(ys, "gy", [(0, 1), (1, 0)])
    pair = lax.ppermute(pair, "ta", ring)
    z = prepare(c, fixed, matrix)
    halos = lax.ppermute(bundle(side, z, xr, dr), "ta", ring)
    coeffs, once, difference, relaxed = own(xr, dr, side, z, matrix)
    return received(n, pair, halos, c, coeffs, once, difference, matrix, relaxed)


def solution(mesh):
    return jax.shard_map(
        local,
        mesh=mesh,
        in_specs=(
            P(("grp", "ta"), "gx", "gy"),
            P(("grp", "gx"), "gy"),
            P(("grp", "gx"), "gy"),
            P(("grp", "gx"), "gy"),
        ),
        out_specs=(P(("grp", "ta"), "gx", "gy"), P(("grp", "ta"), "gx", "gy")),
        check_vma=False,
    )
```

time: 25.6 us -> 24.1 us (0.941)
  Pallas kernels: 17.7 us -> 16.2 us
    pallas_call x1, Pallas kernels: 8.06 us -> 6.25 us  [own(): pl.pallas_call(functools.partial(own_kernel, n), out_shape=(jax.ShapeDtyp...]
    pallas_call x1, Pallas kernels: 0.04 us -> 1.39 us  [take(): pl.pallas_call(take_kernel, out_shape=[jax.ShapeDtypeStruct((count, *dif....]
    pallas_call x1, Pallas kernels: 1.65 us -> 0.33 us  [pack(): pl.pallas_call(functools.partial(pack_kernel, ends), out_shape=(*[jax.Sha...]
    ppermute x1, waiting for transfers between devices: 0.99 us -> 1.77 us  [local(): dr = [lax.ppermute(ds[0], ('gx', 'gy'), [(0, 3), (3, 0), (1, 2), (2, 1)])]]
    ppermute x1, waiting for transfers between devices: 0.76 us -> 0.01 us  [local(): side = lax.ppermute(ys, 'gy', [(0, 1), (1, 0)])]
  transfers between devices with their start and end apart: 5 -> 5, of which waited for: 2 -> 1; matrix products, arithmetic and copies ran while one was open for 0% -> 0% of each run, Pallas kernels for 37% -> 34%
where the time goes in v4:
time: 24.1 us; the launch traced here: 24 us
  Pallas kernels  16.2 us (67%)
  starting transfers between devices  5.35 us (22%)
  waiting for transfers between devices  1.79 us (7%)
  between operations  0.69 us (3%)
    pallas_call x1, Pallas kernels, received(): pl.pallas_call(functools.partial(received_kernel, n), out_shape=(shape, s...  6.7 us
    pallas_call x1, Pallas kernels, own(): pl.pallas_call(functools.partial(own_kernel, n), out_shape=(jax.ShapeDtyp...  6.25 us
    ppermute x1, waiting for transfers between devices, local(): dr = [lax.ppermute(ds[0], ('gx', 'gy'), [(0, 3), (3, 0), (1, 2), (2, 1)])]  1.77 us
    pallas_call x1, Pallas kernels, prepare(): pl.pallas_call(prepare_kernel, out_shape=jax.ShapeDtypeStruct((n, cols //...  1.41 us
    pallas_call x1, Pallas kernels, take(): pl.pallas_call(take_kernel, out_shape=[jax.ShapeDtypeStruct((count, *dif....  1.39 us
    ppermute x1, starting transfers between devices, local(): pair = lax.ppermute(pair, 'ta', ring)  1.35 us
    ppermute x1, starting transfers between devices, local(): halos = lax.ppermute(bundle(side, z, xr, dr), 'ta', ring)  1.35 us
    ppermute x1, starting transfers between devices, local(): xr = [lax.ppermute(xs[0], 'gx', [(0, 1), (1, 0)])]  1.28 us
  transfers between devices with their start and end apart: 5, of which 1 were waited for; matrix products, arithmetic and copies ran while one was open for 0% of the time, Pallas kernels for 34%

profile of v4, /device:TPU:9, one launch (start us, length us, event | category | flops | bytes accessed | tf_op | source)
XLA Modules:
  0.0 24.0 jit_solution(12213264924835190126)
XLA Ops:
  0.6 0.0 copy-start
  0.6 1.4 %take.1 = (f32[2,128,512]{2,1,0:T(8,128)S(1)}, f32[3,128,512]{2,1,0:T(8,128)S(1)}) custom-call(f32[4,128,512]{2,1,0:T(8,128)} %c.7, f32[128,512]{1,0:T(8,128)} %dif.1, f32[128,512]{1,0:T(8,128)} %dx.1, f32[128,512]{1,0:T(8,128)} %dy.1), custom_call_target="tpu_custom_call" | custom-call | tf_op jit(solution)/shard_map/take/pallas_call | solution.py:124
  2.0 1.3 %collective-permute-start = (f32[2,128,512]{2,1,0:T(8,128)S(1)}, f32[2,128,512]{2,1,0:T(8,128)S(1)}, u32[]{:S(2)}, u32[]{:S(2)}) collective-permute-start(f32[2,128,512]{2,1,0:T(8,128)S(1)} %get-tuple-element.12), channel_id=1, source_target_pairs={{0,4},{4,8},{8,12},{12,0},{1,5},{5,9},{9,13},{13,1},{2,6},{6,10},{... | collective-permute-start | bytes 1572872 | tf_op jit(solution)/shard_map/ppermute | solution.py:506
  3.4 0.0 copy-done
  3.4 0.3 %pack.1 = (f32[7,8,512]{2,1,0:T(8,128)S(1)}, f32[8,128]{1,0:T(8,128)S(1)}, f32[128,128]{1,0:T(8,128)S(1)}, bf16[512,512]{1,0:T(8,128)(2,1)S(1)}) custom-call(f32[4,128,512]{2,1,0:T(8,128)S(1)} %copy-done, f32[3,128,512]{2,1,0:T(8,128)S(1)} %get-tuple-element.13.fixed), custom_call_target="tpu_custom_call" | custom-call | tf_op jit(solution)/shard_map/pack/pallas_call | solution.py:101
  3.7 1.3 %collective-permute-start.2 = (f32[7,8,512]{2,1,0:T(8,128)S(1)}, f32[7,8,512]{2,1,0:T(8,128)S(1)}, u32[]{:S(2)}, u32[]{:S(2)}) collective-permute-start(f32[7,8,512]{2,1,0:T(8,128)S(1)} %get-tuple-element.16), channel_id=1, source_target_pairs={{0,2},{2,0},{1,3},{3,1},{4,6},{6,4},{5,7},{7,5},{8,10},{10,8},{9,1... | collective-permute-start | bytes 344072 | tf_op jit(solution)/shard_map/ppermute | solution.py:498
  5.0 1.2 %collective-permute-start.1 = (f32[128,128]{1,0:T(8,128)S(1)}, f32[128,128]{1,0:T(8,128)S(1)}, u32[]{:S(2)}, u32[]{:S(2)}) collective-permute-start(f32[128,128]{1,0:T(8,128)S(1)} %get-tuple-element.14), channel_id=1, source_target_pairs={{0,1},{1,0},{2,3},{3,2},{4,5},{5,4},{6,7},{7,6},{8,9},{9,8},{10,11... | collective-permute-start | bytes 196616 | tf_op jit(solution)/shard_map/ppermute | solution.py:505
  6.2 0.1 collective-permute-start.3
  6.4 1.4 %prepare.1.z.refs_3_ = f32[6,5,128,128]{3,2,1,0:T(8,128)S(1)} custom-call(f32[4,128,512]{2,1,0:T(8,128)S(1)} %copy-done, f32[3,128,512]{2,1,0:T(8,128)S(1)} %get-tuple-element.13.fixed, bf16[512,512]{1,0:T(8,128)(2,1)S(1)} %get-tuple-element.15.matrix.refs_4_), custom_call_target="tpu_custom_call" | custom-call | flops 39321600 | bytes 6291456 | tf_op jit(solution)/shard_map/prepare/pallas_call | solution.py:223
  7.8 1.8 %collective-permute-done.3.refs_1_ = f32[8,128]{1,0:T(8,128)S(1)} collective-permute-done((f32[8,128]{1,0:T(8,128)S(1)}, f32[8,128]{1,0:T(8,128)S(1)}, u32[]{:S(2)}, u32[]{:S(2)}) %collective-permute-start.3) | collective-permute-done | bytes 4128 | tf_op jit(solution)/shard_map/ppermute | solution.py:499
  9.6 0.0 collective-permute-done.1.side.refs_2_
  9.6 0.0 collective-permute-done.2.refs_0_
  9.6 0.1 bundle.1
  9.7 1.3 %collective-permute-start.4 = (f32[88,128]{1,0:T(8,128)S(1)}, f32[88,128]{1,0:T(8,128)S(1)}, u32[]{:S(2)}, u32[]{:S(2)}) collective-permute-start(f32[88,128]{1,0:T(8,128)S(1)} %bundle.1), channel_id=1, source_target_pairs={{0,4},{4,8},{8,12},{12,0},{1,5},{5,9},{9,13},{13,1},{2,6},{6,10},{... | collective-permute-start | bytes 135176 | tf_op jit(solution)/shard_map/ppermute | solution.py:508
  11.0 6.2 %own.1 = (f32[3,17,5,8,128]{4,3,2,1,0:T(8,128)S(1)}, f32[3,17,4,8,128]{4,3,2,1,0:T(8,128)S(1)}, f32[2,17,4,8,128]{4,3,2,1,0:T(8,128)S(1)}, f32[4,128,512]{2,1,0:T(8,128)}) custom-call(f32[7,8,512]{2,1,0:T(8,128)S(1)} %collective-permute-done.2.refs_0_, f32[8,128]{1,0:T(8,128)S(1)} %collective-permute-done.3.refs_1_, ...), custom_call_target="tpu_custom_call" | custom-call | flops 131072000 | bytes 31457280 | tf_op jit(solution)/shard_map/own/pallas_call | solution.py:365
  17.3 0.0 collective-permute-done.4.halos
  17.3 0.0 collective-permute-done.pair
  17.3 6.7 %received.1 = (f32[4,128,512]{2,1,0:T(8,128)}, f32[4,128,512]{2,1,0:T(8,128)}) custom-call(f32[2,128,512]{2,1,0:T(8,128)S(1)} %collective-permute-done.pair, f32[88,128]{1,0:T(8,128)S(1)} %collective-permute-done.4.halos, f32[4,128,512]{2,1,0:T(8,128)S(1)} %copy-done, ...), custom_call_target="tpu_custom_call", output_to_operand_aliasing={{0}: (7, {})} | custom-call | flops 104857600 | bytes 25165824 | tf_op jit(solution)/shard_map/received/pallas_call | solution.py:467
Async XLA Ops:
  0.6 2.8 %copy-start = (f32[4,128,512]{2,1,0:T(8,128)S(1)}, f32[4,128,512]{2,1,0:T(8,128)}, u32[]{:S(2)}) copy-start(f32[4,128,512]{2,1,0:T(8,128)} %c.7) | copy-start | bytes 3145732
  2.0 15.2 %collective-permute-start = (f32[2,128,512]{2,1,0:T(8,128)S(1)}, f32[2,128,512]{2,1,0:T(8,128)S(1)}, u32[]{:S(2)}, u32[]{:S(2)}) collective-permute-start(f32[2,128,512]{2,1,0:T(8,128)S(1)} %get-tuple-element.12), channel_id=1, source_target_pairs={{0,4},{4,8},{8,12},{12,0},{1,5},{5,9},{9,13},{13,1},{2,6},{6,10},{... | collective-permute-start | bytes 1572872 | tf_op jit(solution)/shard_map/ppermute | solution.py:506
  3.7 5.8 %collective-permute-start.2 = (f32[7,8,512]{2,1,0:T(8,128)S(1)}, f32[7,8,512]{2,1,0:T(8,128)S(1)}, u32[]{:S(2)}, u32[]{:S(2)}) collective-permute-start(f32[7,8,512]{2,1,0:T(8,128)S(1)} %get-tuple-element.16), channel_id=1, source_target_pairs={{0,2},{2,0},{1,3},{3,1},{4,6},{6,4},{5,7},{7,5},{8,10},{10,8},{9,1... | collective-permute-start | bytes 344072 | tf_op jit(solution)/shard_map/ppermute | solution.py:498
  5.0 4.6 %collective-permute-start.1 = (f32[128,128]{1,0:T(8,128)S(1)}, f32[128,128]{1,0:T(8,128)S(1)}, u32[]{:S(2)}, u32[]{:S(2)}) collective-permute-start(f32[128,128]{1,0:T(8,128)S(1)} %get-tuple-element.14), channel_id=1, source_target_pairs={{0,1},{1,0},{2,3},{3,2},{4,5},{5,4},{6,7},{7,6},{8,9},{9,8},{10,11... | collective-permute-start | bytes 196616 | tf_op jit(solution)/shard_map/ppermute | solution.py:505
  6.2 3.3 %collective-permute-start.3 = (f32[8,128]{1,0:T(8,128)S(1)}, f32[8,128]{1,0:T(8,128)S(1)}, u32[]{:S(2)}, u32[]{:S(2)}) collective-permute-start(f32[8,128]{1,0:T(8,128)S(1)} %get-tuple-element.17), channel_id=1, source_target_pairs={{0,3},{3,0},{1,2},{2,1},{4,7},{7,4},{5,6},{6,5},{8,11},{11,8},{9,1... | collective-permute-start | bytes 12296 | tf_op jit(solution)/shard_map/ppermute | solution.py:499
  9.7 7.6 %collective-permute-start.4 = (f32[88,128]{1,0:T(8,128)S(1)}, f32[88,128]{1,0:T(8,128)S(1)}, u32[]{:S(2)}, u32[]{:S(2)}) collective-permute-start(f32[88,128]{1,0:T(8,128)S(1)} %bundle.1), channel_id=1, source_target_pairs={{0,4},{4,8},{8,12},{12,0},{1,5},{5,9},{9,13},{13,1},{2,6},{6,10},{... | collective-permute-start | bytes 135176 | tf_op jit(solution)/shard_map/ppermute | solution.py:508

commit v5 on v0

v5 whole, which is shorter than its diff:
```python
import functools

import jax
import jax.numpy as jnp
from jax import lax
from jax.experimental import pallas as pl
from jax.experimental.pallas import tpu as pltpu
from jax.sharding import PartitionSpec as P

FACTOR = 4
HALO = 2 * FACTOR
LANES = 128
SUBLANES = 8
SLOT = 2 * HALO
FOLDS = LANES // (2 * SLOT)
FIELDS = 7
USED = (4, 5, 6, 0, 1, 2)

courant = 0.08

VMEM = pl.BlockSpec(memory_space=pltpu.VMEM)
HBM = pl.BlockSpec(memory_space=pltpu.HBM)
F32 = jnp.float32
BF16 = jnp.bfloat16


def lane_index(shape):
    return lax.broadcasted_iota(jnp.int32, shape, len(shape) - 1)


def order(cols):
    blocks = cols // LANES
    place = lax.broadcasted_iota(jnp.int32, (cols, cols), 0)
    to = (place % blocks) * LANES + place // blocks
    return jnp.where(lane_index((cols, cols)) == to, 1.0, 0.0).astype(BF16)


def permuted(x, matrix):
    high = x.astype(BF16)
    rest = x - high.astype(F32)
    middle = rest.astype(BF16)
    low = (rest - middle.astype(F32)).astype(BF16)
    product = functools.partial(jnp.dot, preferred_element_type=F32)
    return product(high, matrix) + (product(middle, matrix) + product(low, matrix))


def restored(x, matrix):
    high = x.astype(BF16)
    low = (x - high.astype(F32)).astype(BF16)
    dims = (((1,), (1,)), ((), ()))
    product = functools.partial(lax.dot_general, dimension_numbers=dims, preferred_element_type=F32)
    return product(high, matrix) + product(low, matrix)


def start(copies):
    for copy in copies:
        copy.start()


def wait(copies):
    for copy in copies:
        copy.wait()


def place():
    return lax.axis_index("gx"), lax.axis_index("gy")


def edge_column(cols, gy):
    return pl.multiple_of((1 - gy) * (cols - LANES), LANES)


def first_row(ends, e, rows, gx):
    if len(ends) == 1:
        return pl.multiple_of((1 - gx) * (rows - HALO), HALO)
    return ends[e] * (rows - HALO)


def edges(blocks):
    lane = lane_index(blocks[0].shape)
    packed = jnp.zeros(lane.shape, F32)
    for slot, block in enumerate(blocks):
        begin = slot * SLOT
        packed = jnp.where((lane >= begin) & (lane < begin + SLOT), pltpu.roll(block, begin + HALO, 1), packed)
    return packed


def both_sides(own, other, gy):
    return jnp.where(lane_index(own.shape) // HALO % 2 == gy, own, other)


def aligned(value, slots, gy):
    return pltpu.roll(value, (gy - 1 - HALO - slots * SLOT) % LANES, 1)


def fixed_edges(value, gy):
    lane = (lane_index(value.shape) + HALO + 1 - gy) % LANES
    picked = []
    for i in range(4, FIELDS):
        twice = jnp.where(lane < SLOT, aligned(value, i, gy), aligned(value, i - 1, gy))
        picked.append(jnp.where(lane < 2 * SLOT, twice, 0.0))
    return [picked[0], picked[1] * courant, picked[2] * courant]


def state_edges(value, gy):
    return [aligned(value, 2 * i, gy) * courant for i in range(2)]


def pack_kernel(ends, fields, *refs):
    n = len(ends)
    xs, ds, (ys, matrix) = refs[:n], refs[n : 2 * n], refs[2 * n :]
    rows, cols = fields.shape[1:]
    gx, gy = place()
    for e, x in enumerate(xs):
        x[...] = fields[:, pl.ds(first_row(ends, e, rows, gx), HALO), :]
    ys[...] = edges([fields[f, :, pl.ds(edge_column(cols, gy), LANES)] for f in range(FIELDS)])
    for e, d in enumerate(ds):
        d[...] = ys[pl.ds(first_row(ends, e, rows, gx), HALO), :]
    matrix[...] = order(cols)


def pack(ends, fields):
    rows, cols = fields.shape[1:]
    n = len(ends)
    return pl.pallas_call(
        functools.partial(pack_kernel, ends),
        out_shape=(
            *[jax.ShapeDtypeStruct((FIELDS, HALO, cols), F32)] * n,
            *[jax.ShapeDtypeStruct((HALO, LANES), F32)] * n,
            jax.ShapeDtypeStruct((rows, LANES), F32),
            jax.ShapeDtypeStruct((cols, cols), BF16),
        ),
        in_specs=[VMEM],
        out_specs=(VMEM,) * (2 * n + 2),
        compiler_params=pltpu.CompilerParams(vmem_limit_bytes=16 << 20),
        name="pack",
    )(fields)


def take_kernel(c, dif, dx, dy, pair, fields, sems):
    copies = [
        pltpu.make_async_copy(c.at[pl.ds(2, 2)], fields.at[pl.ds(2, 2)], sems.at[0]),
        pltpu.make_async_copy(c.at[pl.ds(0, 2)], fields.at[pl.ds(0, 2)], sems.at[1]),
    ]
    copies += [pltpu.make_async_copy(ref, fields.at[4 + i], sems.at[2 + i]) for i, ref in enumerate((dif, dx, dy))]
    start(copies)
    wait(copies[:1])
    pair[...] = fields[pl.ds(2, 2)]
    wait(copies[1:])


def take(c, dif, dx, dy):
    return pl.pallas_call(
        take_kernel,
        out_shape=[jax.ShapeDtypeStruct((count, *dif.shape), F32) for count in (2, FIELDS)],
        in_specs=[HBM] * 4,
        out_specs=[VMEM] * 2,
        scratch_shapes=[pltpu.SemaphoreType.DMA((5,))],
        compiler_params=pltpu.CompilerParams(vmem_limit_bytes=4 << 20),
        name="take",
    )(*[pltpu.with_memory_space_constraint(x, pltpu.HBM) for x in (c, dif, dx, dy)])


def bundle_kernel(n, folded, corners, rows, out):
    at = folded.shape[0]
    out[pl.ds(0, at)] = folded[...]
    for e in range(n):
        out[pl.ds(at, HALO)] = corners[e]
        at += HALO
        for k in range(rows.shape[2] // LANES):
            out[pl.ds(at, 2 * HALO)] = rows[e, :, pl.ds(k * LANES, LANES)]
            at += 2 * HALO


def bundle(folded, corners, rows):
    n = len(corners)
    height = folded.shape[0] + n * HALO * (1 + 2 * (rows.shape[2] // LANES))
    return pl.pallas_call(
        functools.partial(bundle_kernel, n),
        out_shape=jax.ShapeDtypeStruct((height, LANES), F32),
        in_specs=[VMEM] * 3,
        out_specs=VMEM,
        compiler_params=pltpu.CompilerParams(vmem_limit_bytes=4 << 20),
        name="bundle",
    )(folded, corners, rows)


def put_columns(z, begin, value):
    rows, cols = value.shape
    for k in range(cols // LANES):
        z[k, pl.ds(begin, rows)] = value[:, k * LANES : (k + 1) * LANES]


def fills(n, rows, gx):
    if n == 1:
        return [(rows, None, 0)]
    return [(rows, gx < lax.axis_size("gx") - 1, 1), (rows + HALO, gx > 0, 0)]


def masked(there, value):
    return value if there is None else jnp.where(there, value, 0.0)


def layout(n, rows, cols):
    height = rows + n * HALO
    count = height // SUBLANES
    assert (SUBLANES - 1) * count <= rows and rows % (SUBLANES * FOLDS) == 0
    return height, (count, cols // LANES, SUBLANES, LANES), (count, SUBLANES, LANES)


def to_strided(z, w):
    count = w.shape[0]
    for r in range(count):
        for k in range(w.shape[1]):
            w[r, k] = z[k, pl.ds(r, SUBLANES, stride=count), :]


def prepare_kernel(fields, matrix, ys, side, bodies, edge, folded, z, t):
    _, gy = place()
    rows = fields.shape[1]
    count = edge.shape[1]
    scales = [1.0 if f == 4 else courant for f in USED]
    for i in range(0, len(USED), 2):
        pair = [fields[USED[i + m]] * scales[i + m] for m in range(2)]
        y = permuted(jnp.concatenate(pair, axis=0), matrix[...])
        for m in range(2):
            put_columns(z.at[i + m], 0, y[m * rows : (m + 1) * rows])
            to_strided(z.at[i + m], bodies.at[i + m])
    t[pl.ds(0, rows)] = both_sides(ys[...], side[...], gy)
    for r in range(count):
        value = t[pl.ds(r, SUBLANES, stride=count), :]
        for i, picked in enumerate(fixed_edges(value, gy) + state_edges(value, gy)):
            edge[i, r] = picked
    height = rows // FOLDS
    lane = lane_index((height, LANES))
    value = jnp.zeros((height, LANES), F32)
    for j in range(FOLDS):
        begin = 2 * SLOT * j
        moved = pltpu.roll(t[pl.ds(j * height, height), :], (begin - 2 * SLOT) % LANES, 1)
        value = jnp.where((lane >= begin) & (lane < begin + 2 * SLOT), moved, value)
    folded[...] = value


def prepare(n, fields, matrix, ys, side):
    rows, cols = fields.shape[1:]
    height, body, edge = layout(n, rows, cols)
    return pl.pallas_call(
        prepare_kernel,
        out_shape=(
            jax.ShapeDtypeStruct((len(USED), *body), F32),
            jax.ShapeDtypeStruct((5, *edge), F32),
            jax.ShapeDtypeStruct((rows // FOLDS, LANES), F32),
        ),
        in_specs=[VMEM] * 4,
        out_specs=(VMEM,) * 3,
        scratch_shapes=[
            pltpu.VMEM((len(USED), cols // LANES, height, LANES), F32),
            pltpu.VMEM((height, LANES), F32),
        ],
        compiler_params=pltpu.CompilerParams(vmem_limit_bytes=24 << 20),
        cost_estimate=pl.CostEstimate(flops=100 * FIELDS * rows * cols, bytes_accessed=6 << 20, transcendentals=0),
        name="prepare",
    )(fields, matrix, ys, side)


def from_strided(z, w):
    count = w.shape[0]
    for r in range(count):
        for k in range(z.shape[0]):
            z[k, pl.ds(r, SUBLANES, stride=count), :] = w[r, k] * (1.0 / courant)


def finish(ws, targets, matrix, zs, outs, sems):
    rows = outs.shape[1]
    flat = []
    for i, w in enumerate(ws):
        from_strided(zs.at[i], w)
        flat.append(jnp.concatenate([zs[i, k, pl.ds(0, rows)] for k in range(zs.shape[1])], axis=1))
    values = restored(jnp.concatenate(flat, axis=0), matrix[...])
    copies = []
    for i, target in enumerate(targets):
        outs[i] = values[i * rows : (i + 1) * rows]
        copies.append(pltpu.make_async_copy(outs.at[i], target, sems.at[i]))
        copies[i].start()
    return copies


def update(field, before, after, left, right, diffusion, drift_x, drift_y):
    speed_x = drift_x + field
    speed_y = drift_y + field
    laplace = (after - before) + (right - left)
    upwind_x = jnp.where(speed_x > 0.0, before, after)
    upwind_y = jnp.where(speed_y > 0.0, left, right)
    return field + diffusion * laplace - speed_x * upwind_x - speed_y * upwind_y


def step(rows, gx, gy, ws, edge, fixed, fixed_edge):
    n, count, blocks = ws.shape[:3]
    shape = (SUBLANES, LANES)
    lane, sublane = lane_index(shape), lax.broadcasted_iota(jnp.int32, shape, 0)
    at_left, at_right = lane == 0, lane == LANES - 1
    on_right = gy == 1
    cut = lax.axis_size("gx") == 2
    last_sublane, last_row = divmod(rows - 1, count)
    assert last_row < count - 1
    none_above = sublane == jnp.where(gx == 0, 0, -1)
    none_below = sublane == jnp.where(gx == 1, last_sublane, -1)

    def row(r):
        return [ws[m, r, k] for m in range(n) for k in range(blocks)] + [edge[r]]

    initial = field = row(0)
    above = [pltpu.roll(value, 1, 0) for value in row(count - 1)]
    if cut:
        above = [jnp.where(none_above, 0.0, value) for value in above]
    before = [value - other for value, other in zip(field, above)]
    for r in range(count):
        following = row(r + 1) if r < count - 1 else [pltpu.roll(value, SUBLANES - 1, 0) for value in initial]
        below = following
        if cut and r == last_row:
            below = [jnp.where(none_below, 0.0, value) for value in following]
        after = [other - value for value, other in zip(field, below)]
        border = field[-1] - pltpu.roll(field[-1], 1, 1)
        around = (before[-1], after[-1], border, pltpu.roll(border, LANES - 1, 1))
        edge[r] = update(field[-1], *around, *[fixed_edge[i, r] for i in range(3)])
        for m in range(n):
            part = slice(m * blocks, (m + 1) * blocks)
            body, body_before, body_after = field[part], before[part], after[part]
            across = pltpu.roll(border, LANES - m * SLOT, 1) if m else border
            begin = jnp.where(on_right, across, body[0])
            end = jnp.where(on_right, -body[-1], across)
            left = [jnp.where(at_left, begin, body[0] - pltpu.roll(body[-1], 1, 1))]
            left += [body[k] - body[k - 1] for k in range(1, blocks)]
            right = left[1:]
            right.append(jnp.where(at_right, end, pltpu.roll(body[0], LANES - 1, 1) - body[-1]))
            for k in range(blocks):
                around = (body_before[k], body_after[k], left[k], right[k])
                ws[m, r, k] = update(body[k], *around, *[fixed[i, r, k] for i in range(3)])
        field, before = following, after


def propagate(rows, gx, gy, ws, edge, fixed, fixed_edge):
    def one(count, carry):
        step(rows, gx, gy, ws, edge, fixed, fixed_edge)
        return carry

    lax.fori_loop(0, FACTOR, one, 0)


def once_kernel(n, *refs):
    xr, dr, (bodies, edge, matrix), refs = refs[:n], refs[n : 2 * n], refs[2 * n : 2 * n + 3], refs[2 * n + 3 :]
    corners, sent, fixed, fixed_edge, once, e_pair, e_last = refs
    cols = matrix.shape[0]
    count, blocks = once.shape[1:3]
    rows = count * SUBLANES - n * HALO
    gx, gy = place()
    fixed[...] = bodies[pl.ds(0, 3)]
    once[...] = bodies[pl.ds(3, 3)]
    fixed_edge[...] = edge[pl.ds(0, 3)]
    e_pair[...] = edge[3]
    e_last[...] = edge[4]
    for x, d, corner in zip(xr, dr, [corners.at[e] for e in range(n)]):
        own = edges([x[f, :, pl.ds(edge_column(cols, gy), LANES)] for f in range(FIELDS)])
        corner[...] = both_sides(own, d[...], gy)
    targets = [*[fixed.at[i] for i in range(3)], *[once.at[m] for m in range(3)]]
    edge_targets = [*[fixed_edge.at[i] for i in range(3)], e_pair, e_last]
    in_place = slice(SUBLANES - 1, SUBLANES)
    converted = []
    for e, x in enumerate(xr):
        value = jnp.concatenate([x[f] * (1.0 if f == 4 else courant) for f in (*USED, 3)], axis=0)
        converted.append(permuted(value, matrix[...]))
        sent[e] = converted[e][(len(USED) - 1) * HALO :]
    for begin, there, which in fills(n, rows, gx):
        y = masked(there, converted[which])
        values = fixed_edges(corners[which], gy) + state_edges(corners[which], gy)
        for j in range(HALO):
            r = begin + j - (SUBLANES - 1) * count
            for i, target in enumerate(targets):
                for k in range(blocks):
                    at = i * HALO + j
                    target[r, k, in_place] = y[at : at + 1, k * LANES : (k + 1) * LANES]
            for target, value in zip(edge_targets, values):
                target[r, in_place] = masked(there, value[j : j + 1])

    propagate(rows, gx, gy, once.at[pl.ds(0, 2)], e_pair, fixed, fixed_edge)
    propagate(rows, gx, gy, once.at[pl.ds(2, 1)], e_last, fixed, fixed_edge)


def propagate_once(xr, dr, bodies, edge, matrix):
    n = len(xr)
    body, edge_shape = bodies.shape[1:], edge.shape[1:]
    return pl.pallas_call(
        functools.partial(once_kernel, n),
        out_shape=(
            jax.ShapeDtypeStruct((n, HALO, LANES), F32),
            jax.ShapeDtypeStruct((n, 2 * HALO, matrix.shape[0]), F32),
            jax.ShapeDtypeStruct((3, *body), F32),
            jax.ShapeDtypeStruct((3, *edge_shape), F32),
            jax.ShapeDtypeStruct((3, *body), F32),
            jax.ShapeDtypeStruct(edge_shape, F32),
        ),
        in_specs=[VMEM] * (2 * n + 3),
        out_specs=(VMEM,) * 6,
        scratch_shapes=[pltpu.VMEM(edge_shape, F32)],
        compiler_params=pltpu.CompilerParams(vmem_limit_bytes=16 << 20),
        cost_estimate=pl.CostEstimate(flops=0, bytes_accessed=12 << 20, transcendentals=0),
        name="once",
    )(*xr, *dr, bodies, edge, matrix)


def twice_kernel(n, fixed, fixed_edge, once, edge, matrix, relaxed, difference, ws, e_pair, zs, outs, sems):
    rows = outs.shape[1]
    gx, gy = place()
    written = finish([once.at[m] for m in range(3)], [relaxed.at[m + 1] for m in range(3)], matrix, zs, outs, sems)
    ws[...] = once[pl.ds(0, 2)]
    e_pair[...] = edge[...]
    propagate(rows, gx, gy, ws, e_pair, fixed, fixed_edge)
    difference[...] = ws[...] - once[pl.ds(1, 2)]
    wait(written)


def propagate_twice(n, fixed, fixed_edge, once, edge, matrix):
    body, edge_shape, cols = once.shape[1:], edge.shape, matrix.shape[0]
    height = body[0] * SUBLANES
    rows = height - n * HALO
    return pl.pallas_call(
        functools.partial(twice_kernel, n),
        out_shape=(jax.ShapeDtypeStruct((4, rows, cols), F32), jax.ShapeDtypeStruct((2, *body), F32)),
        in_specs=[VMEM] * 5,
        out_specs=(HBM, VMEM),
        scratch_shapes=[
            pltpu.VMEM((2, *body), F32),
            pltpu.VMEM(edge_shape, F32),
            pltpu.VMEM((3, body[1], height, LANES), F32),
            pltpu.VMEM((3, rows, cols), F32),
            pltpu.SemaphoreType.DMA((3,)),
        ],
        compiler_params=pltpu.CompilerParams(vmem_limit_bytes=16 << 20),
        cost_estimate=pl.CostEstimate(flops=0, bytes_accessed=10 << 20, transcendentals=0),
        name="twice",
    )(fixed, fixed_edge, once, edge, matrix)


def convert_kernel(pair, difference, matrix, bodies, residual, z, zs, outs, sems):
    rows = pair.shape[1]
    sources = [difference.at[m] for m in range(2)]
    written = finish(sources, [residual.at[m + 2] for m in range(2)], matrix, zs, outs, sems)
    y = permuted(jnp.concatenate([pair[m] for m in range(2)], axis=0) * courant, matrix[...])
    for m in range(2):
        put_columns(z.at[m], 0, y[m * rows : (m + 1) * rows])
        to_strided(z.at[m], bodies.at[m])
    wait(written)


def convert(pair, difference, matrix):
    rows, cols = pair.shape[1:]
    body = difference.shape[1:]
    height = body[0] * SUBLANES
    return pl.pallas_call(
        convert_kernel,
        out_shape=(jax.ShapeDtypeStruct((2, *body), F32), jax.ShapeDtypeStruct((4, rows, cols), F32)),
        in_specs=[VMEM] * 3,
        out_specs=(VMEM, HBM),
        scratch_shapes=[
            pltpu.VMEM((2, body[1], height, LANES), F32),
            pltpu.VMEM((2, body[1], height, LANES), F32),
            pltpu.VMEM((2, rows, cols), F32),
            pltpu.SemaphoreType.DMA((2,)),
        ],
        compiler_params=pltpu.CompilerParams(vmem_limit_bytes=16 << 20),
        cost_estimate=pl.CostEstimate(flops=0, bytes_accessed=4 << 20, transcendentals=0),
        name="convert",
    )(pair, difference, matrix)


def received_kernel(n, bodies, halos, fields, fixed, fixed_edge, once, matrix, relaxed_in, residual_in, *refs):
    relaxed, residual, t, ws, edge, late, zs, outs, sems = refs
    del relaxed_in, residual_in
    rows = fields.shape[1]
    count, blocks = ws.shape[1:3]
    first = lax.axis_index("ta") == 0
    gx, gy = place()
    targets = [relaxed.at[0], residual.at[0], residual.at[1]]

    @pl.when(first)
    def _():
        outs[0] = fields[0]
        outs[1] = jnp.zeros_like(outs[1])
        values = [outs.at[0], outs.at[1], outs.at[1]]
        copies = [pltpu.make_async_copy(*ends, sems.at[i]) for i, ends in enumerate(zip(values, targets))]
        start(copies)
        wait(copies)

    @pl.when(jnp.logical_not(first))
    def _():
        fold = rows // FOLDS
        folded = halos[pl.ds(0, fold)]
        for j in range(FOLDS):
            t[pl.ds(j * fold, fold)] = aligned(folded, 2 * j, gy) * courant
        ws[...] = bodies[...]
        in_place = slice(SUBLANES - 1, SUBLANES)
        for begin, there, which in fills(n, rows, gx):
            at = fold + which * HALO * (1 + 2 * blocks)
            t[pl.ds(begin, HALO)] = masked(there, aligned(halos[pl.ds(at, HALO)], 2, gy) * courant)
            at += HALO
            for k in range(blocks):
                value = masked(there, halos[pl.ds(at + k * 2 * HALO, 2 * HALO)])
                for m in range(2):
                    for j in range(HALO):
                        row = m * HALO + j
                        ws[m, begin + j - (SUBLANES - 1) * count, k, in_place] = value[row : row + 1]
        for r in range(count):
            edge[r] = t[pl.ds(r, SUBLANES, stride=count), :]
        propagate(rows, gx, gy, ws, edge, fixed, fixed_edge)
        late[0] = ws[1]
        propagate(rows, gx, gy, ws, edge, fixed, fixed_edge)
        late[1] = ws[0] - late[0]
        late[2] = ws[1] - once[0]
        wait(finish([late.at[m] for m in range(3)], targets, matrix, zs, outs, sems))


def received(n, bodies, halos, fields, fixed, fixed_edge, once, matrix, relaxed, residual):
    rows, cols = fields.shape[1:]
    height, body, edge = layout(n, rows, cols)
    shape = jax.ShapeDtypeStruct((4, rows, cols), F32)
    return pl.pallas_call(
        functools.partial(received_kernel, n),
        out_shape=(shape, shape),
        in_specs=[VMEM] * 7 + [HBM] * 2,
        out_specs=(HBM, HBM),
        scratch_shapes=[
            pltpu.VMEM((height, LANES), F32),
            pltpu.VMEM((2, *body), F32),
            pltpu.VMEM(edge, F32),
            pltpu.VMEM((3, *body), F32),
            pltpu.VMEM((3, body[1], height, LANES), F32),
            pltpu.VMEM((3, rows, cols), F32),
            pltpu.SemaphoreType.DMA((3,)),
        ],
        input_output_aliases={7: 0, 8: 1},
        compiler_params=pltpu.CompilerParams(vmem_limit_bytes=24 << 20),
        cost_estimate=pl.CostEstimate(flops=1600 * rows * cols, bytes_accessed=24 << 20, transcendentals=0),
        name="received",
    )(bodies, halos, fields, fixed, fixed_edge, once, matrix, relaxed, residual)


def local(c, dif, dx, dy):
    groups, nx, ny = (lax.axis_size(name) for name in ("ta", "gx", "gy"))
    rows, cols = dif.shape
    assert ny == 2 and c.shape[0] == 4 and rows % SUBLANES == 0 and cols % LANES == 0
    ends = (1,) if nx == 2 else (1, 0)
    n = len(ends)
    ring = [(i, (i + 1) % groups) for i in range(groups)]
    pair, fields = take(c, dif, dx, dy)
    pair = lax.ppermute(pair, "ta", ring)
    *sent, ys, matrix = pack(ends, fields)
    xs, ds = sent[:n], sent[n:]
    if nx == 2:
        xr = [lax.ppermute(xs[0], "gx", [(0, 1), (1, 0)])]
        dr = [lax.ppermute(ds[0], ("gx", "gy"), [(0, 3), (3, 0), (1, 2), (2, 1)])]
    else:
        hops = [[(i, i + hop) for i in range(nx) if 0 <= i + hop < nx] for hop in (1, -1)]
        xr = [lax.ppermute(x, "gx", pairs) for x, pairs in zip(xs, hops)]
        crossed = [[(i * 2 + s, j * 2 + 1 - s) for i, j in pairs for s in range(2)] for pairs in hops]
        dr = [lax.ppermute(d, ("gx", "gy"), pairs) for d, pairs in zip(ds, crossed)]
    side = lax.ppermute(ys, "gy", [(0, 1), (1, 0)])
    bodies, edge, folded = prepare(n, fields, matrix, ys, side)
    corners, sent, fixed, fixed_edge, once, edge = propagate_once(xr, dr, bodies, edge, matrix)
    halos = lax.ppermute(bundle(folded, corners, sent), "ta", ring)
    relaxed, difference = propagate_twice(n, fixed, fixed_edge, once, edge, matrix)
    bodies, residual = convert(pair, difference, matrix)
    return received(n, bodies, halos, fields, fixed, fixed_edge, once, matrix, relaxed, residual)


def solution(mesh):
    return jax.shard_map(
        local,
        mesh=mesh,
        in_specs=(
            P(("grp", "ta"), "gx", "gy"),
            P(("grp", "gx"), "gy"),
            P(("grp", "gx"), "gy"),
            P(("grp", "gx"), "gy"),
        ),
        out_specs=(P(("grp", "ta"), "gx", "gy"), P(("grp", "ta"), "gx", "gy")),
        check_vma=False,
    )
```

time: 146 us -> 22.6 us (0.15); the launches traced: 144 us -> 22.5 us
  starting transfers between devices: 71.1 us -> 5.35 us
  waiting for transfers between devices: 46 us -> 1.68 us
  other arithmetic: 24.7 us -> 0 us
  Pallas kernels: 0 us -> 14.8 us
    ppermute x34 -> x5, starting transfers between devices: 71.1 us -> 5.35 us  [the longest x1 1.35 us: local(): halos = lax.ppermute(bundle(folded, corners, sent), 'ta', ring)]
    ppermute x34 -> x5, waiting for transfers between devices: 46 us -> 1.68 us  [the longest x1 0.91 us: local(): dr = [lax.ppermute(ds[0], ('gx', 'gy'), [(0, 3), (3, 0), (1, 2), (2, 1)])]]
    sub x9 -> x0, other arithmetic: 21.3 us -> none  [the longest x8 21.2 us: local_step(): return field + coeffs[0] * laplace - courant * advect]
    pallas_call x0 -> x8, Pallas kernels: none -> 14.8 us  [the longest x1 4.81 us: received(): pl.pallas_call(functools.partial(received_kernel, n), out_shape=(shape, s...]
    slice x8 -> x0, other arithmetic: 2.28 us -> none  [with_halo(): last = lax.slice_in_dim(x, length - width, length, axis=dim)]
  transfers between devices with their start and end apart: 34 -> 5, of which waited for: 18 -> 2; matrix products, arithmetic and copies ran while one was open for 0% -> 0% of each run, Pallas kernels for 0% -> 38%
where the time goes in v5:
time: 22.6 us; the launch traced here: 22.5 us
  Pallas kernels  14.8 us (65%)
  starting transfers between devices  5.35 us (24%)
  waiting for transfers between devices  1.68 us (7%)
  between operations  0.71 us (3%)
    pallas_call x1, Pallas kernels, received(): pl.pallas_call(functools.partial(received_kernel, n), out_shape=(shape, s...  4.81 us
    pallas_call x1, Pallas kernels, propagate_once(): pl.pallas_call(functools.partial(once_kernel, n), out_shape=(jax.ShapeDty...  3.07 us
    pallas_call x1, Pallas kernels, propagate_twice(): pl.pallas_call(functools.partial(twice_kernel, n), out_shape=(jax.ShapeDt...  2.31 us
    pallas_call x1, Pallas kernels, prepare(): pl.pallas_call(prepare_kernel, out_shape=(jax.ShapeDtypeStruct((len(USED)...  1.51 us
    pallas_call x1, Pallas kernels, take(): pl.pallas_call(take_kernel, out_shape=[jax.ShapeDtypeStruct((count, *dif....  1.47 us
    ppermute x1, starting transfers between devices, local(): halos = lax.ppermute(bundle(folded, corners, sent), 'ta', ring)  1.35 us
    ppermute x1, starting transfers between devices, local(): pair = lax.ppermute(pair, 'ta', ring)  1.35 us
    ppermute x1, starting transfers between devices, local(): xr = [lax.ppermute(xs[0], 'gx', [(0, 1), (1, 0)])]  1.28 us
  transfers between devices with their start and end apart: 5, of which 2 were waited for; matrix products, arithmetic and copies ran while one was open for 0% of the time, Pallas kernels for 38%

profile of v5, /device:TPU:9, one launch (start us, length us, event | category | flops | bytes accessed | tf_op | source)
XLA Modules:
  0.0 22.5 jit_solution(6897179312648603432)
XLA Ops:
  0.6 1.5 %take.1 = (f32[2,128,512]{2,1,0:T(8,128)S(1)}, f32[7,128,512]{2,1,0:T(8,128)S(1)}) custom-call(f32[4,128,512]{2,1,0:T(8,128)} %c.1, f32[128,512]{1,0:T(8,128)} %dif.1, f32[128,512]{1,0:T(8,128)} %dx.1, f32[128,512]{1,0:T(8,128)} %dy.1), custom_call_target="tpu_custom_call" | custom-call | tf_op jit(solution)/shard_map/take/pallas_call | solution.py:153
  2.1 1.3 %collective-permute-start = (f32[2,128,512]{2,1,0:T(8,128)S(1)}, f32[2,128,512]{2,1,0:T(8,128)S(1)}, u32[]{:S(2)}, u32[]{:S(2)}) collective-permute-start(f32[2,128,512]{2,1,0:T(8,128)S(1)} %get-tuple-element.21), channel_id=1, source_target_pairs={{0,4},{4,8},{8,12},{12,0},{1,5},{5,9},{9,13},{13,1},{2,6},{6,10},{... | collective-permute-start | bytes 1572872 | tf_op jit(solution)/shard_map/ppermute | solution.py:555
  3.5 0.3 %pack.1 = (f32[7,8,512]{2,1,0:T(8,128)S(1)}, f32[8,128]{1,0:T(8,128)S(1)}, f32[128,128]{1,0:T(8,128)S(1)}, bf16[512,512]{1,0:T(8,128)(2,1)S(1)}) custom-call(f32[7,128,512]{2,1,0:T(8,128)S(1)} %get-tuple-element.22.fields), custom_call_target="tpu_custom_call" | custom-call | tf_op jit(solution)/shard_map/pack/pallas_call | solution.py:125
  3.8 1.3 %collective-permute-start.1 = (f32[7,8,512]{2,1,0:T(8,128)S(1)}, f32[7,8,512]{2,1,0:T(8,128)S(1)}, u32[]{:S(2)}, u32[]{:S(2)}) collective-permute-start(f32[7,8,512]{2,1,0:T(8,128)S(1)} %get-tuple-element.23), channel_id=1, source_target_pairs={{0,2},{2,0},{1,3},{3,1},{4,6},{6,4},{5,7},{7,5},{8,10},{10,8},{9,1... | collective-permute-start | bytes 344072 | tf_op jit(solution)/shard_map/ppermute | solution.py:559
  5.1 1.2 %collective-permute-start.3 = (f32[128,128]{1,0:T(8,128)S(1)}, f32[128,128]{1,0:T(8,128)S(1)}, u32[]{:S(2)}, u32[]{:S(2)}) collective-permute-start(f32[128,128]{1,0:T(8,128)S(1)} %get-tuple-element.26.ys), channel_id=1, source_target_pairs={{0,1},{1,0},{2,3},{3,2},{4,5},{5,4},{6,7},{7,6},{8,9},{9,8},{10,11... | collective-permute-start | bytes 196616 | tf_op jit(solution)/shard_map/ppermute | solution.py:566
  6.3 0.1 collective-permute-start.2
  6.4 0.8 %collective-permute-done.3.side = f32[128,128]{1,0:T(8,128)S(1)} collective-permute-done((f32[128,128]{1,0:T(8,128)S(1)}, f32[128,128]{1,0:T(8,128)S(1)}, u32[]{:S(2)}, u32[]{:S(2)}) %collective-permute-start.3) | collective-permute-done | bytes 65568 | tf_op jit(solution)/shard_map/ppermute | solution.py:566
  7.2 1.5 %prepare.1 = (f32[6,17,4,8,128]{4,3,2,1,0:T(8,128)S(1)}, f32[5,17,8,128]{3,2,1,0:T(8,128)S(1)}, f32[32,128]{1,0:T(8,128)S(1)}) custom-call(f32[7,128,512]{2,1,0:T(8,128)S(1)} %get-tuple-element.22.fields, bf16[512,512]{1,0:T(8,128)(2,1)S(1)} %get-tuple-element.25.matrix.refs_4_, f32[128,128]{1,0:T(8,128)S(1)} %get-tuple-element.26.ys, ...), custom_call_target="tpu_custom_call" | custom-call | flops 45875200 | bytes 6291456 | tf_op jit(solution)/shard_map/prepare/pallas_call | solution.py:247
  8.7 0.9 %collective-permute-done.2.refs_1_ = f32[8,128]{1,0:T(8,128)S(1)} collective-permute-done((f32[8,128]{1,0:T(8,128)S(1)}, f32[8,128]{1,0:T(8,128)S(1)}, u32[]{:S(2)}, u32[]{:S(2)}) %collective-permute-start.2) | collective-permute-done | bytes 4128 | tf_op jit(solution)/shard_map/ppermute | solution.py:560
  9.6 0.0 collective-permute-done.1.refs_0_
  9.6 3.1 %once.1 = (f32[1,8,128]{2,1,0:T(8,128)S(1)}, f32[1,16,512]{2,1,0:T(8,128)S(1)}, f32[3,17,4,8,128]{4,3,2,1,0:T(8,128)S(1)}, f32[3,17,8,128]{3,2,1,0:T(8,128)S(1)}...) custom-call(f32[7,8,512]{2,1,0:T(8,128)S(1)} %collective-permute-done.1.refs_0_, ...), custom_call_target="tpu_custom_call" | custom-call | bytes 12582912 | tf_op jit(solution)/shard_map/once/pallas_call | solution.py:392
  12.7 1.3 %collective-permute-start.4 = (f32[104,128]{1,0:T(8,128)S(1)}, f32[104,128]{1,0:T(8,128)S(1)}, u32[]{:S(2)}, u32[]{:S(2)}) collective-permute-start(f32[104,128]{1,0:T(8,128)S(1)} %bundle.1), channel_id=1, source_target_pairs={{0,4},{4,8},{8,12},{12,0},{1,5},{5,9},{9,13},{13,1},{2,6},{6,10},{... | collective-permute-start | bytes 159752 | tf_op jit(solution)/shard_map/ppermute | solution.py:569
  14.1 2.3 %twice.1 = (f32[4,128,512]{2,1,0:T(8,128)}, f32[2,17,4,8,128]{4,3,2,1,0:T(8,128)S(1)}) custom-call(f32[3,17,4,8,128]{4,3,2,1,0:T(8,128)S(1)} %get-tuple-element.29.fixed, f32[3,17,8,128]{3,2,1,0:T(8,128)S(1)} %get-tuple-element.30.fixed_edge, f32[3,17,4,8,128]{4,3,2,1,0:T(8,128)S(1)} %get-tuple-element.31.once, f32[17,8,128]{2,1,0:T(8,128)S(1)} %get-tuple-element.32.edge, ...), custom_call_target="tpu_custom_call" | custom-call | bytes 10485760 | tf_op jit(solution)/shard_map/twice/pallas_call | solution.py:426
  16.4 0.0 collective-permute-done.pair
  16.4 1.3 %convert.1 = (f32[2,17,4,8,128]{4,3,2,1,0:T(8,128)S(1)}, f32[4,128,512]{2,1,0:T(8,128)}) custom-call(f32[2,128,512]{2,1,0:T(8,128)S(1)} %collective-permute-done.pair, f32[2,17,4,8,128]{4,3,2,1,0:T(8,128)S(1)} %get-tuple-element.33.difference, bf16[512,512]{1,0:T(8,128)(2,1)S(1)} %get-tuple-element.25.matrix.refs_4_), custom_call_target="tpu_custom_call" | custom-call | bytes 4194304 | tf_op jit(solution)/shard_map/convert/pallas_call | solution.py:459
  17.7 0.0 collective-permute-done.4.halos
  17.7 4.8 %received.1 = (f32[4,128,512]{2,1,0:T(8,128)}, f32[4,128,512]{2,1,0:T(8,128)}) custom-call(f32[2,17,4,8,128]{4,3,2,1,0:T(8,128)S(1)} %get-tuple-element.34.bodies, f32[104,128]{1,0:T(8,128)S(1)} %collective-permute-done.4.halos, f32[7,128,512]{2,1,0:T(8,128)S(1)} %get-tuple-element.22.fields, ...), custom_call_target="tpu_custom_call", output_to_operand_aliasing={{0}: (7, {}), {1}: (8, {})} | custom-call | flops 104857600 | bytes 25165824 | tf_op jit(solution)/shard_map/received/pallas_call | solution.py:526
  (1 shorter events, 0.0 us)
Async XLA Ops:
  2.1 14.3 %collective-permute-start = (f32[2,128,512]{2,1,0:T(8,128)S(1)}, f32[2,128,512]{2,1,0:T(8,128)S(1)}, u32[]{:S(2)}, u32[]{:S(2)}) collective-permute-start(f32[2,128,512]{2,1,0:T(8,128)S(1)} %get-tuple-element.21), channel_id=1, source_target_pairs={{0,4},{4,8},{8,12},{12,0},{1,5},{5,9},{9,13},{13,1},{2,6},{6,10},{... | collective-permute-start | bytes 1572872 | tf_op jit(solution)/shard_map/ppermute | solution.py:555
  3.8 5.8 %collective-permute-start.1 = (f32[7,8,512]{2,1,0:T(8,128)S(1)}, f32[7,8,512]{2,1,0:T(8,128)S(1)}, u32[]{:S(2)}, u32[]{:S(2)}) collective-permute-start(f32[7,8,512]{2,1,0:T(8,128)S(1)} %get-tuple-element.23), channel_id=1, source_target_pairs={{0,2},{2,0},{1,3},{3,1},{4,6},{6,4},{5,7},{7,5},{8,10},{10,8},{9,1... | collective-permute-start | bytes 344072 | tf_op jit(solution)/shard_map/ppermute | solution.py:559
  5.1 2.1 %collective-permute-start.3 = (f32[128,128]{1,0:T(8,128)S(1)}, f32[128,128]{1,0:T(8,128)S(1)}, u32[]{:S(2)}, u32[]{:S(2)}) collective-permute-start(f32[128,128]{1,0:T(8,128)S(1)} %get-tuple-element.26.ys), channel_id=1, source_target_pairs={{0,1},{1,0},{2,3},{3,2},{4,5},{5,4},{6,7},{7,6},{8,9},{9,8},{10,11... | collective-permute-start | bytes 196616 | tf_op jit(solution)/shard_map/ppermute | solution.py:566
  6.3 3.3 %collective-permute-start.2 = (f32[8,128]{1,0:T(8,128)S(1)}, f32[8,128]{1,0:T(8,128)S(1)}, u32[]{:S(2)}, u32[]{:S(2)}) collective-permute-start(f32[8,128]{1,0:T(8,128)S(1)} %get-tuple-element.24), channel_id=1, source_target_pairs={{0,3},{3,0},{1,2},{2,1},{4,7},{7,4},{5,6},{6,5},{8,11},{11,8},{9,1... | collective-permute-start | bytes 12296 | tf_op jit(solution)/shard_map/ppermute | solution.py:560
  12.7 4.9 %collective-permute-start.4 = (f32[104,128]{1,0:T(8,128)S(1)}, f32[104,128]{1,0:T(8,128)S(1)}, u32[]{:S(2)}, u32[]{:S(2)}) collective-permute-start(f32[104,128]{1,0:T(8,128)S(1)} %bundle.1), channel_id=1, source_target_pairs={{0,4},{4,8},{8,12},{12,0},{1,5},{5,9},{9,13},{13,1},{2,6},{6,10},{... | collective-permute-start | bytes 159752 | tf_op jit(solution)/shard_map/ppermute | solution.py:569

commit v6 on v5

--- a/solution.py
+++ b/solution.py
@@ -90,11 +90,11 @@
 
 
 def aligned(value, slots, gy):
-    return pltpu.roll(value, (gy - 1 - HALO - slots * SLOT) % LANES, 1)
+    return pltpu.roll(value, (2 * gy - 1 - HALO - slots * SLOT) % LANES, 1)
 
 
 def fixed_edges(value, gy):
-    lane = (lane_index(value.shape) + HALO + 1 - gy) % LANES
+    lane = (lane_index(value.shape) + HALO + 1 - 2 * gy) % LANES
     picked = []
     for i in range(4, FIELDS):
         twice = jnp.where(lane < SLOT, aligned(value, i, gy), aligned(value, i - 1, gy))
@@ -270,18 +270,20 @@
             z[k, pl.ds(r, SUBLANES, stride=count), :] = w[r, k] * (1.0 / courant)
 
 
-def finish(ws, targets, matrix, zs, outs, sems):
+def restore(ws, matrix, zs, outs):
     rows = outs.shape[1]
     flat = []
     for i, w in enumerate(ws):
         from_strided(zs.at[i], w)
         flat.append(jnp.concatenate([zs[i, k, pl.ds(0, rows)] for k in range(zs.shape[1])], axis=1))
     values = restored(jnp.concatenate(flat, axis=0), matrix[...])
-    copies = []
-    for i, target in enumerate(targets):
+    for i in range(len(ws)):
         outs[i] = values[i * rows : (i + 1) * rows]
-        copies.append(pltpu.make_async_copy(outs.at[i], target, sems.at[i]))
-        copies[i].start()
+
+
+def write(outs, targets, sems):
+    copies = [pltpu.make_async_copy(outs.at[i], target, sems.at[i]) for i, target in enumerate(targets)]
+    start(copies)
     return copies
 
 
@@ -299,7 +301,7 @@
     shape = (SUBLANES, LANES)
     lane, sublane = lane_index(shape), lax.broadcasted_iota(jnp.int32, shape, 0)
     at_left, at_right = lane == 0, lane == LANES - 1
-    on_right = gy == 1
+    nearest = lane == jnp.where(gy == 1, 0, LANES - 1)
     cut = lax.axis_size("gx") == 2
     last_sublane, last_row = divmod(rows - 1, count)
     assert last_row < count - 1
@@ -326,25 +328,26 @@
         for m in range(n):
             part = slice(m * blocks, (m + 1) * blocks)
             body, body_before, body_after = field[part], before[part], after[part]
-            across = pltpu.roll(border, LANES - m * SLOT, 1) if m else border
-            begin = jnp.where(on_right, across, body[0])
-            end = jnp.where(on_right, -body[-1], across)
-            left = [jnp.where(at_left, begin, body[0] - pltpu.roll(body[-1], 1, 1))]
+            across = jnp.where(nearest, pltpu.roll(field[-1], LANES - m * SLOT, 1) if m else field[-1], 0.0)
+            left = [body[0] - jnp.where(at_left, across, pltpu.roll(body[-1], 1, 1))]
             left += [body[k] - body[k - 1] for k in range(1, blocks)]
             right = left[1:]
-            right.append(jnp.where(at_right, end, pltpu.roll(body[0], LANES - 1, 1) - body[-1]))
+            right.append(jnp.where(at_right, across, pltpu.roll(body[0], LANES - 1, 1)) - body[-1])
             for k in range(blocks):
                 around = (body_before[k], body_after[k], left[k], right[k])
                 ws[m, r, k] = update(body[k], *around, *[fixed[i, r, k] for i in range(3)])
         field, before = following, after
 
 
-def propagate(rows, gx, gy, ws, edge, fixed, fixed_edge):
+def propagate(rows, gx, gy, ws, edge, fixed, fixed_edge, beside=None):
     def one(count, carry):
         step(rows, gx, gy, ws, edge, fixed, fixed_edge)
         return carry
 
-    lax.fori_loop(0, FACTOR, one, 0)
+    if beside is not None:
+        beside()
+        one(0, 0)
+    lax.fori_loop(0, FACTOR - (beside is not None), one, 0)
 
 
 def once_kernel(n, *refs):
@@ -411,7 +414,8 @@
 def twice_kernel(n, fixed, fixed_edge, once, edge, matrix, relaxed, difference, ws, e_pair, zs, outs, sems):
     rows = outs.shape[1]
     gx, gy = place()
-    written = finish([once.at[m] for m in range(3)], [relaxed.at[m + 1] for m in range(3)], matrix, zs, outs, sems)
+    restore([once.at[m] for m in range(3)], matrix, zs, outs)
+    written = write(outs, [relaxed.at[m + 1] for m in range(3)], sems)
     ws[...] = once[pl.ds(0, 2)]
     e_pair[...] = edge[...]
     propagate(rows, gx, gy, ws, e_pair, fixed, fixed_edge)
@@ -441,55 +445,39 @@
     )(fixed, fixed_edge, once, edge, matrix)
 
 
-def convert_kernel(pair, difference, matrix, bodies, residual, z, zs, outs, sems):
+def convert_kernel(pair, matrix, bodies, z):
     rows = pair.shape[1]
-    sources = [difference.at[m] for m in range(2)]
-    written = finish(sources, [residual.at[m + 2] for m in range(2)], matrix, zs, outs, sems)
     y = permuted(jnp.concatenate([pair[m] for m in range(2)], axis=0) * courant, matrix[...])
     for m in range(2):
         put_columns(z.at[m], 0, y[m * rows : (m + 1) * rows])
         to_strided(z.at[m], bodies.at[m])
-    wait(written)
-
-
-def convert(pair, difference, matrix):
-    rows, cols = pair.shape[1:]
-    body = difference.shape[1:]
+
+
+def convert(pair, matrix, body):
     height = body[0] * SUBLANES
     return pl.pallas_call(
         convert_kernel,
-        out_shape=(jax.ShapeDtypeStruct((2, *body), F32), jax.ShapeDtypeStruct((4, rows, cols), F32)),
-        in_specs=[VMEM] * 3,
-        out_specs=(VMEM, HBM),
-        scratch_shapes=[
-            pltpu.VMEM((2, body[1], height, LANES), F32),
-            pltpu.VMEM((2, body[1], height, LANES), F32),
-            pltpu.VMEM((2, rows, cols), F32),
-            pltpu.SemaphoreType.DMA((2,)),
-        ],
+        out_shape=jax.ShapeDtypeStruct((2, *body), F32),
+        in_specs=[VMEM] * 2,
+        out_specs=VMEM,
+        scratch_shapes=[pltpu.VMEM((2, body[1], height, LANES), F32)],
         compiler_params=pltpu.CompilerParams(vmem_limit_bytes=16 << 20),
-        cost_estimate=pl.CostEstimate(flops=0, bytes_accessed=4 << 20, transcendentals=0),
+        cost_estimate=pl.CostEstimate(flops=0, bytes_accessed=3 << 20, transcendentals=0),
         name="convert",
-    )(pair, difference, matrix)
-
-
-def received_kernel(n, bodies, halos, fields, fixed, fixed_edge, once, matrix, relaxed_in, residual_in, *refs):
+    )(pair, matrix)
+
+
+def received_kernel(n, bodies, halos, fields, fixed, fixed_edge, once, difference, matrix, relaxed_in, *refs):
     relaxed, residual, t, ws, edge, late, zs, outs, sems = refs
-    del relaxed_in, residual_in
+    del relaxed_in
     rows = fields.shape[1]
     count, blocks = ws.shape[1:3]
     first = lax.axis_index("ta") == 0
     gx, gy = place()
-    targets = [relaxed.at[0], residual.at[0], residual.at[1]]
-
-    @pl.when(first)
-    def _():
-        outs[0] = fields[0]
-        outs[1] = jnp.zeros_like(outs[1])
-        values = [outs.at[0], outs.at[1], outs.at[1]]
-        copies = [pltpu.make_async_copy(*ends, sems.at[i]) for i, ends in enumerate(zip(values, targets))]
-        start(copies)
-        wait(copies)
+    targets = [residual.at[2], residual.at[3], relaxed.at[0], residual.at[0], residual.at[1]]
+
+    def restore_own():
+        restore([difference.at[m] for m in range(2)], matrix, zs, outs)
 
     @pl.when(jnp.logical_not(first))
     def _():
@@ -511,37 +499,52 @@
                         ws[m, begin + j - (SUBLANES - 1) * count, k, in_place] = value[row : row + 1]
         for r in range(count):
             edge[r] = t[pl.ds(r, SUBLANES, stride=count), :]
-        propagate(rows, gx, gy, ws, edge, fixed, fixed_edge)
+        propagate(rows, gx, gy, ws, edge, fixed, fixed_edge, restore_own)
+        written = write(outs, targets[:2], sems)
         late[0] = ws[1]
-        propagate(rows, gx, gy, ws, edge, fixed, fixed_edge)
+
+        def restore_first():
+            restore([late.at[0]], matrix, zs, outs.at[pl.ds(2, 1)])
+
+        propagate(rows, gx, gy, ws, edge, fixed, fixed_edge, restore_first)
+        written += write(outs.at[pl.ds(2, 1)], targets[2:3], sems.at[pl.ds(2, 1)])
         late[1] = ws[0] - late[0]
         late[2] = ws[1] - once[0]
-        wait(finish([late.at[m] for m in range(3)], targets, matrix, zs, outs, sems))
-
-
-def received(n, bodies, halos, fields, fixed, fixed_edge, once, matrix, relaxed, residual):
+        restore([late.at[1], late.at[2]], matrix, zs, outs.at[pl.ds(3, 2)])
+        wait(written + write(outs.at[pl.ds(3, 2)], targets[3:], sems.at[pl.ds(3, 2)]))
+
+    @pl.when(first)
+    def _():
+        restore_own()
+        outs[2] = fields[0]
+        for m in (3, 4):
+            outs[m] = jnp.zeros(outs.shape[1:], F32)
+        wait(write(outs, targets, sems))
+
+
+def received(n, bodies, halos, fields, fixed, fixed_edge, once, difference, matrix, relaxed):
     rows, cols = fields.shape[1:]
     height, body, edge = layout(n, rows, cols)
     shape = jax.ShapeDtypeStruct((4, rows, cols), F32)
     return pl.pallas_call(
         functools.partial(received_kernel, n),
         out_shape=(shape, shape),
-        in_specs=[VMEM] * 7 + [HBM] * 2,
+        in_specs=[VMEM] * 8 + [HBM],
         out_specs=(HBM, HBM),
         scratch_shapes=[
             pltpu.VMEM((height, LANES), F32),
             pltpu.VMEM((2, *body), F32),
             pltpu.VMEM(edge, F32),
             pltpu.VMEM((3, *body), F32),
-            pltpu.VMEM((3, body[1], height, LANES), F32),
-            pltpu.VMEM((3, rows, cols), F32),
-            pltpu.SemaphoreType.DMA((3,)),
+            pltpu.VMEM((2, body[1], height, LANES), F32),
+            pltpu.VMEM((5, rows, cols), F32),
+            pltpu.SemaphoreType.DMA((5,)),
         ],
-        input_output_aliases={7: 0, 8: 1},
+        input_output_aliases={8: 0},
         compiler_params=pltpu.CompilerParams(vmem_limit_bytes=24 << 20),
         cost_estimate=pl.CostEstimate(flops=1600 * rows * cols, bytes_accessed=24 << 20, transcendentals=0),
         name="received",
-    )(bodies, halos, fields, fixed, fixed_edge, once, matrix, relaxed, residual)
+    )(bodies, halos, fields, fixed, fixed_edge, once, difference, matrix, relaxed)
 
 
 def local(c, dif, dx, dy):
@@ -568,8 +571,8 @@
     corners, sent, fixed, fixed_edge, once, edge = propagate_once(xr, dr, bodies, edge, matrix)
     halos = lax.ppermute(bundle(folded, corners, sent), "ta", ring)
     relaxed, difference = propagate_twice(n, fixed, fixed_edge, once, edge, matrix)
-    bodies, residual = convert(pair, difference, matrix)
-    return received(n, bodies, halos, fields, fixed, fixed_edge, once, matrix, relaxed, residual)
+    bodies = convert(pair, matrix, once.shape[1:])
+    return received(n, bodies, halos, fields, fixed, fixed_edge, once, difference, matrix, relaxed)
 
 
 def solution(mesh):

time: 22.6 us -> 22.1 us (0.978)
  Pallas kernels: 14.8 us -> 14.1 us
    pallas_call x1, Pallas kernels: 1.26 us -> 0.61 us  [convert(): pl.pallas_call(convert_kernel, out_shape=jax.ShapeDtypeStruct((2, *body),...]
  transfers between devices with their start and end apart: 5 -> 5, of which waited for: 2 -> 2; matrix products, arithmetic and copies ran while one was open for 0% -> 0% of each run, Pallas kernels for 38% -> 35%
where the time goes in v6:
time: 22.1 us; the launch traced here: 21.9 us
  Pallas kernels  14.1 us (64%)
  starting transfers between devices  5.35 us (24%)
  waiting for transfers between devices  1.68 us (8%)
  between operations  0.7 us (3%)
    pallas_call x1, Pallas kernels, received(): pl.pallas_call(functools.partial(received_kernel, n), out_shape=(shape, s...  4.96 us
    pallas_call x1, Pallas kernels, propagate_once(): pl.pallas_call(functools.partial(once_kernel, n), out_shape=(jax.ShapeDty...  3.01 us
    pallas_call x1, Pallas kernels, propagate_twice(): pl.pallas_call(functools.partial(twice_kernel, n), out_shape=(jax.ShapeDt...  2.26 us
    pallas_call x1, Pallas kernels, prepare(): pl.pallas_call(prepare_kernel, out_shape=(jax.ShapeDtypeStruct((len(USED)...  1.5 us
    pallas_call x1, Pallas kernels, take(): pl.pallas_call(take_kernel, out_shape=[jax.ShapeDtypeStruct((count, *dif....  1.47 us
    ppermute x1, starting transfers between devices, local(): halos = lax.ppermute(bundle(folded, corners, sent), 'ta', ring)  1.35 us
    ppermute x1, starting transfers between devices, local(): pair = lax.ppermute(pair, 'ta', ring)  1.35 us
    ppermute x1, starting transfers between devices, local(): xr = [lax.ppermute(xs[0], 'gx', [(0, 1), (1, 0)])]  1.28 us
  transfers between devices with their start and end apart: 5, of which 2 were waited for; matrix products, arithmetic and copies ran while one was open for 0% of the time, Pallas kernels for 35%

profile of v6, /device:TPU:9, one launch (start us, length us, event | category | flops | bytes accessed | tf_op | source)
XLA Modules:
  0.0 21.9 jit_solution(14187351251176262588)
XLA Ops:
  0.6 1.5 %take.1 = (f32[2,128,512]{2,1,0:T(8,128)S(1)}, f32[7,128,512]{2,1,0:T(8,128)S(1)}) custom-call(f32[4,128,512]{2,1,0:T(8,128)} %c.1, f32[128,512]{1,0:T(8,128)} %dif.1, f32[128,512]{1,0:T(8,128)} %dx.1, f32[128,512]{1,0:T(8,128)} %dy.1), custom_call_target="tpu_custom_call" | custom-call | tf_op jit(solution)/shard_map/take/pallas_call | solution.py:153
  2.1 1.3 %collective-permute-start = (f32[2,128,512]{2,1,0:T(8,128)S(1)}, f32[2,128,512]{2,1,0:T(8,128)S(1)}, u32[]{:S(2)}, u32[]{:S(2)}) collective-permute-start(f32[2,128,512]{2,1,0:T(8,128)S(1)} %get-tuple-element.19), channel_id=1, source_target_pairs={{0,4},{4,8},{8,12},{12,0},{1,5},{5,9},{9,13},{13,1},{2,6},{6,10},{... | collective-permute-start | bytes 1572872 | tf_op jit(solution)/shard_map/ppermute | solution.py:558
  3.5 0.3 %pack.1 = (f32[7,8,512]{2,1,0:T(8,128)S(1)}, f32[8,128]{1,0:T(8,128)S(1)}, f32[128,128]{1,0:T(8,128)S(1)}, bf16[512,512]{1,0:T(8,128)(2,1)S(1)}) custom-call(f32[7,128,512]{2,1,0:T(8,128)S(1)} %get-tuple-element.20.fields), custom_call_target="tpu_custom_call" | custom-call | tf_op jit(solution)/shard_map/pack/pallas_call | solution.py:125
  3.8 1.3 %collective-permute-start.2 = (f32[7,8,512]{2,1,0:T(8,128)S(1)}, f32[7,8,512]{2,1,0:T(8,128)S(1)}, u32[]{:S(2)}, u32[]{:S(2)}) collective-permute-start(f32[7,8,512]{2,1,0:T(8,128)S(1)} %get-tuple-element.24), channel_id=1, source_target_pairs={{0,2},{2,0},{1,3},{3,1},{4,6},{6,4},{5,7},{7,5},{8,10},{10,8},{9,1... | collective-permute-start | bytes 344072 | tf_op jit(solution)/shard_map/ppermute | solution.py:562
  5.1 1.2 %collective-permute-start.1 = (f32[128,128]{1,0:T(8,128)S(1)}, f32[128,128]{1,0:T(8,128)S(1)}, u32[]{:S(2)}, u32[]{:S(2)}) collective-permute-start(f32[128,128]{1,0:T(8,128)S(1)} %get-tuple-element.22.ys), channel_id=1, source_target_pairs={{0,1},{1,0},{2,3},{3,2},{4,5},{5,4},{6,7},{7,6},{8,9},{9,8},{10,11... | collective-permute-start | bytes 196616 | tf_op jit(solution)/shard_map/ppermute | solution.py:569
  6.3 0.1 collective-permute-start.3
  6.4 0.8 %collective-permute-done.1.side = f32[128,128]{1,0:T(8,128)S(1)} collective-permute-done((f32[128,128]{1,0:T(8,128)S(1)}, f32[128,128]{1,0:T(8,128)S(1)}, u32[]{:S(2)}, u32[]{:S(2)}) %collective-permute-start.1) | collective-permute-done | bytes 65568 | tf_op jit(solution)/shard_map/ppermute | solution.py:569
  7.2 1.5 %prepare.1 = (f32[6,17,4,8,128]{4,3,2,1,0:T(8,128)S(1)}, f32[5,17,8,128]{3,2,1,0:T(8,128)S(1)}, f32[32,128]{1,0:T(8,128)S(1)}) custom-call(f32[7,128,512]{2,1,0:T(8,128)S(1)} %get-tuple-element.20.fields, bf16[512,512]{1,0:T(8,128)(2,1)S(1)} %get-tuple-element.21.matrix.refs_4_, f32[128,128]{1,0:T(8,128)S(1)} %get-tuple-element.22.ys, ...), custom_call_target="tpu_custom_call" | custom-call | flops 45875200 | bytes 6291456 | tf_op jit(solution)/shard_map/prepare/pallas_call | solution.py:247
  8.7 0.9 %collective-permute-done.3.refs_1_ = f32[8,128]{1,0:T(8,128)S(1)} collective-permute-done((f32[8,128]{1,0:T(8,128)S(1)}, f32[8,128]{1,0:T(8,128)S(1)}, u32[]{:S(2)}, u32[]{:S(2)}) %collective-permute-start.3) | collective-permute-done | bytes 4128 | tf_op jit(solution)/shard_map/ppermute | solution.py:563
  9.6 0.0 collective-permute-done.2.refs_0_
  9.6 3.0 %once.1 = (f32[1,8,128]{2,1,0:T(8,128)S(1)}, f32[1,16,512]{2,1,0:T(8,128)S(1)}, f32[3,17,4,8,128]{4,3,2,1,0:T(8,128)S(1)}, f32[3,17,8,128]{3,2,1,0:T(8,128)S(1)}...) custom-call(f32[7,8,512]{2,1,0:T(8,128)S(1)} %collective-permute-done.2.refs_0_, ...), custom_call_target="tpu_custom_call" | custom-call | bytes 12582912 | tf_op jit(solution)/shard_map/once/pallas_call | solution.py:395
  12.7 1.4 %collective-permute-start.4 = (f32[104,128]{1,0:T(8,128)S(1)}, f32[104,128]{1,0:T(8,128)S(1)}, u32[]{:S(2)}, u32[]{:S(2)}) collective-permute-start(f32[104,128]{1,0:T(8,128)S(1)} %bundle.1), channel_id=1, source_target_pairs={{0,4},{4,8},{8,12},{12,0},{1,5},{5,9},{9,13},{13,1},{2,6},{6,10},{... | collective-permute-start | bytes 159752 | tf_op jit(solution)/shard_map/ppermute | solution.py:572
  14.0 2.3 %twice.1 = (f32[4,128,512]{2,1,0:T(8,128)}, f32[2,17,4,8,128]{4,3,2,1,0:T(8,128)S(1)}) custom-call(f32[3,17,4,8,128]{4,3,2,1,0:T(8,128)S(1)} %get-tuple-element.30.fixed, f32[3,17,8,128]{3,2,1,0:T(8,128)S(1)} %get-tuple-element.31.fixed_edge, f32[3,17,4,8,128]{4,3,2,1,0:T(8,128)S(1)} %get-tuple-element.32.once, f32[17,8,128]{2,1,0:T(8,128)S(1)} %get-tuple-element.33.edge, ...), custom_call_target="tpu_custom_call" | custom-call | bytes 10485760 | tf_op jit(solution)/shard_map/twice/pallas_call | solution.py:430
  16.3 0.0 collective-permute-done.pair
  16.3 0.6 %convert.1.bodies = f32[2,17,4,8,128]{4,3,2,1,0:T(8,128)S(1)} custom-call(f32[2,128,512]{2,1,0:T(8,128)S(1)} %collective-permute-done.pair, bf16[512,512]{1,0:T(8,128)(2,1)S(1)} %get-tuple-element.21.matrix.refs_4_), custom_call_target="tpu_custom_call" | custom-call | bytes 3145728 | tf_op jit(solution)/shard_map/convert/pallas_call | solution.py:458
  16.9 0.0 collective-permute-done.4.halos
  16.9 5.0 %received.1 = (f32[4,128,512]{2,1,0:T(8,128)}, f32[4,128,512]{2,1,0:T(8,128)}) custom-call(f32[2,17,4,8,128]{4,3,2,1,0:T(8,128)S(1)} %convert.1.bodies, f32[104,128]{1,0:T(8,128)S(1)} %collective-permute-done.4.halos, f32[7,128,512]{2,1,0:T(8,128)S(1)} %get-tuple-element.20.fields, ...), custom_call_target="tpu_custom_call", output_to_operand_aliasing={{0}: (8, {})} | custom-call | flops 104857600 | bytes 25165824 | tf_op jit(solution)/shard_map/received/pallas_call | solution.py:529
  (1 shorter events, 0.0 us)
Async XLA Ops:
  2.1 14.2 %collective-permute-start = (f32[2,128,512]{2,1,0:T(8,128)S(1)}, f32[2,128,512]{2,1,0:T(8,128)S(1)}, u32[]{:S(2)}, u32[]{:S(2)}) collective-permute-start(f32[2,128,512]{2,1,0:T(8,128)S(1)} %get-tuple-element.19), channel_id=1, source_target_pairs={{0,4},{4,8},{8,12},{12,0},{1,5},{5,9},{9,13},{13,1},{2,6},{6,10},{... | collective-permute-start | bytes 1572872 | tf_op jit(solution)/shard_map/ppermute | solution.py:558
  3.8 5.8 %collective-permute-start.2 = (f32[7,8,512]{2,1,0:T(8,128)S(1)}, f32[7,8,512]{2,1,0:T(8,128)S(1)}, u32[]{:S(2)}, u32[]{:S(2)}) collective-permute-start(f32[7,8,512]{2,1,0:T(8,128)S(1)} %get-tuple-element.24), channel_id=1, source_target_pairs={{0,2},{2,0},{1,3},{3,1},{4,6},{6,4},{5,7},{7,5},{8,10},{10,8},{9,1... | collective-permute-start | bytes 344072 | tf_op jit(solution)/shard_map/ppermute | solution.py:562
  5.1 2.1 %collective-permute-start.1 = (f32[128,128]{1,0:T(8,128)S(1)}, f32[128,128]{1,0:T(8,128)S(1)}, u32[]{:S(2)}, u32[]{:S(2)}) collective-permute-start(f32[128,128]{1,0:T(8,128)S(1)} %get-tuple-element.22.ys), channel_id=1, source_target_pairs={{0,1},{1,0},{2,3},{3,2},{4,5},{5,4},{6,7},{7,6},{8,9},{9,8},{10,11... | collective-permute-start | bytes 196616 | tf_op jit(solution)/shard_map/ppermute | solution.py:569
  6.3 3.3 %collective-permute-start.3 = (f32[8,128]{1,0:T(8,128)S(1)}, f32[8,128]{1,0:T(8,128)S(1)}, u32[]{:S(2)}, u32[]{:S(2)}) collective-permute-start(f32[8,128]{1,0:T(8,128)S(1)} %get-tuple-element.25), channel_id=1, source_target_pairs={{0,3},{3,0},{1,2},{2,1},{4,7},{7,4},{5,6},{6,5},{8,11},{11,8},{9,1... | collective-permute-start | bytes 12296 | tf_op jit(solution)/shard_map/ppermute | solution.py:563
  12.7 4.2 %collective-permute-start.4 = (f32[104,128]{1,0:T(8,128)S(1)}, f32[104,128]{1,0:T(8,128)S(1)}, u32[]{:S(2)}, u32[]{:S(2)}) collective-permute-start(f32[104,128]{1,0:T(8,128)S(1)} %bundle.1), channel_id=1, source_target_pairs={{0,4},{4,8},{8,12},{12,0},{1,5},{5,9},{9,13},{13,1},{2,6},{6,10},{... | collective-permute-start | bytes 159752 | tf_op jit(solution)/shard_map/ppermute | solution.py:572

commit v7 on v6

--- a/solution.py
+++ b/solution.py
@@ -12,7 +12,7 @@
 LANES = 128
 SUBLANES = 8
 SLOT = 2 * HALO
-FOLDS = LANES // (2 * SLOT)
+FOLDS = LANES // (2 * HALO)
 FIELDS = 7
 USED = (4, 5, 6, 0, 1, 2)
 
@@ -93,8 +93,12 @@
     return pltpu.roll(value, (2 * gy - 1 - HALO - slots * SLOT) % LANES, 1)
 
 
+def turned_lane(shape, gy):
+    return (lane_index(shape) + HALO + 1 - 2 * gy) % LANES
+
+
 def fixed_edges(value, gy):
-    lane = (lane_index(value.shape) + HALO + 1 - 2 * gy) % LANES
+    lane = turned_lane(value.shape, gy)
     picked = []
     for i in range(4, FIELDS):
         twice = jnp.where(lane < SLOT, aligned(value, i, gy), aligned(value, i - 1, gy))
@@ -235,9 +239,10 @@
     lane = lane_index((height, LANES))
     value = jnp.zeros((height, LANES), F32)
     for j in range(FOLDS):
-        begin = 2 * SLOT * j
-        moved = pltpu.roll(t[pl.ds(j * height, height), :], (begin - 2 * SLOT) % LANES, 1)
-        value = jnp.where((lane >= begin) & (lane < begin + 2 * SLOT), moved, value)
+        for m in range(2):
+            begin = 2 * HALO * j + HALO * m
+            moved = pltpu.roll(side[pl.ds(j * height, height), :], (begin - (2 + m) * SLOT - HALO * (1 - gy)) % LANES, 1)
+            value = jnp.where((lane >= begin) & (lane < begin + HALO), moved, value)
     folded[...] = value
 
 
@@ -445,21 +450,26 @@
     )(fixed, fixed_edge, once, edge, matrix)
 
 
-def convert_kernel(pair, matrix, bodies, z):
-    rows = pair.shape[1]
+def convert_kernel(pair, matrix, bodies, edge, z):
+    rows, cols = pair.shape[1:]
+    _, gy = place()
     y = permuted(jnp.concatenate([pair[m] for m in range(2)], axis=0) * courant, matrix[...])
     for m in range(2):
         put_columns(z.at[m], 0, y[m * rows : (m + 1) * rows])
         to_strided(z.at[m], bodies.at[m])
+    column = pl.ds(edge_column(cols, gy), LANES)
+    moved = [pltpu.roll(pair[m, :, column], (m * SLOT - 1 + 2 * gy) % LANES, 1) for m in range(2)]
+    edge[...] = jnp.where(turned_lane(moved[0].shape, gy) < SLOT, moved[0], moved[1]) * courant
 
 
 def convert(pair, matrix, body):
     height = body[0] * SUBLANES
+    edge = jax.ShapeDtypeStruct((pair.shape[1], LANES), F32)
     return pl.pallas_call(
         convert_kernel,
-        out_shape=jax.ShapeDtypeStruct((2, *body), F32),
+        out_shape=(jax.ShapeDtypeStruct((2, *body), F32), edge),
         in_specs=[VMEM] * 2,
-        out_specs=VMEM,
+        out_specs=(VMEM, VMEM),
         scratch_shapes=[pltpu.VMEM((2, body[1], height, LANES), F32)],
         compiler_params=pltpu.CompilerParams(vmem_limit_bytes=16 << 20),
         cost_estimate=pl.CostEstimate(flops=0, bytes_accessed=3 << 20, transcendentals=0),
@@ -467,7 +477,7 @@
     )(pair, matrix)
 
 
-def received_kernel(n, bodies, halos, fields, fixed, fixed_edge, once, difference, matrix, relaxed_in, *refs):
+def received_kernel(n, bodies, own_edge, halos, fields, fixed, fixed_edge, once, difference, matrix, relaxed_in, *refs):
     relaxed, residual, t, ws, edge, late, zs, outs, sems = refs
     del relaxed_in
     rows = fields.shape[1]
@@ -483,8 +493,13 @@
     def _():
         fold = rows // FOLDS
         folded = halos[pl.ds(0, fold)]
+        lane = turned_lane((fold, LANES), gy)
         for j in range(FOLDS):
-            t[pl.ds(j * fold, fold)] = aligned(folded, 2 * j, gy) * courant
+            shift = -2 * HALO * j - 1 - 6 * gy
+            moved = [pltpu.roll(folded, (HALO * m + shift) % LANES, 1) for m in range(2)]
+            other = jnp.where(lane < SLOT, moved[0], moved[1]) * courant
+            place_of = pl.ds(j * fold, fold)
+            t[place_of] = jnp.where(lane // HALO % 2 == gy, own_edge[place_of], other)
         ws[...] = bodies[...]
         in_place = slice(SUBLANES - 1, SUBLANES)
         for begin, there, which in fills(n, rows, gx):
@@ -522,14 +537,14 @@
         wait(write(outs, targets, sems))
 
 
-def received(n, bodies, halos, fields, fixed, fixed_edge, once, difference, matrix, relaxed):
+def received(n, bodies, own_edge, halos, fields, fixed, fixed_edge, once, difference, matrix, relaxed):
     rows, cols = fields.shape[1:]
     height, body, edge = layout(n, rows, cols)
     shape = jax.ShapeDtypeStruct((4, rows, cols), F32)
     return pl.pallas_call(
         functools.partial(received_kernel, n),
         out_shape=(shape, shape),
-        in_specs=[VMEM] * 8 + [HBM],
+        in_specs=[VMEM] * 9 + [HBM],
         out_specs=(HBM, HBM),
         scratch_shapes=[
             pltpu.VMEM((height, LANES), F32),
@@ -540,11 +555,11 @@
             pltpu.VMEM((5, rows, cols), F32),
             pltpu.SemaphoreType.DMA((5,)),
         ],
-        input_output_aliases={8: 0},
+        input_output_aliases={9: 0},
         compiler_params=pltpu.CompilerParams(vmem_limit_bytes=24 << 20),
         cost_estimate=pl.CostEstimate(flops=1600 * rows * cols, bytes_accessed=24 << 20, transcendentals=0),
         name="received",
-    )(bodies, halos, fields, fixed, fixed_edge, once, difference, matrix, relaxed)
+    )(bodies, own_edge, halos, fields, fixed, fixed_edge, once, difference, matrix, relaxed)
 
 
 def local(c, dif, dx, dy):
@@ -571,8 +586,8 @@
     corners, sent, fixed, fixed_edge, once, edge = propagate_once(xr, dr, bodies, edge, matrix)
     halos = lax.ppermute(bundle(folded, corners, sent), "ta", ring)
     relaxed, difference = propagate_twice(n, fixed, fixed_edge, once, edge, matrix)
-    bodies = convert(pair, matrix, once.shape[1:])
-    return received(n, bodies, halos, fields, fixed, fixed_edge, once, difference, matrix, relaxed)
+    bodies, own_edge = convert(pair, matrix, once.shape[1:])
+    return received(n, bodies, own_edge, halos, fields, fixed, fixed_edge, once, difference, matrix, relaxed)
 
 
 def solution(mesh):

time: 22.1 us -> 22 us (level)
  transfers between devices with their start and end apart: 5 -> 5, of which waited for: 2 -> 2; matrix products, arithmetic and copies ran while one was open for 0% -> 0% of each run, Pallas kernels for 35% -> 36%
where the time goes in v7:
time: 22 us; the launch traced here: 21.8 us
  Pallas kernels  14.1 us (64%)
  starting transfers between devices  5.35 us (24%)
  waiting for transfers between devices  1.67 us (8%)
  between operations  0.71 us (3%)
    pallas_call x1, Pallas kernels, received(): pl.pallas_call(functools.partial(received_kernel, n), out_shape=(shape, s...  4.86 us
    pallas_call x1, Pallas kernels, propagate_once(): pl.pallas_call(functools.partial(once_kernel, n), out_shape=(jax.ShapeDty...  3.02 us
    pallas_call x1, Pallas kernels, propagate_twice(): pl.pallas_call(functools.partial(twice_kernel, n), out_shape=(jax.ShapeDt...  2.26 us
    pallas_call x1, Pallas kernels, prepare(): pl.pallas_call(prepare_kernel, out_shape=(jax.ShapeDtypeStruct((len(USED)...  1.51 us
    pallas_call x1, Pallas kernels, take(): pl.pallas_call(take_kernel, out_shape=[jax.ShapeDtypeStruct((count, *dif....  1.47 us
    ppermute x1, starting transfers between devices, local(): halos = lax.ppermute(bundle(folded, corners, sent), 'ta', ring)  1.35 us
    ppermute x1, starting transfers between devices, local(): pair = lax.ppermute(pair, 'ta', ring)  1.35 us
    ppermute x1, starting transfers between devices, local(): xr = [lax.ppermute(xs[0], 'gx', [(0, 1), (1, 0)])]  1.28 us
  transfers between devices with their start and end apart: 5, of which 2 were waited for; matrix products, arithmetic and copies ran while one was open for 0% of the time, Pallas kernels for 36%

profile of v7, /device:TPU:9, one launch (start us, length us, event | category | flops | bytes accessed | tf_op | source)
XLA Modules:
  0.0 21.8 jit_solution(7669158578770519404)
XLA Ops:
  0.6 1.5 %take.1 = (f32[2,128,512]{2,1,0:T(8,128)S(1)}, f32[7,128,512]{2,1,0:T(8,128)S(1)}) custom-call(f32[4,128,512]{2,1,0:T(8,128)} %c.1, f32[128,512]{1,0:T(8,128)} %dif.1, f32[128,512]{1,0:T(8,128)} %dx.1, f32[128,512]{1,0:T(8,128)} %dy.1), custom_call_target="tpu_custom_call" | custom-call | tf_op jit(solution)/shard_map/take/pallas_call | solution.py:157
  2.1 1.3 %collective-permute-start = (f32[2,128,512]{2,1,0:T(8,128)S(1)}, f32[2,128,512]{2,1,0:T(8,128)S(1)}, u32[]{:S(2)}, u32[]{:S(2)}) collective-permute-start(f32[2,128,512]{2,1,0:T(8,128)S(1)} %get-tuple-element.21), channel_id=1, source_target_pairs={{0,4},{4,8},{8,12},{12,0},{1,5},{5,9},{9,13},{13,1},{2,6},{6,10},{... | collective-permute-start | bytes 1572872 | tf_op jit(solution)/shard_map/ppermute | solution.py:573
  3.5 0.3 %pack.1 = (f32[7,8,512]{2,1,0:T(8,128)S(1)}, f32[8,128]{1,0:T(8,128)S(1)}, f32[128,128]{1,0:T(8,128)S(1)}, bf16[512,512]{1,0:T(8,128)(2,1)S(1)}) custom-call(f32[7,128,512]{2,1,0:T(8,128)S(1)} %get-tuple-element.22.fields), custom_call_target="tpu_custom_call" | custom-call | tf_op jit(solution)/shard_map/pack/pallas_call | solution.py:129
  3.8 1.3 %collective-permute-start.2 = (f32[7,8,512]{2,1,0:T(8,128)S(1)}, f32[7,8,512]{2,1,0:T(8,128)S(1)}, u32[]{:S(2)}, u32[]{:S(2)}) collective-permute-start(f32[7,8,512]{2,1,0:T(8,128)S(1)} %get-tuple-element.28), channel_id=1, source_target_pairs={{0,2},{2,0},{1,3},{3,1},{4,6},{6,4},{5,7},{7,5},{8,10},{10,8},{9,1... | collective-permute-start | bytes 344072 | tf_op jit(solution)/shard_map/ppermute | solution.py:577
  5.1 1.2 %collective-permute-start.1 = (f32[128,128]{1,0:T(8,128)S(1)}, f32[128,128]{1,0:T(8,128)S(1)}, u32[]{:S(2)}, u32[]{:S(2)}) collective-permute-start(f32[128,128]{1,0:T(8,128)S(1)} %get-tuple-element.26.ys), channel_id=1, source_target_pairs={{0,1},{1,0},{2,3},{3,2},{4,5},{5,4},{6,7},{7,6},{8,9},{9,8},{10,11... | collective-permute-start | bytes 196616 | tf_op jit(solution)/shard_map/ppermute | solution.py:584
  6.3 0.1 collective-permute-start.3
  6.5 0.8 %collective-permute-done.1.side = f32[128,128]{1,0:T(8,128)S(1)} collective-permute-done((f32[128,128]{1,0:T(8,128)S(1)}, f32[128,128]{1,0:T(8,128)S(1)}, u32[]{:S(2)}, u32[]{:S(2)}) %collective-permute-start.1) | collective-permute-done | bytes 65568 | tf_op jit(solution)/shard_map/ppermute | solution.py:584
  7.2 1.5 %prepare.1 = (f32[6,17,4,8,128]{4,3,2,1,0:T(8,128)S(1)}, f32[5,17,8,128]{3,2,1,0:T(8,128)S(1)}, f32[16,128]{1,0:T(8,128)S(1)}) custom-call(f32[7,128,512]{2,1,0:T(8,128)S(1)} %get-tuple-element.22.fields, bf16[512,512]{1,0:T(8,128)(2,1)S(1)} %get-tuple-element.23.matrix.refs_4_, f32[128,128]{1,0:T(8,128)S(1)} %get-tuple-element.26.ys, ...), custom_call_target="tpu_custom_call" | custom-call | flops 45875200 | bytes 6291456 | tf_op jit(solution)/shard_map/prepare/pallas_call | solution.py:252
  8.7 0.9 %collective-permute-done.3.refs_1_ = f32[8,128]{1,0:T(8,128)S(1)} collective-permute-done((f32[8,128]{1,0:T(8,128)S(1)}, f32[8,128]{1,0:T(8,128)S(1)}, u32[]{:S(2)}, u32[]{:S(2)}) %collective-permute-start.3) | collective-permute-done | bytes 4128 | tf_op jit(solution)/shard_map/ppermute | solution.py:578
  9.6 0.0 collective-permute-done.2.refs_0_
  9.6 3.0 %once.1 = (f32[1,8,128]{2,1,0:T(8,128)S(1)}, f32[1,16,512]{2,1,0:T(8,128)S(1)}, f32[3,17,4,8,128]{4,3,2,1,0:T(8,128)S(1)}, f32[3,17,8,128]{3,2,1,0:T(8,128)S(1)}...) custom-call(f32[7,8,512]{2,1,0:T(8,128)S(1)} %collective-permute-done.2.refs_0_, ...), custom_call_target="tpu_custom_call" | custom-call | bytes 12582912 | tf_op jit(solution)/shard_map/once/pallas_call | solution.py:400
  12.7 1.3 %collective-permute-start.4 = (f32[88,128]{1,0:T(8,128)S(1)}, f32[88,128]{1,0:T(8,128)S(1)}, u32[]{:S(2)}, u32[]{:S(2)}) collective-permute-start(f32[88,128]{1,0:T(8,128)S(1)} %bundle.1), channel_id=1, source_target_pairs={{0,4},{4,8},{8,12},{12,0},{1,5},{5,9},{9,13},{13,1},{2,6},{6,10},{... | collective-permute-start | bytes 135176 | tf_op jit(solution)/shard_map/ppermute | solution.py:587
  14.0 2.3 %twice.1 = (f32[4,128,512]{2,1,0:T(8,128)}, f32[2,17,4,8,128]{4,3,2,1,0:T(8,128)S(1)}) custom-call(f32[3,17,4,8,128]{4,3,2,1,0:T(8,128)S(1)} %get-tuple-element.34.fixed, f32[3,17,8,128]{3,2,1,0:T(8,128)S(1)} %get-tuple-element.35.fixed_edge, f32[3,17,4,8,128]{4,3,2,1,0:T(8,128)S(1)} %get-tuple-element.36.once, f32[17,8,128]{2,1,0:T(8,128)S(1)} %get-tuple-element.37.edge, ...), custom_call_target="tpu_custom_call" | custom-call | bytes 10485760 | tf_op jit(solution)/shard_map/twice/pallas_call | solution.py:435
  16.3 0.0 collective-permute-done.pair
  16.3 0.6 %convert.1 = (f32[2,17,4,8,128]{4,3,2,1,0:T(8,128)S(1)}, f32[128,128]{1,0:T(8,128)S(1)}) custom-call(f32[2,128,512]{2,1,0:T(8,128)S(1)} %collective-permute-done.pair, bf16[512,512]{1,0:T(8,128)(2,1)S(1)} %get-tuple-element.23.matrix.refs_4_), custom_call_target="tpu_custom_call" | custom-call | bytes 3145728 | tf_op jit(solution)/shard_map/convert/pallas_call | solution.py:468
  16.9 0.0 collective-permute-done.4.halos
  16.9 4.9 %received.1 = (f32[4,128,512]{2,1,0:T(8,128)}, f32[4,128,512]{2,1,0:T(8,128)}) custom-call(f32[2,17,4,8,128]{4,3,2,1,0:T(8,128)S(1)} %get-tuple-element.24.bodies, f32[128,128]{1,0:T(8,128)S(1)} %get-tuple-element.25.own_edge, f32[88,128]{1,0:T(8,128)S(1)} %collective-permute-done.4.halos, ...), custom_call_target="tpu_custom_call", output_to_operand_aliasing={{0}: (9, {})} | custom-call | flops 104857600 | bytes 25165824 | tf_op jit(solution)/shard_map/received/pallas_call | solution.py:544
  (1 shorter events, 0.0 us)
Async XLA Ops:
  2.1 14.2 %collective-permute-start = (f32[2,128,512]{2,1,0:T(8,128)S(1)}, f32[2,128,512]{2,1,0:T(8,128)S(1)}, u32[]{:S(2)}, u32[]{:S(2)}) collective-permute-start(f32[2,128,512]{2,1,0:T(8,128)S(1)} %get-tuple-element.21), channel_id=1, source_target_pairs={{0,4},{4,8},{8,12},{12,0},{1,5},{5,9},{9,13},{13,1},{2,6},{6,10},{... | collective-permute-start | bytes 1572872 | tf_op jit(solution)/shard_map/ppermute | solution.py:573
  3.8 5.8 %collective-permute-start.2 = (f32[7,8,512]{2,1,0:T(8,128)S(1)}, f32[7,8,512]{2,1,0:T(8,128)S(1)}, u32[]{:S(2)}, u32[]{:S(2)}) collective-permute-start(f32[7,8,512]{2,1,0:T(8,128)S(1)} %get-tuple-element.28), channel_id=1, source_target_pairs={{0,2},{2,0},{1,3},{3,1},{4,6},{6,4},{5,7},{7,5},{8,10},{10,8},{9,1... | collective-permute-start | bytes 344072 | tf_op jit(solution)/shard_map/ppermute | solution.py:577
  5.1 2.1 %collective-permute-start.1 = (f32[128,128]{1,0:T(8,128)S(1)}, f32[128,128]{1,0:T(8,128)S(1)}, u32[]{:S(2)}, u32[]{:S(2)}) collective-permute-start(f32[128,128]{1,0:T(8,128)S(1)} %get-tuple-element.26.ys), channel_id=1, source_target_pairs={{0,1},{1,0},{2,3},{3,2},{4,5},{5,4},{6,7},{7,6},{8,9},{9,8},{10,11... | collective-permute-start | bytes 196616 | tf_op jit(solution)/shard_map/ppermute | solution.py:584
  6.3 3.3 %collective-permute-start.3 = (f32[8,128]{1,0:T(8,128)S(1)}, f32[8,128]{1,0:T(8,128)S(1)}, u32[]{:S(2)}, u32[]{:S(2)}) collective-permute-start(f32[8,128]{1,0:T(8,128)S(1)} %get-tuple-element.29), channel_id=1, source_target_pairs={{0,3},{3,0},{1,2},{2,1},{4,7},{7,4},{5,6},{6,5},{8,11},{11,8},{9,1... | collective-permute-start | bytes 12296 | tf_op jit(solution)/shard_map/ppermute | solution.py:578
  12.7 4.3 %collective-permute-start.4 = (f32[88,128]{1,0:T(8,128)S(1)}, f32[88,128]{1,0:T(8,128)S(1)}, u32[]{:S(2)}, u32[]{:S(2)}) collective-permute-start(f32[88,128]{1,0:T(8,128)S(1)} %bundle.1), channel_id=1, source_target_pairs={{0,4},{4,8},{8,12},{12,0},{1,5},{5,9},{9,13},{13,1},{2,6},{6,10},{... | collective-permute-start | bytes 135176 | tf_op jit(solution)/shard_map/ppermute | solution.py:587

commit v8 on v7

--- a/solution.py
+++ b/solution.py
@@ -268,18 +268,19 @@
     )(fields, matrix, ys, side)
 
 
-def from_strided(z, w):
+def from_strided(z, w, other=None):
     count = w.shape[0]
     for r in range(count):
         for k in range(z.shape[0]):
-            z[k, pl.ds(r, SUBLANES, stride=count), :] = w[r, k] * (1.0 / courant)
-
-
-def restore(ws, matrix, zs, outs):
+            value = w[r, k] if other is None else w[r, k] - other[r, k]
+            z[k, pl.ds(r, SUBLANES, stride=count), :] = value * (1.0 / courant)
+
+
+def restore(ws, matrix, zs, outs, others=None):
     rows = outs.shape[1]
     flat = []
     for i, w in enumerate(ws):
-        from_strided(zs.at[i], w)
+        from_strided(zs.at[i], w, None if others is None else others[i])
         flat.append(jnp.concatenate([zs[i, k, pl.ds(0, rows)] for k in range(zs.shape[1])], axis=1))
     values = restored(jnp.concatenate(flat, axis=0), matrix[...])
     for i in range(len(ws)):
@@ -357,7 +358,7 @@
 
 def once_kernel(n, *refs):
     xr, dr, (bodies, edge, matrix), refs = refs[:n], refs[n : 2 * n], refs[2 * n : 2 * n + 3], refs[2 * n + 3 :]
-    corners, sent, fixed, fixed_edge, once, e_pair, e_last = refs
+    corners, sent, fixed, fixed_edge, once, e_pair, restored_once, e_last, zs = refs
     cols = matrix.shape[0]
     count, blocks = once.shape[1:3]
     rows = count * SUBLANES - n * HALO
@@ -392,6 +393,7 @@
 
     propagate(rows, gx, gy, once.at[pl.ds(0, 2)], e_pair, fixed, fixed_edge)
     propagate(rows, gx, gy, once.at[pl.ds(2, 1)], e_last, fixed, fixed_edge)
+    restore([once.at[m] for m in range(3)], matrix, zs, restored_once)
 
 
 def propagate_once(xr, dr, bodies, edge, matrix):
@@ -406,20 +408,23 @@
             jax.ShapeDtypeStruct((3, *edge_shape), F32),
             jax.ShapeDtypeStruct((3, *body), F32),
             jax.ShapeDtypeStruct(edge_shape, F32),
+            jax.ShapeDtypeStruct((3, body[0] * SUBLANES - n * HALO, matrix.shape[0]), F32),
         ),
         in_specs=[VMEM] * (2 * n + 3),
-        out_specs=(VMEM,) * 6,
-        scratch_shapes=[pltpu.VMEM(edge_shape, F32)],
+        out_specs=(VMEM,) * 7,
+        scratch_shapes=[
+            pltpu.VMEM(edge_shape, F32),
+            pltpu.VMEM((3, body[1], body[0] * SUBLANES, LANES), F32),
+        ],
         compiler_params=pltpu.CompilerParams(vmem_limit_bytes=16 << 20),
         cost_estimate=pl.CostEstimate(flops=0, bytes_accessed=12 << 20, transcendentals=0),
         name="once",
     )(*xr, *dr, bodies, edge, matrix)
 
 
-def twice_kernel(n, fixed, fixed_edge, once, edge, matrix, relaxed, difference, ws, e_pair, zs, outs, sems):
+def twice_kernel(n, fixed, fixed_edge, once, edge, outs, relaxed, difference, ws, e_pair, sems):
     rows = outs.shape[1]
     gx, gy = place()
-    restore([once.at[m] for m in range(3)], matrix, zs, outs)
     written = write(outs, [relaxed.at[m + 1] for m in range(3)], sems)
     ws[...] = once[pl.ds(0, 2)]
     e_pair[...] = edge[...]
@@ -428,10 +433,9 @@
     wait(written)
 
 
-def propagate_twice(n, fixed, fixed_edge, once, edge, matrix):
-    body, edge_shape, cols = once.shape[1:], edge.shape, matrix.shape[0]
-    height = body[0] * SUBLANES
-    rows = height - n * HALO
+def propagate_twice(n, fixed, fixed_edge, once, edge, outs):
+    body, edge_shape = once.shape[1:], edge.shape
+    rows, cols = outs.shape[1:]
     return pl.pallas_call(
         functools.partial(twice_kernel, n),
         out_shape=(jax.ShapeDtypeStruct((4, rows, cols), F32), jax.ShapeDtypeStruct((2, *body), F32)),
@@ -440,14 +444,12 @@
         scratch_shapes=[
             pltpu.VMEM((2, *body), F32),
             pltpu.VMEM(edge_shape, F32),
-            pltpu.VMEM((3, body[1], height, LANES), F32),
-            pltpu.VMEM((3, rows, cols), F32),
             pltpu.SemaphoreType.DMA((3,)),
         ],
         compiler_params=pltpu.CompilerParams(vmem_limit_bytes=16 << 20),
         cost_estimate=pl.CostEstimate(flops=0, bytes_accessed=10 << 20, transcendentals=0),
         name="twice",
-    )(fixed, fixed_edge, once, edge, matrix)
+    )(fixed, fixed_edge, once, edge, outs)
 
 
 def convert_kernel(pair, matrix, bodies, edge, z):
@@ -523,9 +525,7 @@
 
         propagate(rows, gx, gy, ws, edge, fixed, fixed_edge, restore_first)
         written += write(outs.at[pl.ds(2, 1)], targets[2:3], sems.at[pl.ds(2, 1)])
-        late[1] = ws[0] - late[0]
-        late[2] = ws[1] - once[0]
-        restore([late.at[1], late.at[2]], matrix, zs, outs.at[pl.ds(3, 2)])
+        restore([ws.at[0], ws.at[1]], matrix, zs, outs.at[pl.ds(3, 2)], [late.at[0], once.at[0]])
         wait(written + write(outs.at[pl.ds(3, 2)], targets[3:], sems.at[pl.ds(3, 2)]))
 
     @pl.when(first)
@@ -550,7 +550,7 @@
             pltpu.VMEM((height, LANES), F32),
             pltpu.VMEM((2, *body), F32),
             pltpu.VMEM(edge, F32),
-            pltpu.VMEM((3, *body), F32),
+            pltpu.VMEM((1, *body), F32),
             pltpu.VMEM((2, body[1], height, LANES), F32),
             pltpu.VMEM((5, rows, cols), F32),
             pltpu.SemaphoreType.DMA((5,)),
@@ -583,9 +583,9 @@
         dr = [lax.ppermute(d, ("gx", "gy"), pairs) for d, pairs in zip(ds, crossed)]
     side = lax.ppermute(ys, "gy", [(0, 1), (1, 0)])
     bodies, edge, folded = prepare(n, fields, matrix, ys, side)
-    corners, sent, fixed, fixed_edge, once, edge = propagate_once(xr, dr, bodies, edge, matrix)
+    corners, sent, fixed, fixed_edge, once, edge, outs = propagate_once(xr, dr, bodies, edge, matrix)
     halos = lax.ppermute(bundle(folded, corners, sent), "ta", ring)
-    relaxed, difference = propagate_twice(n, fixed, fixed_edge, once, edge, matrix)
+    relaxed, difference = propagate_twice(n, fixed, fixed_edge, once, edge, outs)
     bodies, own_edge = convert(pair, matrix, once.shape[1:])
     return received(n, bodies, own_edge, halos, fields, fixed, fixed_edge, once, difference, matrix, relaxed)
 

time: 22 us -> 22 us (level)
    pallas_call x1, Pallas kernels: 3.02 us -> 3.62 us  [propagate_once(): pl.pallas_call(functools.partial(once_kernel, n), out_shape=(jax.ShapeDty...]
    pallas_call x1, Pallas kernels: 2.26 us -> 1.69 us  [propagate_twice(): pl.pallas_call(functools.partial(twice_kernel, n), out_shape=(jax.ShapeDt...]
where the time goes in v8:
time: 22 us; the launch traced here: 21.8 us
  Pallas kernels  14.1 us (64%)
  starting transfers between devices  5.35 us (24%)
  waiting for transfers between devices  1.67 us (8%)
  between operations  0.7 us (3%)
    pallas_call x1, Pallas kernels, received(): pl.pallas_call(functools.partial(received_kernel, n), out_shape=(shape, s...  4.86 us
    pallas_call x1, Pallas kernels, propagate_once(): pl.pallas_call(functools.partial(once_kernel, n), out_shape=(jax.ShapeDty...  3.62 us
    pallas_call x1, Pallas kernels, propagate_twice(): pl.pallas_call(functools.partial(twice_kernel, n), out_shape=(jax.ShapeDt...  1.69 us
    pallas_call x1, Pallas kernels, prepare(): pl.pallas_call(prepare_kernel, out_shape=(jax.ShapeDtypeStruct((len(USED)...  1.51 us
    pallas_call x1, Pallas kernels, take(): pl.pallas_call(take_kernel, out_shape=[jax.ShapeDtypeStruct((count, *dif....  1.47 us
    ppermute x1, starting transfers between devices, local(): halos = lax.ppermute(bundle(folded, corners, sent), 'ta', ring)  1.35 us
    ppermute x1, starting transfers between devices, local(): pair = lax.ppermute(pair, 'ta', ring)  1.35 us
    ppermute x1, starting transfers between devices, local(): xr = [lax.ppermute(xs[0], 'gx', [(0, 1), (1, 0)])]  1.28 us
  transfers between devices with their start and end apart: 5, of which 2 were waited for; matrix products, arithmetic and copies ran while one was open for 0% of the time, Pallas kernels for 36%

profile of v8, /device:TPU:9, one launch (start us, length us, event | category | flops | bytes accessed | tf_op | source)
XLA Modules:
  0.0 21.8 jit_solution(10423342576032445412)
XLA Ops:
  0.6 1.5 %take.1 = (f32[2,128,512]{2,1,0:T(8,128)S(1)}, f32[7,128,512]{2,1,0:T(8,128)S(1)}) custom-call(f32[4,128,512]{2,1,0:T(8,128)} %c.1, f32[128,512]{1,0:T(8,128)} %dif.1, f32[128,512]{1,0:T(8,128)} %dx.1, f32[128,512]{1,0:T(8,128)} %dy.1), custom_call_target="tpu_custom_call" | custom-call | tf_op jit(solution)/shard_map/take/pallas_call | solution.py:157
  2.1 1.3 %collective-permute-start = (f32[2,128,512]{2,1,0:T(8,128)S(1)}, f32[2,128,512]{2,1,0:T(8,128)S(1)}, u32[]{:S(2)}, u32[]{:S(2)}) collective-permute-start(f32[2,128,512]{2,1,0:T(8,128)S(1)} %get-tuple-element.22), channel_id=1, source_target_pairs={{0,4},{4,8},{8,12},{12,0},{1,5},{5,9},{9,13},{13,1},{2,6},{6,10},{... | collective-permute-start | bytes 1572872 | tf_op jit(solution)/shard_map/ppermute | solution.py:573
  3.5 0.3 %pack.1 = (f32[7,8,512]{2,1,0:T(8,128)S(1)}, f32[8,128]{1,0:T(8,128)S(1)}, f32[128,128]{1,0:T(8,128)S(1)}, bf16[512,512]{1,0:T(8,128)(2,1)S(1)}) custom-call(f32[7,128,512]{2,1,0:T(8,128)S(1)} %get-tuple-element.23.fields), custom_call_target="tpu_custom_call" | custom-call | tf_op jit(solution)/shard_map/pack/pallas_call | solution.py:129
  3.8 1.3 %collective-permute-start.2 = (f32[7,8,512]{2,1,0:T(8,128)S(1)}, f32[7,8,512]{2,1,0:T(8,128)S(1)}, u32[]{:S(2)}, u32[]{:S(2)}) collective-permute-start(f32[7,8,512]{2,1,0:T(8,128)S(1)} %get-tuple-element.29), channel_id=1, source_target_pairs={{0,2},{2,0},{1,3},{3,1},{4,6},{6,4},{5,7},{7,5},{8,10},{10,8},{9,1... | collective-permute-start | bytes 344072 | tf_op jit(solution)/shard_map/ppermute | solution.py:577
  5.1 1.2 %collective-permute-start.1 = (f32[128,128]{1,0:T(8,128)S(1)}, f32[128,128]{1,0:T(8,128)S(1)}, u32[]{:S(2)}, u32[]{:S(2)}) collective-permute-start(f32[128,128]{1,0:T(8,128)S(1)} %get-tuple-element.27.ys), channel_id=1, source_target_pairs={{0,1},{1,0},{2,3},{3,2},{4,5},{5,4},{6,7},{7,6},{8,9},{9,8},{10,11... | collective-permute-start | bytes 196616 | tf_op jit(solution)/shard_map/ppermute | solution.py:584
  6.3 0.1 collective-permute-start.3
  6.5 0.8 %collective-permute-done.1.side = f32[128,128]{1,0:T(8,128)S(1)} collective-permute-done((f32[128,128]{1,0:T(8,128)S(1)}, f32[128,128]{1,0:T(8,128)S(1)}, u32[]{:S(2)}, u32[]{:S(2)}) %collective-permute-start.1) | collective-permute-done | bytes 65568 | tf_op jit(solution)/shard_map/ppermute | solution.py:584
  7.2 1.5 %prepare.1 = (f32[6,17,4,8,128]{4,3,2,1,0:T(8,128)S(1)}, f32[5,17,8,128]{3,2,1,0:T(8,128)S(1)}, f32[16,128]{1,0:T(8,128)S(1)}) custom-call(f32[7,128,512]{2,1,0:T(8,128)S(1)} %get-tuple-element.23.fields, bf16[512,512]{1,0:T(8,128)(2,1)S(1)} %get-tuple-element.24.matrix.refs_4_, f32[128,128]{1,0:T(8,128)S(1)} %get-tuple-element.27.ys, ...), custom_call_target="tpu_custom_call" | custom-call | flops 45875200 | bytes 6291456 | tf_op jit(solution)/shard_map/prepare/pallas_call | solution.py:252
  8.7 0.9 %collective-permute-done.3.refs_1_ = f32[8,128]{1,0:T(8,128)S(1)} collective-permute-done((f32[8,128]{1,0:T(8,128)S(1)}, f32[8,128]{1,0:T(8,128)S(1)}, u32[]{:S(2)}, u32[]{:S(2)}) %collective-permute-start.3) | collective-permute-done | bytes 4128 | tf_op jit(solution)/shard_map/ppermute | solution.py:578
  9.6 0.0 collective-permute-done.2.refs_0_
  9.6 3.6 %once.1 = (f32[1,8,128]{2,1,0:T(8,128)S(1)}, f32[1,16,512]{2,1,0:T(8,128)S(1)}, f32[3,17,4,8,128]{4,3,2,1,0:T(8,128)S(1)}, f32[3,17,8,128]{3,2,1,0:T(8,128)S(1)}...) custom-call(f32[7,8,512]{2,1,0:T(8,128)S(1)} %collective-permute-done.2.refs_0_, ...), custom_call_target="tpu_custom_call" | custom-call | bytes 12582912 | tf_op jit(solution)/shard_map/once/pallas_call | solution.py:402
  13.3 1.4 %collective-permute-start.4 = (f32[88,128]{1,0:T(8,128)S(1)}, f32[88,128]{1,0:T(8,128)S(1)}, u32[]{:S(2)}, u32[]{:S(2)}) collective-permute-start(f32[88,128]{1,0:T(8,128)S(1)} %bundle.1), channel_id=1, source_target_pairs={{0,4},{4,8},{8,12},{12,0},{1,5},{5,9},{9,13},{13,1},{2,6},{6,10},{... | collective-permute-start | bytes 135176 | tf_op jit(solution)/shard_map/ppermute | solution.py:587
  14.6 1.7 %twice.1 = (f32[4,128,512]{2,1,0:T(8,128)}, f32[2,17,4,8,128]{4,3,2,1,0:T(8,128)S(1)}) custom-call(f32[3,17,4,8,128]{4,3,2,1,0:T(8,128)S(1)} %get-tuple-element.35.fixed, f32[3,17,8,128]{3,2,1,0:T(8,128)S(1)} %get-tuple-element.36.fixed_edge, f32[3,17,4,8,128]{4,3,2,1,0:T(8,128)S(1)} %get-tuple-element.37.once, f32[17,8,128]{2,1,0:T(8,128)S(1)} %get-tuple-element.38.edge, ...), custom_call_target="tpu_custom_call" | custom-call | bytes 10485760 | tf_op jit(solution)/shard_map/twice/pallas_call | solution.py:439
  16.3 0.0 collective-permute-done.pair
  16.3 0.6 %convert.1 = (f32[2,17,4,8,128]{4,3,2,1,0:T(8,128)S(1)}, f32[128,128]{1,0:T(8,128)S(1)}) custom-call(f32[2,128,512]{2,1,0:T(8,128)S(1)} %collective-permute-done.pair, bf16[512,512]{1,0:T(8,128)(2,1)S(1)} %get-tuple-element.24.matrix.refs_4_), custom_call_target="tpu_custom_call" | custom-call | bytes 3145728 | tf_op jit(solution)/shard_map/convert/pallas_call | solution.py:470
  17.0 0.0 collective-permute-done.4.halos
  17.0 4.9 %received.1 = (f32[4,128,512]{2,1,0:T(8,128)}, f32[4,128,512]{2,1,0:T(8,128)}) custom-call(f32[2,17,4,8,128]{4,3,2,1,0:T(8,128)S(1)} %get-tuple-element.25.bodies, f32[128,128]{1,0:T(8,128)S(1)} %get-tuple-element.26.own_edge, f32[88,128]{1,0:T(8,128)S(1)} %collective-permute-done.4.halos, ...), custom_call_target="tpu_custom_call", output_to_operand_aliasing={{0}: (9, {})} | custom-call | flops 104857600 | bytes 25165824 | tf_op jit(solution)/shard_map/received/pallas_call | solution.py:544
  (1 shorter events, 0.0 us)
Async XLA Ops:
  2.1 14.2 %collective-permute-start = (f32[2,128,512]{2,1,0:T(8,128)S(1)}, f32[2,128,512]{2,1,0:T(8,128)S(1)}, u32[]{:S(2)}, u32[]{:S(2)}) collective-permute-start(f32[2,128,512]{2,1,0:T(8,128)S(1)} %get-tuple-element.22), channel_id=1, source_target_pairs={{0,4},{4,8},{8,12},{12,0},{1,5},{5,9},{9,13},{13,1},{2,6},{6,10},{... | collective-permute-start | bytes 1572872 | tf_op jit(solution)/shard_map/ppermute | solution.py:573
  3.8 5.8 %collective-permute-start.2 = (f32[7,8,512]{2,1,0:T(8,128)S(1)}, f32[7,8,512]{2,1,0:T(8,128)S(1)}, u32[]{:S(2)}, u32[]{:S(2)}) collective-permute-start(f32[7,8,512]{2,1,0:T(8,128)S(1)} %get-tuple-element.29), channel_id=1, source_target_pairs={{0,2},{2,0},{1,3},{3,1},{4,6},{6,4},{5,7},{7,5},{8,10},{10,8},{9,1... | collective-permute-start | bytes 344072 | tf_op jit(solution)/shard_map/ppermute | solution.py:577
  5.1 2.1 %collective-permute-start.1 = (f32[128,128]{1,0:T(8,128)S(1)}, f32[128,128]{1,0:T(8,128)S(1)}, u32[]{:S(2)}, u32[]{:S(2)}) collective-permute-start(f32[128,128]{1,0:T(8,128)S(1)} %get-tuple-element.27.ys), channel_id=1, source_target_pairs={{0,1},{1,0},{2,3},{3,2},{4,5},{5,4},{6,7},{7,6},{8,9},{9,8},{10,11... | collective-permute-start | bytes 196616 | tf_op jit(solution)/shard_map/ppermute | solution.py:584
  6.3 3.3 %collective-permute-start.3 = (f32[8,128]{1,0:T(8,128)S(1)}, f32[8,128]{1,0:T(8,128)S(1)}, u32[]{:S(2)}, u32[]{:S(2)}) collective-permute-start(f32[8,128]{1,0:T(8,128)S(1)} %get-tuple-element.30), channel_id=1, source_target_pairs={{0,3},{3,0},{1,2},{2,1},{4,7},{7,4},{5,6},{6,5},{8,11},{11,8},{9,1... | collective-permute-start | bytes 12296 | tf_op jit(solution)/shard_map/ppermute | solution.py:578
  13.3 3.7 %collective-permute-start.4 = (f32[88,128]{1,0:T(8,128)S(1)}, f32[88,128]{1,0:T(8,128)S(1)}, u32[]{:S(2)}, u32[]{:S(2)}) collective-permute-start(f32[88,128]{1,0:T(8,128)S(1)} %bundle.1), channel_id=1, source_target_pairs={{0,4},{4,8},{8,12},{12,0},{1,5},{5,9},{9,13},{13,1},{2,6},{6,10},{... | collective-permute-start | bytes 135176 | tf_op jit(solution)/shard_map/ppermute | solution.py:587

commit v9 on v8

--- a/solution.py
+++ b/solution.py
@@ -276,7 +276,7 @@
             z[k, pl.ds(r, SUBLANES, stride=count), :] = value * (1.0 / courant)
 
 
-def restore(ws, matrix, zs, outs, others=None):
+def restore(ws, matrix, zs, outs, others=None, then=None):
     rows = outs.shape[1]
     flat = []
     for i, w in enumerate(ws):
@@ -285,6 +285,8 @@
     values = restored(jnp.concatenate(flat, axis=0), matrix[...])
     for i in range(len(ws)):
         outs[i] = values[i * rows : (i + 1) * rows]
+        if then is not None:
+            then(i)
 
 
 def write(outs, targets, sems):
@@ -302,7 +304,7 @@
     return field + diffusion * laplace - speed_x * upwind_x - speed_y * upwind_y
 
 
-def step(rows, gx, gy, ws, edge, fixed, fixed_edge):
+def step(rows, gx, gy, ws, edge, fixed, fixed_edge, last=False):
     n, count, blocks = ws.shape[:3]
     shape = (SUBLANES, LANES)
     lane, sublane = lane_index(shape), lax.broadcasted_iota(jnp.int32, shape, 0)
@@ -328,9 +330,10 @@
         if cut and r == last_row:
             below = [jnp.where(none_below, 0.0, value) for value in following]
         after = [other - value for value, other in zip(field, below)]
-        border = field[-1] - pltpu.roll(field[-1], 1, 1)
-        around = (before[-1], after[-1], border, pltpu.roll(border, LANES - 1, 1))
-        edge[r] = update(field[-1], *around, *[fixed_edge[i, r] for i in range(3)])
+        if not last:
+            border = field[-1] - pltpu.roll(field[-1], 1, 1)
+            around = (before[-1], after[-1], border, pltpu.roll(border, LANES - 1, 1))
+            edge[r] = update(field[-1], *around, *[fixed_edge[i, r] for i in range(3)])
         for m in range(n):
             part = slice(m * blocks, (m + 1) * blocks)
             body, body_before, body_after = field[part], before[part], after[part]
@@ -345,7 +348,7 @@
         field, before = following, after
 
 
-def propagate(rows, gx, gy, ws, edge, fixed, fixed_edge, beside=None):
+def propagate(rows, gx, gy, ws, edge, fixed, fixed_edge, beside=None, last=False):
     def one(count, carry):
         step(rows, gx, gy, ws, edge, fixed, fixed_edge)
         return carry
@@ -353,7 +356,9 @@
     if beside is not None:
         beside()
         one(0, 0)
-    lax.fori_loop(0, FACTOR - (beside is not None), one, 0)
+    lax.fori_loop(0, FACTOR - (beside is not None) - last, one, 0)
+    if last:
+        step(rows, gx, gy, ws, edge, fixed, fixed_edge, True)
 
 
 def once_kernel(n, *refs):
@@ -523,10 +528,14 @@
         def restore_first():
             restore([late.at[0]], matrix, zs, outs.at[pl.ds(2, 1)])
 
-        propagate(rows, gx, gy, ws, edge, fixed, fixed_edge, restore_first)
+        propagate(rows, gx, gy, ws, edge, fixed, fixed_edge, restore_first, True)
         written += write(outs.at[pl.ds(2, 1)], targets[2:3], sems.at[pl.ds(2, 1)])
-        restore([ws.at[0], ws.at[1]], matrix, zs, outs.at[pl.ds(3, 2)], [late.at[0], once.at[0]])
-        wait(written + write(outs.at[pl.ds(3, 2)], targets[3:], sems.at[pl.ds(3, 2)]))
+
+        def write_one(i):
+            written.extend(write(outs.at[pl.ds(3 + i, 1)], targets[3 + i : 4 + i], sems.at[pl.ds(3 + i, 1)]))
+
+        restore([ws.at[0], ws.at[1]], matrix, zs, outs.at[pl.ds(3, 2)], [late.at[0], once.at[0]], write_one)
+        wait(written)
 
     @pl.when(first)
     def _():

time: 22 us -> 21.9 us (level)
  no operation moved by 1% of the time
where the time goes in v9:
time: 21.9 us; the launch traced here: 21.7 us
  Pallas kernels  14 us (64%)
  starting transfers between devices  5.35 us (24%)
  waiting for transfers between devices  1.67 us (8%)
  between operations  0.7 us (3%)
    pallas_call x1, Pallas kernels, received(): pl.pallas_call(functools.partial(received_kernel, n), out_shape=(shape, s...  4.76 us
    pallas_call x1, Pallas kernels, propagate_once(): pl.pallas_call(functools.partial(once_kernel, n), out_shape=(jax.ShapeDty...  3.62 us
    pallas_call x1, Pallas kernels, propagate_twice(): pl.pallas_call(functools.partial(twice_kernel, n), out_shape=(jax.ShapeDt...  1.69 us
    pallas_call x1, Pallas kernels, prepare(): pl.pallas_call(prepare_kernel, out_shape=(jax.ShapeDtypeStruct((len(USED)...  1.51 us
    pallas_call x1, Pallas kernels, take(): pl.pallas_call(take_kernel, out_shape=[jax.ShapeDtypeStruct((count, *dif....  1.47 us
    ppermute x1, starting transfers between devices, local(): halos = lax.ppermute(bundle(folded, corners, sent), 'ta', ring)  1.35 us
    ppermute x1, starting transfers between devices, local(): pair = lax.ppermute(pair, 'ta', ring)  1.35 us
    ppermute x1, starting transfers between devices, local(): xr = [lax.ppermute(xs[0], 'gx', [(0, 1), (1, 0)])]  1.28 us
  transfers between devices with their start and end apart: 5, of which 2 were waited for; matrix products, arithmetic and copies ran while one was open for 0% of the time, Pallas kernels for 36%

profile of v9, /device:TPU:9, one launch (start us, length us, event | category | flops | bytes accessed | tf_op | source)
XLA Modules:
  0.0 21.7 jit_solution(8861172666656977111)
XLA Ops:
  0.6 1.5 %take.1 = (f32[2,128,512]{2,1,0:T(8,128)S(1)}, f32[7,128,512]{2,1,0:T(8,128)S(1)}) custom-call(f32[4,128,512]{2,1,0:T(8,128)} %c.1, f32[128,512]{1,0:T(8,128)} %dif.1, f32[128,512]{1,0:T(8,128)} %dx.1, f32[128,512]{1,0:T(8,128)} %dy.1), custom_call_target="tpu_custom_call" | custom-call | tf_op jit(solution)/shard_map/take/pallas_call | solution.py:157
  2.1 1.3 %collective-permute-start = (f32[2,128,512]{2,1,0:T(8,128)S(1)}, f32[2,128,512]{2,1,0:T(8,128)S(1)}, u32[]{:S(2)}, u32[]{:S(2)}) collective-permute-start(f32[2,128,512]{2,1,0:T(8,128)S(1)} %get-tuple-element.22), channel_id=1, source_target_pairs={{0,4},{4,8},{8,12},{12,0},{1,5},{5,9},{9,13},{13,1},{2,6},{6,10},{... | collective-permute-start | bytes 1572872 | tf_op jit(solution)/shard_map/ppermute | solution.py:582
  3.5 0.3 %pack.1 = (f32[7,8,512]{2,1,0:T(8,128)S(1)}, f32[8,128]{1,0:T(8,128)S(1)}, f32[128,128]{1,0:T(8,128)S(1)}, bf16[512,512]{1,0:T(8,128)(2,1)S(1)}) custom-call(f32[7,128,512]{2,1,0:T(8,128)S(1)} %get-tuple-element.23.fields), custom_call_target="tpu_custom_call" | custom-call | tf_op jit(solution)/shard_map/pack/pallas_call | solution.py:129
  3.8 1.3 %collective-permute-start.2 = (f32[7,8,512]{2,1,0:T(8,128)S(1)}, f32[7,8,512]{2,1,0:T(8,128)S(1)}, u32[]{:S(2)}, u32[]{:S(2)}) collective-permute-start(f32[7,8,512]{2,1,0:T(8,128)S(1)} %get-tuple-element.29), channel_id=1, source_target_pairs={{0,2},{2,0},{1,3},{3,1},{4,6},{6,4},{5,7},{7,5},{8,10},{10,8},{9,1... | collective-permute-start | bytes 344072 | tf_op jit(solution)/shard_map/ppermute | solution.py:586
  5.1 1.2 %collective-permute-start.1 = (f32[128,128]{1,0:T(8,128)S(1)}, f32[128,128]{1,0:T(8,128)S(1)}, u32[]{:S(2)}, u32[]{:S(2)}) collective-permute-start(f32[128,128]{1,0:T(8,128)S(1)} %get-tuple-element.27.ys), channel_id=1, source_target_pairs={{0,1},{1,0},{2,3},{3,2},{4,5},{5,4},{6,7},{7,6},{8,9},{9,8},{10,11... | collective-permute-start | bytes 196616 | tf_op jit(solution)/shard_map/ppermute | solution.py:593
  6.3 0.1 collective-permute-start.3
  6.5 0.8 %collective-permute-done.1.side = f32[128,128]{1,0:T(8,128)S(1)} collective-permute-done((f32[128,128]{1,0:T(8,128)S(1)}, f32[128,128]{1,0:T(8,128)S(1)}, u32[]{:S(2)}, u32[]{:S(2)}) %collective-permute-start.1) | collective-permute-done | bytes 65568 | tf_op jit(solution)/shard_map/ppermute | solution.py:593
  7.2 1.5 %prepare.1 = (f32[6,17,4,8,128]{4,3,2,1,0:T(8,128)S(1)}, f32[5,17,8,128]{3,2,1,0:T(8,128)S(1)}, f32[16,128]{1,0:T(8,128)S(1)}) custom-call(f32[7,128,512]{2,1,0:T(8,128)S(1)} %get-tuple-element.23.fields, bf16[512,512]{1,0:T(8,128)(2,1)S(1)} %get-tuple-element.24.matrix.refs_4_, f32[128,128]{1,0:T(8,128)S(1)} %get-tuple-element.27.ys, ...), custom_call_target="tpu_custom_call" | custom-call | flops 45875200 | bytes 6291456 | tf_op jit(solution)/shard_map/prepare/pallas_call | solution.py:252
  8.7 0.9 %collective-permute-done.3.refs_1_ = f32[8,128]{1,0:T(8,128)S(1)} collective-permute-done((f32[8,128]{1,0:T(8,128)S(1)}, f32[8,128]{1,0:T(8,128)S(1)}, u32[]{:S(2)}, u32[]{:S(2)}) %collective-permute-start.3) | collective-permute-done | bytes 4128 | tf_op jit(solution)/shard_map/ppermute | solution.py:587
  9.6 0.0 collective-permute-done.2.refs_0_
  9.6 3.6 %once.1 = (f32[1,8,128]{2,1,0:T(8,128)S(1)}, f32[1,16,512]{2,1,0:T(8,128)S(1)}, f32[3,17,4,8,128]{4,3,2,1,0:T(8,128)S(1)}, f32[3,17,8,128]{3,2,1,0:T(8,128)S(1)}...) custom-call(f32[7,8,512]{2,1,0:T(8,128)S(1)} %collective-permute-done.2.refs_0_, ...), custom_call_target="tpu_custom_call" | custom-call | bytes 12582912 | tf_op jit(solution)/shard_map/once/pallas_call | solution.py:407
  13.3 1.4 %collective-permute-start.4 = (f32[88,128]{1,0:T(8,128)S(1)}, f32[88,128]{1,0:T(8,128)S(1)}, u32[]{:S(2)}, u32[]{:S(2)}) collective-permute-start(f32[88,128]{1,0:T(8,128)S(1)} %bundle.1), channel_id=1, source_target_pairs={{0,4},{4,8},{8,12},{12,0},{1,5},{5,9},{9,13},{13,1},{2,6},{6,10},{... | collective-permute-start | bytes 135176 | tf_op jit(solution)/shard_map/ppermute | solution.py:596
  14.6 1.7 %twice.1 = (f32[4,128,512]{2,1,0:T(8,128)}, f32[2,17,4,8,128]{4,3,2,1,0:T(8,128)S(1)}) custom-call(f32[3,17,4,8,128]{4,3,2,1,0:T(8,128)S(1)} %get-tuple-element.35.fixed, f32[3,17,8,128]{3,2,1,0:T(8,128)S(1)} %get-tuple-element.36.fixed_edge, f32[3,17,4,8,128]{4,3,2,1,0:T(8,128)S(1)} %get-tuple-element.37.once, f32[17,8,128]{2,1,0:T(8,128)S(1)} %get-tuple-element.38.edge, ...), custom_call_target="tpu_custom_call" | custom-call | bytes 10485760 | tf_op jit(solution)/shard_map/twice/pallas_call | solution.py:444
  16.3 0.0 collective-permute-done.pair
  16.3 0.6 %convert.1 = (f32[2,17,4,8,128]{4,3,2,1,0:T(8,128)S(1)}, f32[128,128]{1,0:T(8,128)S(1)}) custom-call(f32[2,128,512]{2,1,0:T(8,128)S(1)} %collective-permute-done.pair, bf16[512,512]{1,0:T(8,128)(2,1)S(1)} %get-tuple-element.24.matrix.refs_4_), custom_call_target="tpu_custom_call" | custom-call | bytes 3145728 | tf_op jit(solution)/shard_map/convert/pallas_call | solution.py:475
  17.0 0.0 collective-permute-done.4.halos
  17.0 4.8 %received.1 = (f32[4,128,512]{2,1,0:T(8,128)}, f32[4,128,512]{2,1,0:T(8,128)}) custom-call(f32[2,17,4,8,128]{4,3,2,1,0:T(8,128)S(1)} %get-tuple-element.25.bodies, f32[128,128]{1,0:T(8,128)S(1)} %get-tuple-element.26.own_edge, f32[88,128]{1,0:T(8,128)S(1)} %collective-permute-done.4.halos, ...), custom_call_target="tpu_custom_call", output_to_operand_aliasing={{0}: (9, {})} | custom-call | flops 104857600 | bytes 25165824 | tf_op jit(solution)/shard_map/received/pallas_call | solution.py:553
  (1 shorter events, 0.0 us)
Async XLA Ops:
  2.1 14.2 %collective-permute-start = (f32[2,128,512]{2,1,0:T(8,128)S(1)}, f32[2,128,512]{2,1,0:T(8,128)S(1)}, u32[]{:S(2)}, u32[]{:S(2)}) collective-permute-start(f32[2,128,512]{2,1,0:T(8,128)S(1)} %get-tuple-element.22), channel_id=1, source_target_pairs={{0,4},{4,8},{8,12},{12,0},{1,5},{5,9},{9,13},{13,1},{2,6},{6,10},{... | collective-permute-start | bytes 1572872 | tf_op jit(solution)/shard_map/ppermute | solution.py:582
  3.8 5.8 %collective-permute-start.2 = (f32[7,8,512]{2,1,0:T(8,128)S(1)}, f32[7,8,512]{2,1,0:T(8,128)S(1)}, u32[]{:S(2)}, u32[]{:S(2)}) collective-permute-start(f32[7,8,512]{2,1,0:T(8,128)S(1)} %get-tuple-element.29), channel_id=1, source_target_pairs={{0,2},{2,0},{1,3},{3,1},{4,6},{6,4},{5,7},{7,5},{8,10},{10,8},{9,1... | collective-permute-start | bytes 344072 | tf_op jit(solution)/shard_map/ppermute | solution.py:586
  5.1 2.1 %collective-permute-start.1 = (f32[128,128]{1,0:T(8,128)S(1)}, f32[128,128]{1,0:T(8,128)S(1)}, u32[]{:S(2)}, u32[]{:S(2)}) collective-permute-start(f32[128,128]{1,0:T(8,128)S(1)} %get-tuple-element.27.ys), channel_id=1, source_target_pairs={{0,1},{1,0},{2,3},{3,2},{4,5},{5,4},{6,7},{7,6},{8,9},{9,8},{10,11... | collective-permute-start | bytes 196616 | tf_op jit(solution)/shard_map/ppermute | solution.py:593
  6.3 3.3 %collective-permute-start.3 = (f32[8,128]{1,0:T(8,128)S(1)}, f32[8,128]{1,0:T(8,128)S(1)}, u32[]{:S(2)}, u32[]{:S(2)}) collective-permute-start(f32[8,128]{1,0:T(8,128)S(1)} %get-tuple-element.30), channel_id=1, source_target_pairs={{0,3},{3,0},{1,2},{2,1},{4,7},{7,4},{5,6},{6,5},{8,11},{11,8},{9,1... | collective-permute-start | bytes 12296 | tf_op jit(solution)/shard_map/ppermute | solution.py:587
  13.3 3.7 %collective-permute-start.4 = (f32[88,128]{1,0:T(8,128)S(1)}, f32[88,128]{1,0:T(8,128)S(1)}, u32[]{:S(2)}, u32[]{:S(2)}) collective-permute-start(f32[88,128]{1,0:T(8,128)S(1)} %bundle.1), channel_id=1, source_target_pairs={{0,4},{4,8},{8,12},{12,0},{1,5},{5,9},{9,13},{13,1},{2,6},{6,10},{... | collective-permute-start | bytes 135176 | tf_op jit(solution)/shard_map/ppermute | solution.py:596
